TPU v7x, 32 devices: a whole 2x2x4 slice. The times are simulated.
32 devices in a mesh: grp: 2 (over x), scen: 16 (over z, y, core).
Axes of the slice: x: 2, y: 2, z: 4, core: 2. Of those that a mesh axis runs over, the one named last changes fastest.
Arguments:
- returns: bfloat16 [64, 32768], P(None, ('grp', 'scen')), parts along dimension 1, may hold values from -2 to 2
- exposures: bfloat16 [32768, 64], P(('grp', 'scen')), parts along dimension 0, may hold values from -0.75 to 0.75
- guarantees: float32 [32768], P(('grp', 'scen')), parts along dimension 0, may hold values from 0.7 to 1.3
- guar_type: int32 [32768], P(('grp', 'scen')), parts along dimension 0, may hold values from 0 to 2
- line_ids: int32 [32768], P(('grp', 'scen')), parts along dimension 0, may hold values from 0 to 63
- drivers: float32 [40, 32768], P(None, ('grp', 'scen')), parts along dimension 1, may hold values from -1.7 to 1.7
- exponents: int32 [512, 40], replicated, may hold values from 0 to 3, as said below
Outputs:
- gram: float32 [1024, 512], P('grp'), parts along dimension 0
- rhs: float32 [1024, 64], P('grp'), parts along dimension 0
There are 2 independent parts, one for each index of `grp`. A program takes and returns all parts, laid end to end along the dimension named above; an argument that names none is the same for every part. Nothing has to cross between parts.
Inputs may be any that keep to these rules, and one draw needn't show every extreme that they name: Each row of exponents sums to 3, and every eighth row (0, 8, 16, ...) is one driver cubed.
All inputs are finite; a program needn't handle non-finite values.
Results may differ from a plain program's by a relative error of at most 0.009.
Values may be sent and summed in bfloat16 or wider, within the bound.
No kernel may reach another device: no remote copies, remote signals or barrier semaphores. Data moves between devices by JAX's collectives and lax.ppermute only.
A program may use at most 320 MiB of HBM per device.

v0:
```python
import math

import jax
import jax.numpy as jnp
from jax import lax
from jax.sharding import PartitionSpec as P

LINES = 64


def basis_of(drivers, exponents):
    basis = jnp.ones((exponents.shape[0], drivers.shape[1]), jnp.float32)
    for j in range(drivers.shape[0]):
        power = exponents[:, j][:, None]
        value = drivers[j][None, :]
        factor = jnp.where(
            power == 1,
            value,
            jnp.where(
                power == 2,
                value * value,
                jnp.where(power == 3, value * value * value, jnp.float32(1.0)),
            ),
        )
        basis = basis * factor
    return basis


def line_terms(exp_rows, guar_rows, type_rows, line_rows, scen_returns, line_count):
    fund = jnp.exp(jnp.dot(exp_rows, scen_returns, preferred_element_type=jnp.float32))
    level = guar_rows * (1.0 + 0.15 * type_rows.astype(jnp.float32))
    payoff = jnp.maximum(level[:, None] - fund, 0.0)
    labels = jnp.arange(line_count, dtype=jnp.int32)[:, None]
    onehot = (line_rows[None, :] == labels).astype(jnp.float32)
    return jnp.dot(onehot, payoff, precision=lax.Precision.HIGHEST)


def local(returns, exposures, guarantees, guar_type, line_ids, drivers, exponents):
    line_count = LINES
    all_points = exposures.shape[0] * lax.axis_size("scen")
    scen_total = returns.shape[1] * lax.axis_size("scen")
    partials = line_terms(
        exposures,
        guarantees,
        guar_type,
        line_ids,
        lax.all_gather(returns, "scen", axis=1, tiled=True),
        line_count,
    )
    summed = lax.psum_scatter(partials, "scen", scatter_dimension=1, tiled=True)
    line_value = summed / math.sqrt(all_points / line_count)
    basis = basis_of(drivers, exponents)
    gram_part = jnp.dot(basis, basis.T, precision=lax.Precision.HIGHEST) / scen_total
    rhs_part = jnp.dot(basis, line_value.T, precision=lax.Precision.HIGHEST) / scen_total
    gram, rhs = lax.psum((gram_part, rhs_part), "scen")
    return (gram, rhs)


def solution(mesh):
    placed = (
        P(None, ("grp", "scen")),
        P(("grp", "scen"), None),
        P(("grp", "scen")),
        P(("grp", "scen")),
        P(("grp", "scen")),
        P(None, ("grp", "scen")),
        P(),
    )
    return jax.shard_map(
        local,
        mesh=mesh,
        in_specs=placed,
        out_specs=(P("grp", None), P("grp", None)),
        check_vma=False,
    )
```

profile of v0, /device:TPU:0, one launch (start us, length us, event | category | flops | bytes accessed | tf_op | source)
XLA Modules:
  0.0 300.4 jit_solution(14586082089665933152)
XLA Ops:
  7.2 0.0 copy-start
  7.2 0.0 all-gather.2.cloned.1.call-start
  7.2 0.7 all-gather.2.cloned.1.call-update
  7.9 0.0 reduce-scatter.2.cloned.1.call-start
  8.0 0.7 add_multiply_fusion
  8.7 45.7 %all-gather.2.cloned.1.call-done = bf16[64,16384]{1,0:T(8,128)(2,1)} async-done(((bf16[64,1024]{1,0:T(8,128)(2,1)}), bf16[64,16384]{1,0:T(8,128)(2,1)}) %all-gather.2.cloned.1.call-update) | async-done | bytes 2097168 | tf_op jit(solution)/shard_map/all_gather | solution.py:47
  54.4 0.0 copy-done
  54.4 24.7 %fusion.18 = f32[1024,16384]{1,0:T(8,128)} fusion(bf16[1024,64]{0,1:T(8,128)(2,1)S(1)} %copy-done, bf16[64,16384]{1,0:T(8,128)(2,1)} %all-gather.2.cloned.1.call-done), kind=kOutput, calls=%fused_computation.223 | convolution fusion | flops 2147483648 | bytes 69337088 | tf_op jit(solution)/shard_map/dot_general | solution.py:30
  79.0 0.0 copy-done.4
  79.0 43.1 %fusion = f32[64,16384]{1,0:T(8,128)} fusion(f32[1024,16384]{1,0:T(8,128)} %fusion.18, f32[1024]{0:T(1024)S(1)} %add_multiply_fusion, s32[1024]{0:T(1024)S(1)} %copy-done.4), kind=kOutput, calls=%fused_computation | convolution fusion | flops 12918521856 | bytes 71311360 | tf_op jit(solution)/shard_map/dot_general | solution.py:35
  122.1 0.0 reduce-scatter.2.cloned.1.call-update
  122.2 0.2 all-reduce.3.cloned.1.call-start
  122.4 0.6 copy-done.2
  123.0 0.1 compare_reduce_fusion.113
  123.1 0.1 compare_reduce_fusion.107
  123.3 0.2 compare_reduce_fusion.116
  123.5 0.1 compare_reduce_fusion.104
  123.6 0.3 compare_reduce_fusion.119
  123.9 0.0 copy-done.1
  124.0 0.1 fusion.14
  124.0 0.1 fusion.15
  124.1 0.1 fusion.16
  124.2 0.1 fusion.12
  124.2 0.1 fusion.13
  124.3 28.7 %select_multiply_fusion = f32[512,1024]{1,0:T(8,128)S(1)} fusion(f32[1024]{0:T(1024)S(1)} %bitcast.158, f32[1024]{0:T(1024)S(1)} %bitcast.157, f32[1024]{0:T(1024)S(1)} %bitcast.129, f32[1024]{0:T(1024)S(1)} %bitcast.156, f32[1024]{0:T(1024)S(1)} %bitcast.155, f32[1024]{0:T(1024)S(1)} %bitcast.130, f32[1024]{0:T(1024)S(1)} %bitcast.154, ...), kind=kLoop, calls=%fused_computation.6 | loop fusion | flops 83361792 | bytes 2650112 | tf_op jit(solution)/shard_map/mul | solution.py:25
  153.0 4.5 %convolution_multiply_fusion = f32[512,512]{1,0:T(8,128)} fusion(f32[512,1024]{1,0:T(8,128)S(1)} %select_multiply_fusion), kind=kOutput, calls=%fused_computation.7 | convolution fusion | flops 3221487616 | bytes 3145728 | tf_op jit(solution)/shard_map/dot_general | solution.py:53
  157.5 36.0 %reduce-scatter.2.cloned.1.call-done = f32[64,1024]{1,0:T(8,128)} async-done(((f32[64,16384]{1,0:T(8,128)}), f32[64,1024]{1,0:T(8,128)}) %reduce-scatter.2.cloned.1.call-update) | async-done | bytes 262160 | tf_op jit(solution)/shard_map/reduce_scatter | solution.py:50
  193.4 3.8 %convolution_multiply_fusion.1 = f32[512,64]{0,1:T(8,128)} fusion(f32[512,1024]{1,0:T(8,128)S(1)} %select_multiply_fusion, f32[64,1024]{1,0:T(8,128)} %reduce-scatter.2.cloned.1.call-done), kind=kOutput, calls=%fused_computation.8 | convolution fusion | flops 402751488 | bytes 2490368 | tf_op jit(solution)/shard_map/dot_general | solution.py:54
  197.2 0.0 all-reduce.3.cloned.1.call-update
  197.2 93.7 %all-reduce.3.cloned.1.call-done = (f32[512,512]{1,0:T(8,128)}, f32[512,64]{0,1:T(8,128)}) async-done(((f32[512,512]{1,0:T(8,128)}, f32[512,64]{0,1:T(8,128)}), (f32[512,512]{1,0:T(8,128)}, f32[512,64]{0,1:T(8,128)})) %all-reduce.3.cloned.1.call-update) | async-done | bytes 1179664 | tf_op jit(solution)/shard_map/psum | solution.py:55
  291.0 2.3 copy.11
  293.3 0.7 copy.12
  (7 shorter events, 0.1 us)
Async XLA Ops:
  7.2 47.2 %copy-start = (bf16[1024,64]{0,1:T(8,128)(2,1)S(1)}, bf16[1024,64]{0,1:T(8,128)(2,1)}, u32[]{:S(2)}) copy-start(bf16[1024,64]{0,1:T(8,128)(2,1)} %param.8) | copy-start | bytes 393220
  7.2 47.2 %all-gather.2.cloned.1.call-start = ((), (), s32[]{:S(2)}) async-start(), calls=%async_computation.1 | async-start | bytes 2228224 | tf_op jit(solution)/shard_map/all_gather | solution.py:47
  7.9 185.5 %reduce-scatter.2.cloned.1.call-start = ((), (), s32[]{:S(2)}) async-start(), calls=%async_computation.2 | async-start | bytes 4456448 | tf_op jit(solution)/shard_map/reduce_scatter | solution.py:50
  8.7 70.4 %copy-start.4 = (s32[1024]{0:T(1024)S(1)}, s32[1024]{0:T(1024)}, u32[]{:S(2)}) copy-start(s32[1024]{0:T(1024)} %param.11) | copy-start | bytes 12292
  122.1 0.9 copy-start.2
  122.1 1.7 copy-start.1
  122.2 168.8 %all-reduce.3.cloned.1.call-start = ((), (), s32[]{:S(2)}) async-start(), calls=%async_computation.3 | async-start | bytes 2359296 | tf_op jit(solution)/shard_map/psum | solution.py:55
  291.0 2.3 copy-start.3
Sparse Core Ops, SparseCore 0:
  10.2 44.1 all-gather.1
  122.3 71.1 reduce-scatter.1
  197.9 92.9 all-reduce.2
where the time goes:
time: 301 us; the launch traced here: 300 us
  waiting for transfers between devices  176 us (58%)
  matrix products  76 us (25%)
  other arithmetic  30.5 us (10%)
  between operations  13.8 us (5%)
  local copies, waits for them, and re-layouts  3.68 us (1%)
    psum x1, waiting for transfers between devices, local(): gram, rhs = lax.psum((gram_part, rhs_part), 'scen')  93.7 us
    all_gather x1, waiting for transfers between devices, local(): lax.all_gather(returns, 'scen', axis=1, tiled=True)  45.7 us
    dot_general x1, matrix products, line_terms(): return jnp.dot(onehot, payoff, precision=lax.Precision.HIGHEST)  43.1 us
    reduce_scatter x1, waiting for transfers between devices, local(): summed = lax.psum_scatter(partials, 'scen', scatter_dimension=1, tiled=True)  36 us
    mul x1, other arithmetic, basis_of(): basis = basis * factor  28.7 us
    dot_general x1, matrix products, line_terms(): jnp.dot(exp_rows, scen_returns, preferred_element_type=jnp.float32)  24.7 us
  transfers between devices with their start and end apart: 3, of which 3 were waited for; matrix products, arithmetic and copies ran while one was open for 12% of the time, Pallas kernels for 0%

commit v1 on v0

v1 whole, which is shorter than its diff:
```python
import functools
import math

import jax
import jax.numpy as jnp
from jax import lax
from jax.experimental import pallas as pl
from jax.experimental.pallas import tpu as pltpu
from jax.sharding import PartitionSpec as P

LINES = 64
TAIL = 16
CHUNK = 512
LOG2E = 1.4426950408889634
BF = jnp.bfloat16
F32 = jnp.float32
VMEM = 56 * 2**20


def params():
    return pltpu.CompilerParams(vmem_limit_bytes=VMEM)


def three_parts(x):
    a = x.astype(BF)
    b = (x - a.astype(F32)).astype(BF)
    c = (x - a.astype(F32) - b.astype(F32)).astype(BF)
    return a, b, c


def value_kernel(factors, count, *refs):
    rets, packs, out, rt, w, oh, lev = refs[0:2], refs[2 : 2 + count], *refs[2 + count :]
    own = rets[0].shape[1]
    for i in range(2):
        r = rets[i][...].astype(F32).T.astype(BF)
        rt[i * own : (i + 1) * own, :factors] = r
        rt[i * own : (i + 1) * own, factors:] = r
    points = packs[0].shape[1]
    lines = oh.shape[0]
    for i in range(count):
        at = slice(i * points, (i + 1) * points)
        e = packs[i][:factors, :].astype(F32) * LOG2E
        high = e.astype(BF)
        w[:factors, at] = high
        w[factors:, at] = (e - high.astype(F32)).astype(BF)
        tail = packs[i][factors:, :].astype(F32)
        lev[:, at] = tail[0:1] + tail[1:2] + tail[2:3]
        label = lax.broadcasted_iota(jnp.int32, (lines, points), 0).astype(F32)
        oh[:, at] = (label == tail[3:4]).astype(BF)

    def step(i, carry):
        s0 = pl.multiple_of(i * CHUNK, CHUNK)
        r = rt[pl.ds(s0, CHUNK), :]
        total = None
        for j in range(count):
            at = slice(j * points, (j + 1) * points)
            power = jnp.dot(r, w[:, at], preferred_element_type=F32)
            payoff = jnp.maximum(lev[:, at] - jnp.exp2(power), 0.0).astype(BF)
            part = lax.dot_general(
                payoff, oh[:, at], (((1,), (1,)), ((), ())), preferred_element_type=F32
            )
            total = part if total is None else total + part
        out[pl.ds(s0, CHUNK), :] = total
        return carry

    lax.fori_loop(0, 2 * own // CHUNK, step, 0)


def values_of(rets, packs, lines):
    factors, own = rets[0].shape
    points = packs[0].shape[1]
    count = len(packs)
    pairs = 2 * own * points * count
    return pl.pallas_call(
        functools.partial(value_kernel, factors, count),
        out_shape=jax.ShapeDtypeStruct((2 * own, lines), F32),
        scratch_shapes=[
            pltpu.VMEM((2 * own, 2 * factors), BF),
            pltpu.VMEM((2 * factors, points * count), BF),
            pltpu.VMEM((lines, points * count), BF),
            pltpu.VMEM((1, points * count), F32),
        ],
        compiler_params=params(),
        cost_estimate=pl.CostEstimate(
            flops=1700 * pairs, bytes_accessed=2**20, transcendentals=pairs
        ),
    )(*rets, *packs)


def basis_kernel(half, exps, d0, d1, high, low, gram):
    terms, count = exps.shape
    own = d0.shape[1]
    e = exps[...].astype(F32)
    row = lax.broadcasted_iota(jnp.int32, (count, count), 0)
    col = lax.broadcasted_iota(jnp.int32, (count, count), 1)
    upto = (row <= col).astype(BF)
    cum = jnp.dot(e.astype(BF), upto, preferred_element_type=F32)
    before = cum - e
    picks = [
        jnp.where((cum > t + 0.5) & (before < t + 0.5), 1.0, 0.0).astype(BF) for t in range(3)
    ]
    picks = [jnp.concatenate([p, p, p], axis=1) for p in picks]
    for i, d in enumerate((d0, d1)):
        parts = jnp.concatenate(three_parts(d[...]), axis=0)
        for c in range(own // CHUNK):
            part = parts[:, c * CHUNK : (c + 1) * CHUNK]
            x = [jnp.dot(p, part, preferred_element_type=F32) for p in picks]
            b = x[0] * x[1] * x[2]
            h = b.astype(BF)
            at = slice(i * own + c * CHUNK, i * own + (c + 1) * CHUNK)
            high[:, at] = h
            low[:, at] = (b - h.astype(F32)).astype(BF)
    rows = terms // 2
    r0 = pl.multiple_of(half[0] * rows, rows)
    gram[...] = lax.dot_general(
        high[pl.ds(r0, rows), :], high[...], (((1,), (1,)), ((), ())), preferred_element_type=F32
    )


def basis_of(half, exponents, drivers):
    terms, _ = exponents.shape
    own = drivers[0].shape[1]
    return pl.pallas_call(
        basis_kernel,
        in_specs=[pl.BlockSpec(memory_space=pltpu.SMEM)]
        + [pl.BlockSpec(memory_space=pltpu.VMEM)] * 3,
        out_shape=(
            jax.ShapeDtypeStruct((terms, 2 * own), BF),
            jax.ShapeDtypeStruct((terms, 2 * own), BF),
            jax.ShapeDtypeStruct((terms // 2, terms), F32),
        ),
        compiler_params=params(),
        cost_estimate=pl.CostEstimate(
            flops=6 * 10**9, bytes_accessed=6 * 2**20, transcendentals=0
        ),
    )(half, exponents, *drivers)


def rhs_kernel(scale, count, high, low, *refs):
    values, out = refs[:count], refs[count]
    v = values[0][...]
    for other in values[1:]:
        v = v + other[...]
    lines = v.shape[1]
    vh = v.astype(BF)
    vl = (v - vh.astype(F32)).astype(BF)
    both = jnp.concatenate([vh, vl], axis=1)
    a = jnp.dot(high[...], both, preferred_element_type=F32)
    b = jnp.dot(low[...], vh, preferred_element_type=F32)
    out[...] = ((a[:, :lines] + a[:, lines:] + b) * scale).T


def rhs_of(scale, high, low, values):
    terms = high.shape[0]
    lines = values[0].shape[1]
    return pl.pallas_call(
        functools.partial(rhs_kernel, scale, len(values)),
        out_shape=jax.ShapeDtypeStruct((lines, terms), F32),
        compiler_params=params(),
        cost_estimate=pl.CostEstimate(
            flops=3 * 10**9, bytes_accessed=6 * 2**20, transcendentals=0
        ),
    )(high, low, *values)


def place_kernel(scale, blocks, *refs):
    order, pieces, out = refs[0], refs[1:-1], refs[-1]
    rows = out.shape[0] // blocks
    k = 0
    for piece in pieces:
        for i in range(piece.shape[0] // rows):
            at = pl.multiple_of(order[k] * rows, rows)
            out[pl.ds(at, rows), :] = piece[i * rows : (i + 1) * rows, :] * scale
            k += 1


def placed(scale, blocks, order, pieces, terms):
    return pl.pallas_call(
        functools.partial(place_kernel, scale, blocks),
        in_specs=[pl.BlockSpec(memory_space=pltpu.SMEM)]
        + [pl.BlockSpec(memory_space=pltpu.VMEM)] * len(pieces),
        out_shape=jax.ShapeDtypeStruct((terms, terms), F32),
        compiler_params=params(),
        cost_estimate=pl.CostEstimate(
            flops=2**20, bytes_accessed=2 * 2**20, transcendentals=0
        ),
    )(order, *pieces)


def local(n, returns, exposures, guarantees, guar_type, line_ids, drivers, exponents):
    lines = LINES
    scen_total = returns.shape[1] * n
    all_points = exposures.shape[0] * n
    terms = exponents.shape[0]
    me = lax.axis_index("scen")

    def swap(x, mask):
        return lax.ppermute(x, "scen", [(i, i ^ mask) for i in range(n)])

    def bit(mask):
        return (me // mask) % 2

    far = [m for m in range(4, n, 4)]
    level = guarantees * (1.0 + 0.15 * guar_type.astype(F32))
    rows = [*three_parts(level), line_ids.astype(BF)]
    rows = jnp.stack(rows + [jnp.zeros_like(rows[0])] * (TAIL - 4))
    pack = jnp.concatenate([exposures.T, rows], axis=0)

    rets = (returns, swap(returns, 2))
    packs = {0: pack, 1: swap(pack, 1)}
    for m in far:
        packs[m] = swap(pack, m)
        packs[m ^ 1] = swap(packs[m], 1)
    both = (drivers, swap(drivers, 2))

    half = bit(2).astype(jnp.int32).reshape(1)
    high, low, gram = basis_of(half, exponents, both)

    groups = [[0, 1], [4, 5]] + [[m, m ^ 1, m + 4, m ^ 5] for m in range(8, n, 8)]
    values = [values_of(rets, [packs[k] for k in g], lines) for g in groups]
    scale = 1.0 / (math.sqrt(all_points / lines) * scen_total)
    rhs = rhs_of(scale, high, low, values)

    masks = [1] + [4 << i for i in range((n // 4).bit_length() - 1)]
    for m in masks:
        size = gram.shape[0] // 2
        mine = lax.dynamic_slice_in_dim(gram, bit(m) * size, size, 0)
        theirs = lax.dynamic_slice_in_dim(gram, (1 - bit(m)) * size, size, 0)
        gram = mine + swap(theirs, m)
    pieces, order = [gram], [0]
    for m in [*masks[:0:-1], 2, 1]:
        sent = pieces[0] if len(pieces) == 1 else jnp.concatenate(pieces, axis=0)
        pieces.append(swap(sent, m))
        order += [k ^ m for k in order]

    def block_of(k):
        who = me ^ k
        place = (who // 2) % 2
        for m in masks:
            place = place * 2 + (who // m) % 2
        return place

    order = jnp.stack([block_of(k) for k in order]).astype(jnp.int32)
    gram = placed(1.0 / scen_total, n, order, pieces, terms)

    for m in [1, 2] + masks[1:]:
        rhs = rhs + swap(rhs, m)
    return (gram, rhs.T)


def solution(mesh):
    spots = (
        P(None, ("grp", "scen")),
        P(("grp", "scen"), None),
        P(("grp", "scen")),
        P(("grp", "scen")),
        P(("grp", "scen")),
        P(None, ("grp", "scen")),
        P(),
    )
    return jax.shard_map(
        functools.partial(local, mesh.shape["scen"]),
        mesh=mesh,
        in_specs=spots,
        out_specs=(P("grp", None), P("grp", None)),
        check_vma=False,
    )
```

time: 301 us -> 109 us (0.36)
  waiting for transfers between devices: 176 us -> 27.8 us
  matrix products: 76 us -> 0 us
  Pallas kernels: 0 us -> 48.8 us
  other arithmetic: 30.5 us -> 2.73 us
  starting transfers between devices: 0.3 us -> 21.2 us
  between operations: 13.8 us -> 0.92 us
  local copies, waits for them, and re-layouts: 3.68 us -> 7.62 us
    psum x1 -> x0, waiting for transfers between devices: 93.7 us -> none  [local(): gram, rhs = lax.psum((gram_part, rhs_part), 'scen')]
    dot_general x4 -> x0, matrix products: 76 us -> none  [the longest x1 43.1 us: line_terms(): return jnp.dot(onehot, payoff, precision=lax.Precision.HIGHEST)]
    pallas_call x0 -> x6, Pallas kernels: none -> 48.8 us  [the longest x3 35.9 us: values_of(): pl.pallas_call(functools.partial(value_kernel, factors, count), out_shape...]
    all_gather x1 -> x0, waiting for transfers between devices: 45.7 us -> none  [local(): lax.all_gather(returns, 'scen', axis=1, tiled=True)]
    reduce_scatter x1 -> x0, waiting for transfers between devices: 36 us -> none  [local(): summed = lax.psum_scatter(partials, 'scen', scatter_dimension=1, tiled=True)]
    mul x2 -> x0, other arithmetic: 29.4 us -> none  [the longest x1 28.7 us: basis_of(): basis = basis * factor]
    ppermute x0 -> x20, waiting for transfers between devices: none -> 27.8 us  [swap(): return lax.ppermute(x, 'scen', [(i, i ^ mask) for i in range(n)])]
    ppermute x0 -> x20, starting transfers between devices: none -> 21.2 us  [swap(): return lax.ppermute(x, 'scen', [(i, i ^ mask) for i in range(n)])]
  transfers between devices with their start and end apart: 3 -> 20, of which waited for: 3 -> 7; matrix products, arithmetic and copies ran while one was open for 12% -> 5% of each run, Pallas kernels for 0% -> 38%
where the time goes in v1:
time: 109 us
  Pallas kernels  48.8 us (45%)
  waiting for transfers between devices  27.8 us (26%)
  starting transfers between devices  21.2 us (19%)
  local copies, waits for them, and re-layouts  7.62 us (7%)
  other arithmetic  2.73 us (3%)
    pallas_call x3, Pallas kernels, values_of(): pl.pallas_call(functools.partial(value_kernel, factors, count), out_shape...  35.9 us
    ppermute x20, waiting for transfers between devices, swap(): return lax.ppermute(x, 'scen', [(i, i ^ mask) for i in range(n)])  27.8 us
    ppermute x20, starting transfers between devices, swap(): return lax.ppermute(x, 'scen', [(i, i ^ mask) for i in range(n)])  21.2 us
    unnamed x41, local copies, waits for them, and re-layouts  5.88 us
    pallas_call x1, Pallas kernels, basis_of(): pl.pallas_call(basis_kernel, in_specs=[pl.BlockSpec(memory_space=pltpu.SM...  5.36 us
    pallas_call x1, Pallas kernels, rhs_of(): pl.pallas_call(functools.partial(rhs_kernel, scale, len(values)), out_sha...  5.26 us
    pallas_call x1, Pallas kernels, placed(): pl.pallas_call(functools.partial(place_kernel, scale, blocks), in_specs=[...  2.31 us
  transfers between devices with their start and end apart: 20, of which 7 were waited for; matrix products, arithmetic and copies ran while one was open for 5% of the time, Pallas kernels for 38%

profile of v1, /device:TPU:0, one launch (start us, length us, event | category | flops | bytes accessed | tf_op | source)
XLA Modules:
  0.0 109.1 jit_solution(11713033143651904128)
XLA Ops:
  0.6 3.0 %collective-permute-start = (f32[40,1024]{1,0:T(8,128)}, f32[40,1024]{1,0:T(8,128)S(1)}, u32[]{:S(2)}, u32[]{:S(2)}) collective-permute-start(f32[40,1024]{1,0:T(8,128)} %d0.1), channel_id=1, source_target_pairs={{0,2},{1,3},{2,0},{3,1},{4,6},{5,7},{6,4},{7,5},{8,10},{9,11},{10,... | collective-permute-start | bytes 491528 | tf_op jit(solution)/shard_map/ppermute | solution.py:198
  3.7 1.7 %copy.9.exps = s32[512,40]{1,0:T(8,128)} copy(s32[512,40]{0,1:T(8,128)} %param.13) | data formatting | bytes 163840 | tf_op args[6]
  5.4 2.7 %collective-permute-done.d1 = f32[40,1024]{1,0:T(8,128)S(1)} collective-permute-done((f32[40,1024]{1,0:T(8,128)}, f32[40,1024]{1,0:T(8,128)S(1)}, u32[]{:S(2)}, u32[]{:S(2)}) %collective-permute-start) | collective-permute-done | bytes 163872 | tf_op jit(solution)/shard_map/ppermute | solution.py:198
  8.1 0.7 copy-done.14
  8.8 5.4 %shard_map.86 = (bf16[512,2048]{1,0:T(8,128)(2,1)}, bf16[512,2048]{1,0:T(8,128)(2,1)}, f32[256,512]{1,0:T(8,128)}) custom-call(s32[1]{0:T(128)} %bitcast.16.half, s32[512,40]{1,0:T(8,128)} %copy.9.exps, f32[40,1024]{1,0:T(8,128)} %d0.1, f32[40,1024]{1,0:T(8,128)} %copy-done.14), custom_call_target="tpu_custom_call" | custom-call | flops 6000000000 | bytes 6291456 | tf_op jit(solution)/shard_map/pallas_call | solution.py:123
  14.1 1.0 constant_dynamic-slice_fusion.2
  15.4 3.9 %collective-permute-start.14 = (bf16[80,1024]{1,0:T(8,128)(2,1)S(1)}, bf16[80,1024]{1,0:T(8,128)(2,1)S(1)}, u32[]{:S(2)}, u32[]{:S(2)}) collective-permute-start(bf16[80,1024]{1,0:T(8,128)(2,1)S(1)} %concatenate.23.refs_2_), channel_id=1, source_target_pairs={{0,12},{1,13},{2,14},{3,15},{4,8},{5,9},{6,10},{7,11},{8,4},{9,5},... | collective-permute-start | bytes 491528 | tf_op jit(solution)/shard_map/ppermute | solution.py:198
  19.9 1.0 dynamic-slice_add_fusion
  21.0 1.5 %collective-permute-start.2 = (f32[64,512]{1,0:T(8,128)S(1)}, f32[64,512]{1,0:T(8,128)S(1)}, u32[]{:S(2)}, u32[]{:S(2)}) collective-permute-start(f32[64,512]{1,0:T(8,128)S(1)} %constant_dynamic-slice_fusion.1), channel_id=1, source_target_pairs={{0,4},{1,5},{2,6},{3,7},{4,0},{5,1},{6,2},{7,3},{8,12},{9,13},{10,... | collective-permute-start | bytes 393224 | tf_op jit(solution)/shard_map/ppermute | solution.py:198
  22.4 2.1 %collective-permute-done.14.refs_4_ = bf16[80,1024]{1,0:T(8,128)(2,1)S(1)} collective-permute-done((bf16[80,1024]{1,0:T(8,128)(2,1)S(1)}, bf16[80,1024]{1,0:T(8,128)(2,1)S(1)}, u32[]{:S(2)}, u32[]{:S(2)}) %collective-permute-start.14) | collective-permute-done | bytes 163872 | tf_op jit(solution)/shard_map/ppermute | solution.py:198
  24.5 1.6 %collective-permute-start.8 = (bf16[64,1024]{1,0:T(8,128)(2,1)S(1)}, bf16[64,1024]{1,0:T(8,128)(2,1)S(1)}, u32[]{:S(2)}, u32[]{:S(2)}) collective-permute-start(bf16[64,1024]{1,0:T(8,128)(2,1)S(1)} %copy-done.18), channel_id=1, source_target_pairs={{0,2},{1,3},{2,0},{3,1},{4,6},{5,7},{6,4},{7,5},{8,10},{9,11},{10,... | collective-permute-start | bytes 393224 | tf_op jit(solution)/shard_map/ppermute | solution.py:198
  26.1 7.8 %collective-permute-done.12.refs_2_ = bf16[80,1024]{1,0:T(8,128)(2,1)S(1)} collective-permute-done((bf16[80,1024]{1,0:T(8,128)(2,1)S(1)}, bf16[80,1024]{1,0:T(8,128)(2,1)S(1)}, u32[]{:S(2)}, u32[]{:S(2)}) %collective-permute-start.12) | collective-permute-done | bytes 163872 | tf_op jit(solution)/shard_map/ppermute | solution.py:198
  34.6 2.7 %collective-permute-start.3 = (f32[32,512]{1,0:T(8,128)S(1)}, f32[32,512]{1,0:T(8,128)S(1)}, u32[]{:S(2)}, u32[]{:S(2)}) collective-permute-start(f32[32,512]{1,0:T(8,128)S(1)} %constant_dynamic-slice_fusion), channel_id=1, source_target_pairs={{0,8},{1,9},{2,10},{3,11},{4,12},{5,13},{6,14},{7,15},{8,0},{9,1},... | collective-permute-start | bytes 196616 | tf_op jit(solution)/shard_map/ppermute | solution.py:198
  38.0 10.5 %shard_map.88.refs_0_ = f32[2048,64]{1,0:T(8,128)} custom-call(bf16[64,1024]{1,0:T(8,128)(2,1)} %refs_0_.5, bf16[64,1024]{1,0:T(8,128)(2,1)} %copy-done.19, bf16[80,1024]{1,0:T(8,128)(2,1)} %copy-done.5, bf16[80,1024]{1,0:T(8,128)(2,1)} %copy-done.13), custom_call_target="tpu_custom_call" | custom-call | flops 7130316800 | bytes 1048576 | tf_op jit(solution)/shard_map/pallas_call | solution.py:74
  48.5 0.7 collective-permute-start.4
  49.2 0.7 copy-done.16
  50.6 15.0 %shard_map.90.refs_2_ = f32[2048,64]{1,0:T(8,128)} custom-call(bf16[64,1024]{1,0:T(8,128)(2,1)} %refs_0_.5, bf16[64,1024]{1,0:T(8,128)(2,1)} %copy-done.19, bf16[80,1024]{1,0:T(8,128)(2,1)} %copy-done.12, bf16[80,1024]{1,0:T(8,128)(2,1)} %copy-done.17, bf16[80,1024]{1,0:T(8,128)(2,1)} %copy-done.11, bf16[80,1024]{1,0:T(8,128)(2,1)} %copy-done.16), custom_call_target="tpu_custom_call" | custom-call | flops 14260633600 | bytes 1048576 | tf_op jit(solution)/shard_map/pallas_call | solution.py:74
  65.6 1.3 %collective-permute-start.5 = (f32[64,512]{1,0:T(8,128)S(1)}, f32[64,512]{1,0:T(8,128)S(1)}, u32[]{:S(2)}, u32[]{:S(2)}) collective-permute-start(f32[64,512]{1,0:T(8,128)S(1)} %pad_maximum_fusion.2), channel_id=1, source_target_pairs={{0,4},{1,5},{2,6},{3,7},{4,0},{5,1},{6,2},{7,3},{8,12},{9,13},{10,... | collective-permute-start | bytes 393224 | tf_op jit(solution)/shard_map/ppermute | solution.py:198
  66.9 0.7 copy-done.15
  67.6 10.4 %shard_map.89.refs_1_ = f32[2048,64]{1,0:T(8,128)} custom-call(bf16[64,1024]{1,0:T(8,128)(2,1)} %refs_0_.5, bf16[64,1024]{1,0:T(8,128)(2,1)} %copy-done.19, bf16[80,1024]{1,0:T(8,128)(2,1)} %copy-done.10, bf16[80,1024]{1,0:T(8,128)(2,1)} %copy-done.15), custom_call_target="tpu_custom_call" | custom-call | flops 7130316800 | bytes 1048576 | tf_op jit(solution)/shard_map/pallas_call | solution.py:74
  78.0 1.6 %collective-permute-start.6 = (f32[128,512]{1,0:T(8,128)S(1)}, f32[128,512]{1,0:T(8,128)S(1)}, u32[]{:S(2)}, u32[]{:S(2)}) collective-permute-start(f32[128,512]{1,0:T(8,128)S(1)} %pad_maximum_fusion.1), channel_id=1, source_target_pairs={{0,2},{1,3},{2,0},{3,1},{4,6},{5,7},{6,4},{7,5},{8,10},{9,11},{10,... | collective-permute-start | bytes 786440 | tf_op jit(solution)/shard_map/ppermute | solution.py:198
  79.6 5.3 %shard_map.91 = f32[64,512]{1,0:T(8,128)} custom-call(bf16[512,2048]{1,0:T(8,128)(2,1)} %get-tuple-element.6.high, bf16[512,2048]{1,0:T(8,128)(2,1)} %get-tuple-element.7.low, f32[2048,64]{1,0:T(8,128)} %shard_map.88.refs_0_, f32[2048,64]{1,0:T(8,128)} %shard_map.89.refs_1_, f32[2048,64]{1,0:T(8,128)} %shard_map.90.refs_2_), custom_call_target="tpu_custom_call" | custom-call | flops 3000000000 | bytes 6291456 | tf_op jit(solution)/shard_map/pallas_call | solution.py:156
  84.8 1.6 %collective-permute-done.16 = f32[64,512]{1,0:T(8,128)S(1)} collective-permute-done((f32[64,512]{1,0:T(8,128)}, f32[64,512]{1,0:T(8,128)S(1)}, u32[]{:S(2)}, u32[]{:S(2)}) %collective-permute-start.16) | collective-permute-done | bytes 131104 | tf_op jit(solution)/shard_map/ppermute | solution.py:198
  86.4 0.9 add.576
  88.0 4.9 %collective-permute-done.17 = f32[64,512]{1,0:T(8,128)S(1)} collective-permute-done((f32[64,512]{1,0:T(8,128)S(1)}, f32[64,512]{1,0:T(8,128)S(1)}, u32[]{:S(2)}, u32[]{:S(2)}) %collective-permute-start.17) | collective-permute-done | bytes 131104 | tf_op jit(solution)/shard_map/ppermute | solution.py:198
  92.9 0.8 collective-permute-start.18
  93.8 4.2 %collective-permute-done.18 = f32[64,512]{1,0:T(8,128)S(1)} collective-permute-done((f32[64,512]{1,0:T(8,128)S(1)}, f32[64,512]{1,0:T(8,128)S(1)}, u32[]{:S(2)}, u32[]{:S(2)}) %collective-permute-start.18) | collective-permute-done | bytes 131104 | tf_op jit(solution)/shard_map/ppermute | solution.py:198
  98.0 2.1 %collective-permute-start.19 = (f32[64,512]{1,0:T(8,128)S(1)}, f32[64,512]{1,0:T(8,128)S(1)}, u32[]{:S(2)}, u32[]{:S(2)}) collective-permute-start(f32[64,512]{1,0:T(8,128)S(1)} %add.578), channel_id=1, source_target_pairs={{0,8},{1,9},{2,10},{3,11},{4,12},{5,13},{6,14},{7,15},{8,0},{9,1},... | collective-permute-start | bytes 393224 | tf_op jit(solution)/shard_map/ppermute | solution.py:198
  100.8 4.6 %collective-permute-done.19 = f32[64,512]{1,0:T(8,128)S(1)} collective-permute-done((f32[64,512]{1,0:T(8,128)S(1)}, f32[64,512]{1,0:T(8,128)S(1)}, u32[]{:S(2)}, u32[]{:S(2)}) %collective-permute-start.19) | collective-permute-done | bytes 131104 | tf_op jit(solution)/shard_map/ppermute | solution.py:198
  105.3 0.7 add_bitcast_fusion
  106.0 0.8 copy-done.4
  106.8 2.3 %shard_map.87 = f32[512,512]{1,0:T(8,128)} custom-call(s32[16]{0:T(128)} %stack.79.refs_0_, f32[32,512]{1,0:T(8,128)} %copy-done, f32[32,512]{1,0:T(8,128)} %copy-done.3, f32[64,512]{1,0:T(8,128)} %copy-done.1, f32[128,512]{1,0:T(8,128)} %copy-done.2, f32[256,512]{1,0:T(8,128)} %copy-done.4), custom_call_target="tpu_custom_call" | custom-call | flops 1048576 | bytes 2097152 | tf_op jit(solution)/shard_map/pallas_call | solution.py:178
  (78 shorter events, 4.3 us)
Async XLA Ops:
  0.6 7.4 %collective-permute-start = (f32[40,1024]{1,0:T(8,128)}, f32[40,1024]{1,0:T(8,128)S(1)}, u32[]{:S(2)}, u32[]{:S(2)}) collective-permute-start(f32[40,1024]{1,0:T(8,128)} %d0.1), channel_id=1, source_target_pairs={{0,2},{1,3},{2,0},{3,1},{4,6},{5,7},{6,4},{7,5},{8,10},{9,11},{10,... | collective-permute-start | bytes 491528 | tf_op jit(solution)/shard_map/ppermute | solution.py:198
  8.7 6.5 %copy-start.7 = (f32[1024]{0:T(1024)S(1)}, f32[1024]{0:T(1024)}, u32[]{:S(2)}) copy-start(f32[1024]{0:T(1024)} %param.9) | copy-start | bytes 12292
  8.8 6.5 %copy-start.8 = (s32[1024]{0:T(1024)S(1)}, s32[1024]{0:T(1024)}, u32[]{:S(2)}) copy-start(s32[1024]{0:T(1024)} %param.10) | copy-start | bytes 12292
  8.8 6.6 %copy-start.6 = (bf16[1024,64]{0,1:T(8,128)(2,1)S(1)}, bf16[1024,64]{0,1:T(8,128)(2,1)}, u32[]{:S(2)}) copy-start(bf16[1024,64]{0,1:T(8,128)(2,1)} %param.8) | copy-start | bytes 393220
  14.1 10.4 %copy-start.18 = (bf16[64,1024]{1,0:T(8,128)(2,1)S(1)}, bf16[64,1024]{1,0:T(8,128)(2,1)}, u32[]{:S(2)}) copy-start(bf16[64,1024]{1,0:T(8,128)(2,1)} %refs_0_.5) | copy-start | bytes 393220
  15.1 4.8 %collective-permute-start.1 = (f32[128,512]{1,0:T(8,128)S(1)}, f32[128,512]{1,0:T(8,128)S(1)}, u32[]{:S(2)}, u32[]{:S(2)}) collective-permute-start(f32[128,512]{1,0:T(8,128)S(1)} %constant_dynamic-slice_fusion.2), channel_id=1, source_target_pairs={{0,1},{1,0},{2,3},{3,2},{4,5},{5,4},{6,7},{7,6},{8,9},{9,8},{10,11... | collective-permute-start | bytes 786440 | tf_op jit(solution)/shard_map/ppermute | solution.py:198
  15.4 21.9 %copy-start.5 = (bf16[80,1024]{1,0:T(8,128)(2,1)}, bf16[80,1024]{1,0:T(8,128)(2,1)S(1)}, u32[]{:S(2)}) copy-start(bf16[80,1024]{1,0:T(8,128)(2,1)S(1)} %concatenate.23.refs_2_) | copy-start | bytes 491524
  15.4 9.1 %collective-permute-start.14 = (bf16[80,1024]{1,0:T(8,128)(2,1)S(1)}, bf16[80,1024]{1,0:T(8,128)(2,1)S(1)}, u32[]{:S(2)}, u32[]{:S(2)}) collective-permute-start(bf16[80,1024]{1,0:T(8,128)(2,1)S(1)} %concatenate.23.refs_2_), channel_id=1, source_target_pairs={{0,12},{1,13},{2,14},{3,15},{4,8},{5,9},{6,10},{7,11},{8,4},{9,5},... | collective-permute-start | bytes 491528 | tf_op jit(solution)/shard_map/ppermute | solution.py:198
  19.3 14.6 %collective-permute-start.12 = (bf16[80,1024]{1,0:T(8,128)(2,1)S(1)}, bf16[80,1024]{1,0:T(8,128)(2,1)S(1)}, u32[]{:S(2)}, u32[]{:S(2)}) collective-permute-start(bf16[80,1024]{1,0:T(8,128)(2,1)S(1)} %concatenate.23.refs_2_), channel_id=1, source_target_pairs={{0,8},{1,9},{2,10},{3,11},{4,12},{5,13},{6,14},{7,15},{8,0},{9,1},... | collective-permute-start | bytes 491528 | tf_op jit(solution)/shard_map/ppermute | solution.py:198
  19.3 14.6 %collective-permute-start.10 = (bf16[80,1024]{1,0:T(8,128)(2,1)S(1)}, bf16[80,1024]{1,0:T(8,128)(2,1)S(1)}, u32[]{:S(2)}, u32[]{:S(2)}) collective-permute-start(bf16[80,1024]{1,0:T(8,128)(2,1)S(1)} %concatenate.23.refs_2_), channel_id=1, source_target_pairs={{0,4},{1,5},{2,6},{3,7},{4,0},{5,1},{6,2},{7,3},{8,12},{9,13},{10,... | collective-permute-start | bytes 491528 | tf_op jit(solution)/shard_map/ppermute | solution.py:198
  21.0 13.5 %collective-permute-start.2 = (f32[64,512]{1,0:T(8,128)S(1)}, f32[64,512]{1,0:T(8,128)S(1)}, u32[]{:S(2)}, u32[]{:S(2)}) collective-permute-start(f32[64,512]{1,0:T(8,128)S(1)} %constant_dynamic-slice_fusion.1), channel_id=1, source_target_pairs={{0,4},{1,5},{2,6},{3,7},{4,0},{5,1},{6,2},{7,3},{8,12},{9,13},{10,... | collective-permute-start | bytes 393224 | tf_op jit(solution)/shard_map/ppermute | solution.py:198
  22.4 14.9 %collective-permute-start.9 = (bf16[80,1024]{1,0:T(8,128)(2,1)S(1)}, bf16[80,1024]{1,0:T(8,128)(2,1)S(1)}, u32[]{:S(2)}, u32[]{:S(2)}) collective-permute-start(bf16[80,1024]{1,0:T(8,128)(2,1)S(1)} %concatenate.23.refs_2_), channel_id=1, source_target_pairs={{0,1},{1,0},{2,3},{3,2},{4,5},{5,4},{6,7},{7,6},{8,9},{9,8},{10,11... | collective-permute-start | bytes 491528 | tf_op jit(solution)/shard_map/ppermute | solution.py:198
  24.5 24.0 %copy-start.11 = (bf16[80,1024]{1,0:T(8,128)(2,1)}, bf16[80,1024]{1,0:T(8,128)(2,1)S(1)}, u32[]{:S(2)}) copy-start(bf16[80,1024]{1,0:T(8,128)(2,1)S(1)} %collective-permute-done.14.refs_4_) | copy-start | bytes 491524
  24.5 10.1 %collective-permute-start.8 = (bf16[64,1024]{1,0:T(8,128)(2,1)S(1)}, bf16[64,1024]{1,0:T(8,128)(2,1)S(1)}, u32[]{:S(2)}, u32[]{:S(2)}) collective-permute-start(bf16[64,1024]{1,0:T(8,128)(2,1)S(1)} %copy-done.18), channel_id=1, source_target_pairs={{0,2},{1,3},{2,0},{3,1},{4,6},{5,7},{6,4},{7,5},{8,10},{9,11},{10,... | collective-permute-start | bytes 393224 | tf_op jit(solution)/shard_map/ppermute | solution.py:198
  33.9 14.5 %copy-start.12 = (bf16[80,1024]{1,0:T(8,128)(2,1)}, bf16[80,1024]{1,0:T(8,128)(2,1)S(1)}, u32[]{:S(2)}) copy-start(bf16[80,1024]{1,0:T(8,128)(2,1)S(1)} %collective-permute-done.12.refs_2_) | copy-start | bytes 491524
  33.9 15.3 %collective-permute-start.15 = (bf16[80,1024]{1,0:T(8,128)(2,1)S(1)}, bf16[80,1024]{1,0:T(8,128)(2,1)S(1)}, u32[]{:S(2)}, u32[]{:S(2)}) collective-permute-start(bf16[80,1024]{1,0:T(8,128)(2,1)S(1)} %collective-permute-done.14.refs_4_), channel_id=1, source_target_pairs={{0,1},{1,0},{2,3},{3,2},{4,5},{5,4},{6,7},{7,6},{8,9},{9,8},{10,11... | collective-permute-start | bytes 491528 | tf_op jit(solution)/shard_map/ppermute | solution.py:198
  33.9 14.5 %copy-start.10 = (bf16[80,1024]{1,0:T(8,128)(2,1)}, bf16[80,1024]{1,0:T(8,128)(2,1)S(1)}, u32[]{:S(2)}) copy-start(bf16[80,1024]{1,0:T(8,128)(2,1)S(1)} %collective-permute-done.10.refs_2_) | copy-start | bytes 491524
  34.0 15.3 %collective-permute-start.13 = (bf16[80,1024]{1,0:T(8,128)(2,1)S(1)}, bf16[80,1024]{1,0:T(8,128)(2,1)S(1)}, u32[]{:S(2)}, u32[]{:S(2)}) collective-permute-start(bf16[80,1024]{1,0:T(8,128)(2,1)S(1)} %collective-permute-done.12.refs_2_), channel_id=1, source_target_pairs={{0,1},{1,0},{2,3},{3,2},{4,5},{5,4},{6,7},{7,6},{8,9},{9,8},{10,11... | collective-permute-start | bytes 491528 | tf_op jit(solution)/shard_map/ppermute | solution.py:198
  34.5 32.5 %collective-permute-start.11 = (bf16[80,1024]{1,0:T(8,128)(2,1)S(1)}, bf16[80,1024]{1,0:T(8,128)(2,1)S(1)}, u32[]{:S(2)}, u32[]{:S(2)}) collective-permute-start(bf16[80,1024]{1,0:T(8,128)(2,1)S(1)} %collective-permute-done.10.refs_2_), channel_id=1, source_target_pairs={{0,1},{1,0},{2,3},{3,2},{4,5},{5,4},{6,7},{7,6},{8,9},{9,8},{10,11... | collective-permute-start | bytes 491528 | tf_op jit(solution)/shard_map/ppermute | solution.py:198
  34.6 13.9 %collective-permute-start.3 = (f32[32,512]{1,0:T(8,128)S(1)}, f32[32,512]{1,0:T(8,128)S(1)}, u32[]{:S(2)}, u32[]{:S(2)}) collective-permute-start(f32[32,512]{1,0:T(8,128)S(1)} %constant_dynamic-slice_fusion), channel_id=1, source_target_pairs={{0,8},{1,9},{2,10},{3,11},{4,12},{5,13},{6,14},{7,15},{8,0},{9,1},... | collective-permute-start | bytes 196616 | tf_op jit(solution)/shard_map/ppermute | solution.py:198
  48.5 39.4 %copy-start = (f32[32,512]{1,0:T(8,128)}, f32[32,512]{1,0:T(8,128)S(1)}, u32[]{:S(2)}) copy-start(f32[32,512]{1,0:T(8,128)S(1)} %dynamic-slice_add_fusion.2.refs_1_) | copy-start | bytes 196612
  48.5 17.1 %collective-permute-start.4 = (f32[32,512]{1,0:T(8,128)S(1)}, f32[32,512]{1,0:T(8,128)S(1)}, u32[]{:S(2)}, u32[]{:S(2)}) collective-permute-start(f32[32,512]{1,0:T(8,128)S(1)} %dynamic-slice_add_fusion.2.refs_1_), channel_id=1, source_target_pairs={{0,8},{1,9},{2,10},{3,11},{4,12},{5,13},{6,14},{7,15},{8,0},{9,1},... | collective-permute-start | bytes 196616 | tf_op jit(solution)/shard_map/ppermute | solution.py:198
  65.6 22.3 %copy-start.3 = (f32[32,512]{1,0:T(8,128)}, f32[32,512]{1,0:T(8,128)S(1)}, u32[]{:S(2)}) copy-start(f32[32,512]{1,0:T(8,128)S(1)} %collective-permute-done.4.refs_2_) | copy-start | bytes 196612
  65.6 12.4 %collective-permute-start.5 = (f32[64,512]{1,0:T(8,128)S(1)}, f32[64,512]{1,0:T(8,128)S(1)}, u32[]{:S(2)}, u32[]{:S(2)}) collective-permute-start(f32[64,512]{1,0:T(8,128)S(1)} %pad_maximum_fusion.2), channel_id=1, source_target_pairs={{0,4},{1,5},{2,6},{3,7},{4,0},{5,1},{6,2},{7,3},{8,12},{9,13},{10,... | collective-permute-start | bytes 393224 | tf_op jit(solution)/shard_map/ppermute | solution.py:198
  78.0 9.9 %copy-start.1 = (f32[64,512]{1,0:T(8,128)}, f32[64,512]{1,0:T(8,128)S(1)}, u32[]{:S(2)}) copy-start(f32[64,512]{1,0:T(8,128)S(1)} %collective-permute-done.5.refs_3_) | copy-start | bytes 393220
  78.0 9.9 %collective-permute-start.6 = (f32[128,512]{1,0:T(8,128)S(1)}, f32[128,512]{1,0:T(8,128)S(1)}, u32[]{:S(2)}, u32[]{:S(2)}) collective-permute-start(f32[128,512]{1,0:T(8,128)S(1)} %pad_maximum_fusion.1), channel_id=1, source_target_pairs={{0,2},{1,3},{2,0},{3,1},{4,6},{5,7},{6,4},{7,5},{8,10},{9,11},{10,... | collective-permute-start | bytes 786440 | tf_op jit(solution)/shard_map/ppermute | solution.py:198
  84.8 1.6 %collective-permute-start.16 = (f32[64,512]{1,0:T(8,128)}, f32[64,512]{1,0:T(8,128)S(1)}, u32[]{:S(2)}, u32[]{:S(2)}) collective-permute-start(f32[64,512]{1,0:T(8,128)} %shard_map.91), channel_id=1, source_target_pairs={{0,1},{1,0},{2,3},{3,2},{4,5},{5,4},{6,7},{7,6},{8,9},{9,8},{10,11... | collective-permute-start | bytes 393224 | tf_op jit(solution)/shard_map/ppermute | solution.py:198
  87.3 5.6 %collective-permute-start.17 = (f32[64,512]{1,0:T(8,128)S(1)}, f32[64,512]{1,0:T(8,128)S(1)}, u32[]{:S(2)}, u32[]{:S(2)}) collective-permute-start(f32[64,512]{1,0:T(8,128)S(1)} %add.576), channel_id=1, source_target_pairs={{0,2},{1,3},{2,0},{3,1},{4,6},{5,7},{6,4},{7,5},{8,10},{9,11},{10,... | collective-permute-start | bytes 393224 | tf_op jit(solution)/shard_map/ppermute | solution.py:198
  87.9 12.2 %copy-start.2 = (f32[128,512]{1,0:T(8,128)}, f32[128,512]{1,0:T(8,128)S(1)}, u32[]{:S(2)}) copy-start(f32[128,512]{1,0:T(8,128)S(1)} %collective-permute-done.6.refs_4_) | copy-start | bytes 786436
  88.0 18.1 %collective-permute-start.7 = (f32[256,512]{1,0:T(8,128)S(1)}, f32[256,512]{1,0:T(8,128)S(1)}, u32[]{:S(2)}, u32[]{:S(2)}) collective-permute-start(f32[256,512]{1,0:T(8,128)S(1)} %pad_maximum_fusion), channel_id=1, source_target_pairs={{0,1},{1,0},{2,3},{3,2},{4,5},{5,4},{6,7},{7,6},{8,9},{9,8},{10,11... | collective-permute-start | bytes 1572872 | tf_op jit(solution)/shard_map/ppermute | solution.py:198
  92.9 5.0 %collective-permute-start.18 = (f32[64,512]{1,0:T(8,128)S(1)}, f32[64,512]{1,0:T(8,128)S(1)}, u32[]{:S(2)}, u32[]{:S(2)}) collective-permute-start(f32[64,512]{1,0:T(8,128)S(1)} %add.577), channel_id=1, source_target_pairs={{0,4},{1,5},{2,6},{3,7},{4,0},{5,1},{6,2},{7,3},{8,12},{9,13},{10,... | collective-permute-start | bytes 393224 | tf_op jit(solution)/shard_map/ppermute | solution.py:198
  98.0 7.3 %collective-permute-start.19 = (f32[64,512]{1,0:T(8,128)S(1)}, f32[64,512]{1,0:T(8,128)S(1)}, u32[]{:S(2)}, u32[]{:S(2)}) collective-permute-start(f32[64,512]{1,0:T(8,128)S(1)} %add.578), channel_id=1, source_target_pairs={{0,8},{1,9},{2,10},{3,11},{4,12},{5,13},{6,14},{7,15},{8,0},{9,1},... | collective-permute-start | bytes 393224 | tf_op jit(solution)/shard_map/ppermute | solution.py:198
  (8 other events, 13.3 us)

commit v2 on v1

v2 whole, which is shorter than its diff:
```python
import functools
import math

import jax
import jax.numpy as jnp
from jax import lax
from jax.experimental import pallas as pl
from jax.experimental.pallas import tpu as pltpu
from jax.sharding import PartitionSpec as P

LINES = 64
TAIL = 16
CHUNK = 512
LOG2E = 1.4426950408889634
BF = jnp.bfloat16
F32 = jnp.float32
VMEM = 24 * 2**20


def params():
    return pltpu.CompilerParams(vmem_limit_bytes=VMEM)


def three_parts(x):
    a = x.astype(BF)
    b = (x - a.astype(F32)).astype(BF)
    c = (x - a.astype(F32) - b.astype(F32)).astype(BF)
    return a, b, c


def value_kernel(plan, count, earlier, scale, *refs):
    blocks = len(plan)
    rts, refs = refs[:blocks], refs[blocks:]
    packs, refs = refs[:count], refs[count:]
    if scale:
        before, refs = refs[: len(earlier)], refs[len(earlier) :]
        basis, refs = refs[: 2 * blocks], refs[2 * blocks :]
        out, w, oh, lev, held, sems = refs
        loads = [
            pltpu.make_async_copy(basis[i], held.at[i], sems.at[i]) for i in range(2 * blocks)
        ]
        for load in loads:
            load.start()
    else:
        outs, (w, oh, lev) = refs[:blocks], refs[blocks:]
    own, double = rts[0].shape
    factors = double // 2
    points = packs[0].shape[1]
    lines = oh.shape[0]
    for i in range(count):
        at = slice(i * points, (i + 1) * points)
        e = packs[i][:factors, :].astype(F32) * LOG2E
        high = e.astype(BF)
        w[:factors, at] = high
        w[factors:, at] = (e - high.astype(F32)).astype(BF)
        tail = packs[i][factors:, :].astype(F32)
        lev[:, at] = tail[0:1] + tail[1:2] + tail[2:3]
        label = lax.broadcasted_iota(jnp.int32, (lines, points), 0).astype(F32)
        oh[:, at] = (label == tail[3:4]).astype(BF)
    sums = []
    for i in range(blocks):
        for s0 in range(0, own, CHUNK):
            r = rts[i][s0 : s0 + CHUNK, :]
            total = None
            for j in plan[i]:
                at = slice(j * points, (j + 1) * points)
                power = jnp.dot(r, w[:, at], preferred_element_type=F32)
                payoff = jnp.maximum(lev[:, at] - jnp.exp2(power), 0.0).astype(BF)
                part = lax.dot_general(
                    payoff, oh[:, at], (((1,), (1,)), ((), ())), preferred_element_type=F32
                )
                total = part if total is None else total + part
            if not scale:
                outs[i][s0 : s0 + CHUNK, :] = total
                continue
            for k, at in enumerate(earlier):
                if at == i:
                    total = total + before[k][s0 : s0 + CHUNK, :]
            sums.append((i, s0, total))
    if not scale:
        return
    for load in loads:
        load.wait()
    result = None
    for i in range(blocks):
        v = jnp.concatenate([t for at, _, t in sums if at == i], axis=0)
        vh = v.astype(BF)
        vl = (v - vh.astype(F32)).astype(BF)
        both = jnp.concatenate([vh, vl], axis=1)
        a = jnp.dot(held[2 * i], both, preferred_element_type=F32)
        b = jnp.dot(held[2 * i + 1], vh, preferred_element_type=F32)
        part = a[:, :lines] + a[:, lines:] + b
        result = part if result is None else result + part
    out[...] = (result * scale).T


def values_of(rts, packs, plan, lines, before=(), basis=(), scale=None):
    own, double = rts[0].shape
    points = packs[0].shape[1]
    count = len(packs)
    pairs = own * points * sum(len(p) for p in plan)
    scratch = [
        pltpu.VMEM((double, points * count), BF),
        pltpu.VMEM((lines, points * count), BF),
        pltpu.VMEM((1, points * count), F32),
    ]
    specs = [pl.BlockSpec(memory_space=pltpu.VMEM)] * (len(rts) + count + len(before))
    if scale:
        terms = basis[0].shape[0]
        specs += [pl.BlockSpec(memory_space=pl.ANY)] * len(basis)
        scratch += [
            pltpu.VMEM((len(basis), terms, own), BF),
            pltpu.SemaphoreType.DMA((len(basis),)),
        ]
        shape = jax.ShapeDtypeStruct((lines, terms), F32)
    else:
        shape = [jax.ShapeDtypeStruct((own, lines), F32)] * len(rts)
    kernel = functools.partial(value_kernel, plan, count, [i for i, _ in before], scale)
    return pl.pallas_call(
        kernel,
        in_specs=specs,
        out_shape=shape,
        scratch_shapes=scratch,
        compiler_params=params(),
        cost_estimate=pl.CostEstimate(
            flops=1700 * pairs, bytes_accessed=2**20, transcendentals=pairs
        ),
    )(*rts, *packs, *[v for _, v in before], *basis)


def picks_of(exps):
    count = exps.shape[1]
    e = exps[...].astype(F32)
    row = lax.broadcasted_iota(jnp.int32, (count, count), 0)
    col = lax.broadcasted_iota(jnp.int32, (count, count), 1)
    upto = (row <= col).astype(BF)
    cum = jnp.dot(e.astype(BF), upto, preferred_element_type=F32)
    before = cum - e
    picks = [
        jnp.where((cum > t + 0.5) & (before < t + 0.5), 1.0, 0.0).astype(BF) for t in range(3)
    ]
    return [jnp.concatenate([p, p, p], axis=1) for p in picks]


def basis_kernel(exps, drivers, returns, high, low, rt):
    factors = returns.shape[0]
    r = returns[...].astype(F32).T.astype(BF)
    rt[:, :factors] = r
    rt[:, factors:] = r
    picks = picks_of(exps)
    parts = jnp.concatenate(three_parts(drivers[...]), axis=0)
    for c in range(0, drivers.shape[1], CHUNK):
        x = [jnp.dot(p, parts[:, c : c + CHUNK], preferred_element_type=F32) for p in picks]
        b = x[0] * x[1] * x[2]
        h = b.astype(BF)
        high[:, c : c + CHUNK] = h
        low[:, c : c + CHUNK] = (b - h.astype(F32)).astype(BF)


def gram_kernel(start, exps, drivers, returns, first, high, low, rt, keep, send):
    basis_kernel(exps, drivers, returns, high, low, rt)
    rows = keep.shape[0]
    for i, out in enumerate((keep, send)):
        r0 = pl.multiple_of(start[i] * rows, rows)
        out[...] = lax.dot_general(
            first[pl.ds(r0, rows), :],
            first[...],
            (((1,), (1,)), ((), ())),
            preferred_element_type=F32,
        ) + lax.dot_general(
            high[pl.ds(r0, rows), :],
            high[...],
            (((1,), (1,)), ((), ())),
            preferred_element_type=F32,
        )


def basis_of(exponents, drivers, returns, start=None, first=None):
    terms = exponents.shape[0]
    factors, own = returns.shape
    shapes = [jax.ShapeDtypeStruct((terms, own), BF)] * 2
    shapes.append(jax.ShapeDtypeStruct((own, 2 * factors), BF))
    vmem = pl.BlockSpec(memory_space=pltpu.VMEM)
    cost = pl.CostEstimate(flops=3 * 10**9, bytes_accessed=3 * 2**20, transcendentals=0)
    if start is None:
        return pl.pallas_call(
            basis_kernel, out_shape=shapes, compiler_params=params(), cost_estimate=cost
        )(exponents, drivers, returns)
    shapes += [jax.ShapeDtypeStruct((terms // 4, terms), F32)] * 2
    return pl.pallas_call(
        gram_kernel,
        in_specs=[pl.BlockSpec(memory_space=pltpu.SMEM)] + [vmem] * 4,
        out_shape=shapes,
        compiler_params=params(),
        cost_estimate=cost,
    )(start, exponents, drivers, returns, first)


def split_kernel(order, keep, more, *outs):
    rows = outs[0].shape[0]
    for i, out in enumerate(outs):
        at = pl.ds(pl.multiple_of(order[i] * rows, rows), rows)
        out[...] = keep[at, :] + more[at, :]


def split(order, keep, more, count):
    rows, terms = keep.shape
    return pl.pallas_call(
        split_kernel,
        in_specs=[pl.BlockSpec(memory_space=pltpu.SMEM)]
        + [pl.BlockSpec(memory_space=pltpu.VMEM)] * 2,
        out_shape=[jax.ShapeDtypeStruct((rows // count, terms), F32)] * count,
        compiler_params=params(),
        cost_estimate=pl.CostEstimate(flops=2**20, bytes_accessed=2**19, transcendentals=0),
    )(order, keep, more)


def place_kernel(scale, blocks, *refs):
    order, pieces, out = refs[0], refs[1:-1], refs[-1]
    rows = out.shape[0] // blocks
    k = 0
    for piece in pieces:
        for i in range(piece.shape[0] // rows):
            at = pl.multiple_of(order[k] * rows, rows)
            out[pl.ds(at, rows), :] = piece[i * rows : (i + 1) * rows, :] * scale
            k += 1


def placed(scale, blocks, order, pieces, terms):
    return pl.pallas_call(
        functools.partial(place_kernel, scale, blocks),
        in_specs=[pl.BlockSpec(memory_space=pltpu.SMEM)]
        + [pl.BlockSpec(memory_space=pltpu.VMEM)] * len(pieces),
        out_shape=jax.ShapeDtypeStruct((terms, terms), F32),
        compiler_params=params(),
        cost_estimate=pl.CostEstimate(
            flops=2**20, bytes_accessed=2 * 2**20, transcendentals=0
        ),
    )(order, *pieces)


def after(x, done):
    return lax.optimization_barrier((x, done))[0]


def local(n, returns, exposures, guarantees, guar_type, line_ids, drivers, exponents):
    lines = LINES
    scen_total = returns.shape[1] * n
    all_points = exposures.shape[0] * n
    terms = exponents.shape[0]
    me = lax.axis_index("scen").astype(jnp.int32)
    core, side, depth = me & 1, (me >> 1) & 1, me >> 2

    def swap(x, mask):
        return lax.ppermute(x, "scen", [(i, i ^ mask) for i in range(n)])

    far = list(range(4, n, 4))
    level = guarantees * (1.0 + 0.15 * guar_type.astype(F32))
    rows = [*three_parts(level), line_ids.astype(BF)]
    rows = jnp.stack(rows + [jnp.zeros_like(rows[0])] * (TAIL - 4))
    pack = jnp.concatenate([exposures.T, rows], axis=0)

    packs = {0: pack, 1: swap(pack, 1)}
    returns1 = swap(returns, 2)
    for m in far:
        packs[m] = swap(pack, m)
        packs[m ^ 1] = swap(packs[m], 1)
    drivers1 = swap(after(drivers, pack), 2)

    high0, low0, rt0 = basis_of(exponents, after(drivers, pack), returns)
    (v,) = values_of([after(rt0, low0)], [packs[0], packs[1]], [[0, 1]], lines)
    before = [(0, v)]

    base = side * 2 + core
    start = jnp.stack([base, base ^ 1])
    high1, low1, rt1, keep, send = basis_of(
        exponents, after(drivers1, v), returns1, start, high0
    )
    more = swap(send, 1)
    (v,) = values_of([rt1], [packs[0], packs[1]], [[0, 1]], lines)
    before.append((1, v))

    near = jnp.stack([depth ^ (m // 4) for m in [0] + far])
    keep, more = after((keep, more), v)
    parts = split(near, keep, more, n // 4)
    share = parts[0]
    for m, part in zip(far, parts[1:], strict=True):
        share = share + swap(part, m)

    scale = 1.0 / (math.sqrt(all_points / lines) * scen_total)
    tie = parts[0]
    for m in far[:-1]:
        duo = after((packs[m], packs[m ^ 1]), tie)
        v0, v1 = values_of([rt0, rt1], duo, [[0, 1], [0, 1]], lines)
        before += [(0, v0), (1, v1)]
        tie = v0
    tie = share = after(share, tie)
    duo = after((packs[far[-1]], packs[far[-1] ^ 1]), tie)
    basis = (high0, low0, high1, low1)
    rhs = values_of([rt0, rt1], duo, [[0, 1], [0, 1]], lines, before, basis, scale)

    a = jnp.concatenate([share] + [swap(share, m) for m in far], axis=0)
    b = swap(a, 2)
    c, d = swap(a, 1), swap(b, 1)
    order = jnp.concatenate([near + (base ^ k) * (n // 4) for k in (0, 2, 1, 3)])
    gram = placed(1.0 / scen_total, n, order, [a, b, c, d], terms)

    for m in [1, 2] + [4 << i for i in range((n // 4).bit_length() - 1)]:
        rhs = rhs + swap(rhs, m)
    return (gram, rhs.T)


def solution(mesh):
    spots = (
        P(None, ("grp", "scen")),
        P(("grp", "scen"), None),
        P(("grp", "scen")),
        P(("grp", "scen")),
        P(("grp", "scen")),
        P(None, ("grp", "scen")),
        P(),
    )
    return jax.shard_map(
        functools.partial(local, mesh.shape["scen"]),
        mesh=mesh,
        in_specs=spots,
        out_specs=(P("grp", None), P("grp", None)),
        check_vma=False,
    )
```

time: 109 us -> 73.2 us (0.67)
  Pallas kernels: 48.8 us -> 29.7 us
  waiting for transfers between devices: 27.8 us -> 16.1 us
  local copies, waits for them, and re-layouts: 7.62 us -> 2.84 us
    pallas_call x5 -> x8, Pallas kernels: 46.5 us -> 28.1 us  [the longest x5 23.1 us: values_of(): pl.pallas_call(kernel, in_specs=specs, out_shape=shape, scratch_shapes=sc...]
    ppermute x20 -> x23, waiting for transfers between devices: 27.8 us -> 16.1 us  [swap(): return lax.ppermute(x, 'scen', [(i, i ^ mask) for i in range(n)])]
    unnamed x41 -> x18, local copies, waits for them, and re-layouts: 5.88 us -> 1.8 us
    ppermute x20 -> x23, starting transfers between devices: 21.2 us -> 21.6 us  [swap(): return lax.ppermute(x, 'scen', [(i, i ^ mask) for i in range(n)])]
  transfers between devices with their start and end apart: 20 -> 23, of which waited for: 7 -> 8; matrix products, arithmetic and copies ran while one was open for 5% -> 2% of each run, Pallas kernels for 38% -> 29%
where the time goes in v2:
time: 73.2 us; the launch traced here: 72.9 us
  Pallas kernels  29.7 us (41%)
  starting transfers between devices  21.6 us (30%)
  waiting for transfers between devices  16.1 us (22%)
  local copies, waits for them, and re-layouts  2.84 us (4%)
  other arithmetic  1.69 us (2%)
  between operations  0.93 us (1%)
    pallas_call x5, Pallas kernels, values_of(): pl.pallas_call(kernel, in_specs=specs, out_shape=shape, scratch_shapes=sc...  23.1 us
    ppermute x23, starting transfers between devices, swap(): return lax.ppermute(x, 'scen', [(i, i ^ mask) for i in range(n)])  21.6 us
    ppermute x23, waiting for transfers between devices, swap(): return lax.ppermute(x, 'scen', [(i, i ^ mask) for i in range(n)])  16.1 us
    pallas_call x1, Pallas kernels, basis_of(): pl.pallas_call(gram_kernel, in_specs=[pl.BlockSpec(memory_space=pltpu.SME...  3.21 us
    unnamed x18, local copies, waits for them, and re-layouts  1.8 us
    pallas_call x1, Pallas kernels, placed(): pl.pallas_call(functools.partial(place_kernel, scale, blocks), in_specs=[...  1.59 us
  transfers between devices with their start and end apart: 23, of which 8 were waited for; matrix products, arithmetic and copies ran while one was open for 2% of the time, Pallas kernels for 29%

profile of v2, /device:TPU:0, one launch (start us, length us, event | category | flops | bytes accessed | tf_op | source)
XLA Modules:
  0.0 72.9 jit_solution(18337488829236384542)
XLA Ops:
  0.6 0.7 convert_element_type.28
  1.4 0.7 copy-done.5
  2.1 1.0 %concatenate.18.refs_1_ = bf16[80,1024]{1,0:T(8,128)(2,1)S(1)} concatenate(bf16[64,1024]{1,0:T(8,128)(2,1)} %bitcast.9, bf16[1,1024]{1,0:T(2,128)(2,1)S(1)} %stack.44, bf16[1,1024]{1,0:T(2,128)(2,1)S(1)} %stack.45, bf16[1,1024]{1,0:T(2,128)(2,1)S(1)} %stack.46, bf16[1,1024]{1,0:T(2,128)(2,1)S(1)} %stack.47, bf16[4,1024]{1,0:T(4,128)(2,1)S(1)} %concatenate.16, ...), dimensions={0} | concatenate | bytes 327680 | tf_op jit(solution)/shard_map/concatenate | solution.py:261
  3.1 5.1 %collective-permute-start.17 = (bf16[80,1024]{1,0:T(8,128)(2,1)S(1)}, bf16[80,1024]{1,0:T(8,128)(2,1)S(1)}, u32[]{:S(2)}, u32[]{:S(2)}) collective-permute-start(bf16[80,1024]{1,0:T(8,128)(2,1)S(1)} %concatenate.18.refs_1_), channel_id=1, source_target_pairs={{0,12},{1,13},{2,14},{3,15},{4,8},{5,9},{6,10},{7,11},{8,4},{9,5},... | collective-permute-start | bytes 491528 | tf_op jit(solution)/shard_map/ppermute | solution.py:255
  8.3 1.6 %collective-permute-start.2 = (bf16[64,1024]{1,0:T(8,128)(2,1)S(1)}, bf16[64,1024]{1,0:T(8,128)(2,1)S(1)}, u32[]{:S(2)}, u32[]{:S(2)}) collective-permute-start(bf16[64,1024]{1,0:T(8,128)(2,1)S(1)} %copy-done.1), channel_id=1, source_target_pairs={{0,2},{1,3},{2,0},{3,1},{4,6},{5,7},{6,4},{7,5},{8,10},{9,11},{10,... | collective-permute-start | bytes 393224 | tf_op jit(solution)/shard_map/ppermute | solution.py:255
  10.5 1.2 %shard_map.86 = (bf16[512,1024]{1,0:T(8,128)(2,1)S(1)}, bf16[512,1024]{1,0:T(8,128)(2,1)S(1)}, bf16[1024,128]{1,0:T(8,128)(2,1)S(1)}) custom-call(s32[512,40]{1,0:T(8,128)S(1)} %copy.10.exps, f32[40,1024]{1,0:T(8,128)S(1)} %copy-done, bf16[64,1024]{1,0:T(8,128)(2,1)S(1)} %copy-done.1), custom_call_target="tpu_custom_call" | custom-call | flops 3000000000 | bytes 3145728 | tf_op jit(solution)/shard_map/pallas_call | solution.py:186
  11.7 1.0 %copy-done.2 = bf16[512,1024]{1,0:T(8,128)(2,1)} copy-done((bf16[512,1024]{1,0:T(8,128)(2,1)}, bf16[512,1024]{1,0:T(8,128)(2,1)S(1)}, u32[]{:S(2)}) %copy-start.2) | copy-done | bytes 1048600
  12.8 0.6 collective-permute-start.7
  13.4 3.0 %shard_map.87.refs_4_ = f32[1024,64]{1,0:T(8,128)S(1)} custom-call(bf16[1024,128]{1,0:T(8,128)(2,1)S(1)} %get-tuple-element.33.refs_0_, bf16[80,1024]{1,0:T(8,128)(2,1)S(1)} %concatenate.18.refs_1_, bf16[80,1024]{1,0:T(8,128)(2,1)S(1)} %collective-permute-done.1.refs_2_), custom_call_target="tpu_custom_call" | custom-call | flops 3565158400 | bytes 1048576 | tf_op jit(solution)/shard_map/pallas_call | solution.py:119
  16.4 1.3 %collective-permute-done.drivers = f32[40,1024]{1,0:T(8,128)S(1)} collective-permute-done((f32[40,1024]{1,0:T(8,128)S(1)}, f32[40,1024]{1,0:T(8,128)S(1)}, u32[]{:S(2)}, u32[]{:S(2)}) %collective-permute-start) | collective-permute-done | bytes 163872 | tf_op jit(solution)/shard_map/ppermute | solution.py:255
  17.7 3.2 %shard_map.88 = (bf16[512,1024]{1,0:T(8,128)(2,1)S(1)}, bf16[512,1024]{1,0:T(8,128)(2,1)S(1)}, bf16[1024,128]{1,0:T(8,128)(2,1)S(1)}, f32[128,512]{1,0:T(8,128)S(1)}, f32[128,512]{1,0:T(8,128)S(1)}) custom-call(s32[2]{0:T(128)S(1)} %pad_add_fusion.2.start, s32[512,40]{1,0:T(8,128)S(1)} %copy.10.exps, f32[40,1024]{1,0:T(8,128)S(1)} %collective-permute-done.drivers, ...), custom_call_target="tpu_custom_call" | custom-call | flops 3000000000 | bytes 3145728 | tf_op jit(solution)/shard_map/pallas_call | solution.py:190
  21.6 1.7 %collective-permute-done.7.refs_2_ = bf16[80,1024]{1,0:T(8,128)(2,1)S(1)} collective-permute-done((bf16[80,1024]{1,0:T(8,128)(2,1)S(1)}, bf16[80,1024]{1,0:T(8,128)(2,1)S(1)}, u32[]{:S(2)}, u32[]{:S(2)}) %collective-permute-start.7) | collective-permute-done | bytes 163872 | tf_op jit(solution)/shard_map/ppermute | solution.py:255
  23.2 3.0 %shard_map.89.refs_5_ = f32[1024,64]{1,0:T(8,128)S(1)} custom-call(bf16[1024,128]{1,0:T(8,128)(2,1)S(1)} %get-tuple-element.38.refs_0_.refs_1_, bf16[80,1024]{1,0:T(8,128)(2,1)S(1)} %concatenate.18.refs_1_, bf16[80,1024]{1,0:T(8,128)(2,1)S(1)} %collective-permute-done.1.refs_2_), custom_call_target="tpu_custom_call" | custom-call | flops 3565158400 | bytes 1048576 | tf_op jit(solution)/shard_map/pallas_call | solution.py:119
  26.2 0.6 shard_map.90
  26.8 0.8 %collective-permute-start.4 = (f32[32,512]{1,0:T(8,128)S(1)}, f32[32,512]{1,0:T(8,128)S(1)}, u32[]{:S(2)}, u32[]{:S(2)}) collective-permute-start(f32[32,512]{1,0:T(8,128)S(1)} %get-tuple-element.42), channel_id=1, source_target_pairs={{0,4},{1,5},{2,6},{3,7},{4,0},{5,1},{6,2},{7,3},{8,12},{9,13},{10,... | collective-permute-start | bytes 196616 | tf_op jit(solution)/shard_map/ppermute | solution.py:255
  27.7 1.5 %collective-permute-start.5 = (f32[32,512]{1,0:T(8,128)S(1)}, f32[32,512]{1,0:T(8,128)S(1)}, u32[]{:S(2)}, u32[]{:S(2)}) collective-permute-start(f32[32,512]{1,0:T(8,128)S(1)} %get-tuple-element.43), channel_id=1, source_target_pairs={{0,8},{1,9},{2,10},{3,11},{4,12},{5,13},{6,14},{7,15},{8,0},{9,1},... | collective-permute-start | bytes 196616 | tf_op jit(solution)/shard_map/ppermute | solution.py:255
  29.2 2.1 %collective-permute-start.6 = (f32[32,512]{1,0:T(8,128)S(1)}, f32[32,512]{1,0:T(8,128)S(1)}, u32[]{:S(2)}, u32[]{:S(2)}) collective-permute-start(f32[32,512]{1,0:T(8,128)S(1)} %get-tuple-element.44), channel_id=1, source_target_pairs={{0,12},{1,13},{2,14},{3,15},{4,8},{5,9},{6,10},{7,11},{8,4},{9,5},... | collective-permute-start | bytes 196616 | tf_op jit(solution)/shard_map/ppermute | solution.py:255
  31.3 5.4 %shard_map.91 = (f32[1024,64]{1,0:T(8,128)S(1)}, f32[1024,64]{1,0:T(8,128)S(1)}) custom-call(bf16[1024,128]{1,0:T(8,128)(2,1)S(1)} %get-tuple-element.33.refs_0_, bf16[1024,128]{1,0:T(8,128)(2,1)S(1)} %get-tuple-element.38.refs_0_.refs_1_, bf16[80,1024]{1,0:T(8,128)(2,1)S(1)} %collective-permute-done.9.refs_2_, ...), custom_call_target="tpu_custom_call" | custom-call | flops 7130316800 | bytes 1048576 | tf_op jit(solution)/shard_map/pallas_call | solution.py:119
  36.7 5.2 %shard_map.92 = (f32[1024,64]{1,0:T(8,128)S(1)}, f32[1024,64]{1,0:T(8,128)S(1)}) custom-call(bf16[1024,128]{1,0:T(8,128)(2,1)S(1)} %get-tuple-element.33.refs_0_, bf16[1024,128]{1,0:T(8,128)(2,1)S(1)} %get-tuple-element.38.refs_0_.refs_1_, bf16[80,1024]{1,0:T(8,128)(2,1)S(1)} %collective-permute-done.7.refs_2_, ...), custom_call_target="tpu_custom_call" | custom-call | flops 7130316800 | bytes 1048576 | tf_op jit(solution)/shard_map/pallas_call | solution.py:119
  41.9 6.7 %shard_map.94 = f32[64,512]{1,0:T(8,128)S(1)} custom-call(bf16[1024,128]{1,0:T(8,128)(2,1)S(1)} %get-tuple-element.33.refs_0_, bf16[1024,128]{1,0:T(8,128)(2,1)S(1)} %get-tuple-element.38.refs_0_.refs_1_, bf16[80,1024]{1,0:T(8,128)(2,1)S(1)} %collective-permute-done.17.refs_2_, bf16[80,1024]{1,0:T(8,128)(2,1)S(1)} %collective-permute-done.18.refs_3_, ...), custom_call_target="tpu_custom_call" | custom-call | flops 7130316800 | bytes 1048576 | tf_op jit(solution)/shard_map/pallas_call | solution.py:119
  48.7 1.8 %collective-permute-start.13 = (f32[32,512]{1,0:T(8,128)S(1)}, f32[32,512]{1,0:T(8,128)S(1)}, u32[]{:S(2)}, u32[]{:S(2)}) collective-permute-start(f32[32,512]{1,0:T(8,128)S(1)} %add_add_fusion), channel_id=1, source_target_pairs={{0,12},{1,13},{2,14},{3,15},{4,8},{5,9},{6,10},{7,11},{8,4},{9,5},... | collective-permute-start | bytes 196616 | tf_op jit(solution)/shard_map/ppermute | solution.py:255
  50.5 2.6 %collective-permute-start.11 = (f32[32,512]{1,0:T(8,128)S(1)}, f32[32,512]{1,0:T(8,128)S(1)}, u32[]{:S(2)}, u32[]{:S(2)}) collective-permute-start(f32[32,512]{1,0:T(8,128)S(1)} %add_add_fusion), channel_id=1, source_target_pairs={{0,4},{1,5},{2,6},{3,7},{4,0},{5,1},{6,2},{7,3},{8,12},{9,13},{10,... | collective-permute-start | bytes 196616 | tf_op jit(solution)/shard_map/ppermute | solution.py:255
  53.2 1.6 %collective-permute-start.20 = (f32[64,512]{1,0:T(8,128)S(1)}, f32[64,512]{1,0:T(8,128)S(1)}, u32[]{:S(2)}, u32[]{:S(2)}) collective-permute-start(f32[64,512]{1,0:T(8,128)S(1)} %add.68), channel_id=1, source_target_pairs={{0,2},{1,3},{2,0},{3,1},{4,6},{5,7},{6,4},{7,5},{8,10},{9,11},{10,... | collective-permute-start | bytes 393224 | tf_op jit(solution)/shard_map/ppermute | solution.py:255
  54.8 2.1 %collective-permute-done.11 = f32[32,512]{1,0:T(8,128)S(1)} collective-permute-done((f32[32,512]{1,0:T(8,128)S(1)}, f32[32,512]{1,0:T(8,128)S(1)}, u32[]{:S(2)}, u32[]{:S(2)}) %collective-permute-start.11) | collective-permute-done | bytes 65568 | tf_op jit(solution)/shard_map/ppermute | solution.py:255
  56.9 0.9 %collective-permute-done.12 = f32[32,512]{1,0:T(8,128)S(1)} collective-permute-done((f32[32,512]{1,0:T(8,128)S(1)}, f32[32,512]{1,0:T(8,128)S(1)}, u32[]{:S(2)}, u32[]{:S(2)}) %collective-permute-start.12) | collective-permute-done | bytes 65568 | tf_op jit(solution)/shard_map/ppermute | solution.py:255
  58.6 1.6 %collective-permute-start.14 = (f32[128,512]{1,0:T(8,128)S(1)}, f32[128,512]{1,0:T(8,128)S(1)}, u32[]{:S(2)}, u32[]{:S(2)}) collective-permute-start(f32[128,512]{1,0:T(8,128)S(1)} %constant_dynamic-update-slice_fusion.refs_1_), channel_id=1, source_target_pairs={{0,2},{1,3},{2,0},{3,1},{4,6},{5,7},{6,4},{7,5},{8,10},{9,11},{10,... | collective-permute-start | bytes 786440 | tf_op jit(solution)/shard_map/ppermute | solution.py:255
  60.2 3.1 %collective-permute-done.21 = f32[64,512]{1,0:T(8,128)S(1)} collective-permute-done((f32[64,512]{1,0:T(8,128)S(1)}, f32[64,512]{1,0:T(8,128)S(1)}, u32[]{:S(2)}, u32[]{:S(2)}) %collective-permute-start.21) | collective-permute-done | bytes 131104 | tf_op jit(solution)/shard_map/ppermute | solution.py:255
  63.4 0.6 collective-permute-start.22
  64.0 2.2 %collective-permute-done.14.refs_2_ = f32[128,512]{1,0:T(8,128)S(1)} collective-permute-done((f32[128,512]{1,0:T(8,128)S(1)}, f32[128,512]{1,0:T(8,128)S(1)}, u32[]{:S(2)}, u32[]{:S(2)}) %collective-permute-start.14) | collective-permute-done | bytes 262176 | tf_op jit(solution)/shard_map/ppermute | solution.py:255
  66.3 4.3 %collective-permute-done.22 = f32[64,512]{1,0:T(8,128)S(1)} collective-permute-done((f32[64,512]{1,0:T(8,128)S(1)}, f32[64,512]{1,0:T(8,128)S(1)}, u32[]{:S(2)}, u32[]{:S(2)}) %collective-permute-start.22) | collective-permute-done | bytes 131104 | tf_op jit(solution)/shard_map/ppermute | solution.py:255
  70.7 0.7 add_bitcast_fusion
  71.4 1.6 %shard_map.93 = f32[512,512]{1,0:T(8,128)} custom-call(s32[16]{0:T(128)S(1)} %pad_add_fusion.1.refs_0_, f32[128,512]{1,0:T(8,128)S(1)} %constant_dynamic-update-slice_fusion.refs_1_, f32[128,512]{1,0:T(8,128)S(1)} %collective-permute-done.14.refs_2_, f32[128,512]{1,0:T(8,128)S(1)} %collective-permute-done.15.refs_3_, ...), custom_call_target="tpu_custom_call" | custom-call | flops 1048576 | bytes 2097152 | tf_op jit(solution)/shard_map/pallas_call | solution.py:230
  (60 shorter events, 2.6 us)
Async XLA Ops:
  0.6 0.7 copy-start.6
  1.3 0.7 copy-start.5
  2.0 8.3 %copy-start.4 = (s32[512,40]{0,1:T(8,128)S(1)}, s32[512,40]{0,1:T(8,128)}, u32[]{:S(2)}) copy-start(s32[512,40]{0,1:T(8,128)} %param.13) | copy-start | bytes 245764
  2.1 6.1 %copy-start.1 = (bf16[64,1024]{1,0:T(8,128)(2,1)S(1)}, bf16[64,1024]{1,0:T(8,128)(2,1)}, u32[]{:S(2)}) copy-start(bf16[64,1024]{1,0:T(8,128)(2,1)} %returns.1) | copy-start | bytes 393220
  2.1 7.7 %copy-start = (f32[40,1024]{1,0:T(8,128)S(1)}, f32[40,1024]{1,0:T(8,128)}, u32[]{:S(2)}) copy-start(f32[40,1024]{1,0:T(8,128)} %drivers) | copy-start | bytes 491524
  3.1 17.8 %collective-permute-start.17 = (bf16[80,1024]{1,0:T(8,128)(2,1)S(1)}, bf16[80,1024]{1,0:T(8,128)(2,1)S(1)}, u32[]{:S(2)}, u32[]{:S(2)}) collective-permute-start(bf16[80,1024]{1,0:T(8,128)(2,1)S(1)} %concatenate.18.refs_1_), channel_id=1, source_target_pairs={{0,12},{1,13},{2,14},{3,15},{4,8},{5,9},{6,10},{7,11},{8,4},{9,5},... | collective-permute-start | bytes 491528 | tf_op jit(solution)/shard_map/ppermute | solution.py:255
  8.2 13.2 %collective-permute-start.9 = (bf16[80,1024]{1,0:T(8,128)(2,1)S(1)}, bf16[80,1024]{1,0:T(8,128)(2,1)S(1)}, u32[]{:S(2)}, u32[]{:S(2)}) collective-permute-start(bf16[80,1024]{1,0:T(8,128)(2,1)S(1)} %concatenate.18.refs_1_), channel_id=1, source_target_pairs={{0,4},{1,5},{2,6},{3,7},{4,0},{5,1},{6,2},{7,3},{8,12},{9,13},{10,... | collective-permute-start | bytes 491528 | tf_op jit(solution)/shard_map/ppermute | solution.py:255
  8.2 4.6 %collective-permute-start.1 = (bf16[80,1024]{1,0:T(8,128)(2,1)S(1)}, bf16[80,1024]{1,0:T(8,128)(2,1)S(1)}, u32[]{:S(2)}, u32[]{:S(2)}) collective-permute-start(bf16[80,1024]{1,0:T(8,128)(2,1)S(1)} %concatenate.18.refs_1_), channel_id=1, source_target_pairs={{0,1},{1,0},{2,3},{3,2},{4,5},{5,4},{6,7},{7,6},{8,9},{9,8},{10,11... | collective-permute-start | bytes 491528 | tf_op jit(solution)/shard_map/ppermute | solution.py:255
  8.3 9.4 %collective-permute-start.2 = (bf16[64,1024]{1,0:T(8,128)(2,1)S(1)}, bf16[64,1024]{1,0:T(8,128)(2,1)S(1)}, u32[]{:S(2)}, u32[]{:S(2)}) collective-permute-start(bf16[64,1024]{1,0:T(8,128)(2,1)S(1)} %copy-done.1), channel_id=1, source_target_pairs={{0,2},{1,3},{2,0},{3,1},{4,6},{5,7},{6,4},{7,5},{8,10},{9,11},{10,... | collective-permute-start | bytes 393224 | tf_op jit(solution)/shard_map/ppermute | solution.py:255
  9.8 7.8 %collective-permute-start = (f32[40,1024]{1,0:T(8,128)S(1)}, f32[40,1024]{1,0:T(8,128)S(1)}, u32[]{:S(2)}, u32[]{:S(2)}) collective-permute-start(f32[40,1024]{1,0:T(8,128)S(1)} %copy-done), channel_id=1, source_target_pairs={{0,2},{1,3},{2,0},{3,1},{4,6},{5,7},{6,4},{7,5},{8,10},{9,11},{10,... | collective-permute-start | bytes 491528 | tf_op jit(solution)/shard_map/ppermute | solution.py:255
  11.7 1.0 %copy-start.2 = (bf16[512,1024]{1,0:T(8,128)(2,1)}, bf16[512,1024]{1,0:T(8,128)(2,1)S(1)}, u32[]{:S(2)}) copy-start(bf16[512,1024]{1,0:T(8,128)(2,1)S(1)} %get-tuple-element.32.refs_11_) | copy-start | bytes 3145732
  12.8 10.4 %collective-permute-start.7 = (bf16[80,1024]{1,0:T(8,128)(2,1)S(1)}, bf16[80,1024]{1,0:T(8,128)(2,1)S(1)}, u32[]{:S(2)}, u32[]{:S(2)}) collective-permute-start(bf16[80,1024]{1,0:T(8,128)(2,1)S(1)} %concatenate.18.refs_1_), channel_id=1, source_target_pairs={{0,8},{1,9},{2,10},{3,11},{4,12},{5,13},{6,14},{7,15},{8,0},{9,1},... | collective-permute-start | bytes 491528 | tf_op jit(solution)/shard_map/ppermute | solution.py:255
  20.9 5.3 %collective-permute-start.3 = (f32[128,512]{1,0:T(8,128)S(1)}, f32[128,512]{1,0:T(8,128)S(1)}, u32[]{:S(2)}, u32[]{:S(2)}) collective-permute-start(f32[128,512]{1,0:T(8,128)S(1)} %get-tuple-element.37), channel_id=1, source_target_pairs={{0,1},{1,0},{2,3},{3,2},{4,5},{5,4},{6,7},{7,6},{8,9},{9,8},{10,11... | collective-permute-start | bytes 786440 | tf_op jit(solution)/shard_map/ppermute | solution.py:255
  21.0 20.9 %collective-permute-start.18 = (bf16[80,1024]{1,0:T(8,128)(2,1)S(1)}, bf16[80,1024]{1,0:T(8,128)(2,1)S(1)}, u32[]{:S(2)}, u32[]{:S(2)}) collective-permute-start(bf16[80,1024]{1,0:T(8,128)(2,1)S(1)} %collective-permute-done.17.refs_2_), channel_id=1, source_target_pairs={{0,1},{1,0},{2,3},{3,2},{4,5},{5,4},{6,7},{7,6},{8,9},{9,8},{10,11... | collective-permute-start | bytes 491528 | tf_op jit(solution)/shard_map/ppermute | solution.py:255
  21.5 5.3 %collective-permute-start.10 = (bf16[80,1024]{1,0:T(8,128)(2,1)S(1)}, bf16[80,1024]{1,0:T(8,128)(2,1)S(1)}, u32[]{:S(2)}, u32[]{:S(2)}) collective-permute-start(bf16[80,1024]{1,0:T(8,128)(2,1)S(1)} %collective-permute-done.9.refs_2_), channel_id=1, source_target_pairs={{0,1},{1,0},{2,3},{3,2},{4,5},{5,4},{6,7},{7,6},{8,9},{9,8},{10,11... | collective-permute-start | bytes 491528 | tf_op jit(solution)/shard_map/ppermute | solution.py:255
  23.2 13.4 %collective-permute-start.8 = (bf16[80,1024]{1,0:T(8,128)(2,1)S(1)}, bf16[80,1024]{1,0:T(8,128)(2,1)S(1)}, u32[]{:S(2)}, u32[]{:S(2)}) collective-permute-start(bf16[80,1024]{1,0:T(8,128)(2,1)S(1)} %collective-permute-done.7.refs_2_), channel_id=1, source_target_pairs={{0,1},{1,0},{2,3},{3,2},{4,5},{5,4},{6,7},{7,6},{8,9},{9,8},{10,11... | collective-permute-start | bytes 491528 | tf_op jit(solution)/shard_map/ppermute | solution.py:255
  26.8 15.0 %collective-permute-start.4 = (f32[32,512]{1,0:T(8,128)S(1)}, f32[32,512]{1,0:T(8,128)S(1)}, u32[]{:S(2)}, u32[]{:S(2)}) collective-permute-start(f32[32,512]{1,0:T(8,128)S(1)} %get-tuple-element.42), channel_id=1, source_target_pairs={{0,4},{1,5},{2,6},{3,7},{4,0},{5,1},{6,2},{7,3},{8,12},{9,13},{10,... | collective-permute-start | bytes 196616 | tf_op jit(solution)/shard_map/ppermute | solution.py:255
  27.7 14.2 %collective-permute-start.5 = (f32[32,512]{1,0:T(8,128)S(1)}, f32[32,512]{1,0:T(8,128)S(1)}, u32[]{:S(2)}, u32[]{:S(2)}) collective-permute-start(f32[32,512]{1,0:T(8,128)S(1)} %get-tuple-element.43), channel_id=1, source_target_pairs={{0,8},{1,9},{2,10},{3,11},{4,12},{5,13},{6,14},{7,15},{8,0},{9,1},... | collective-permute-start | bytes 196616 | tf_op jit(solution)/shard_map/ppermute | solution.py:255
  29.2 12.7 %collective-permute-start.6 = (f32[32,512]{1,0:T(8,128)S(1)}, f32[32,512]{1,0:T(8,128)S(1)}, u32[]{:S(2)}, u32[]{:S(2)}) collective-permute-start(f32[32,512]{1,0:T(8,128)S(1)} %get-tuple-element.44), channel_id=1, source_target_pairs={{0,12},{1,13},{2,14},{3,15},{4,8},{5,9},{6,10},{7,11},{8,4},{9,5},... | collective-permute-start | bytes 196616 | tf_op jit(solution)/shard_map/ppermute | solution.py:255
  36.7 5.3 %copy-start.3 = (bf16[512,1024]{1,0:T(8,128)(2,1)S(1)}, bf16[512,1024]{1,0:T(8,128)(2,1)}, u32[]{:S(2)}) copy-start(bf16[512,1024]{1,0:T(8,128)(2,1)} %copy-done.2) | copy-start | bytes 3145732
  48.6 4.5 %collective-permute-start.19 = (f32[64,512]{1,0:T(8,128)S(1)}, f32[64,512]{1,0:T(8,128)S(1)}, u32[]{:S(2)}, u32[]{:S(2)}) collective-permute-start(f32[64,512]{1,0:T(8,128)S(1)} %shard_map.94), channel_id=1, source_target_pairs={{0,1},{1,0},{2,3},{3,2},{4,5},{5,4},{6,7},{7,6},{8,9},{9,8},{10,11... | collective-permute-start | bytes 393224 | tf_op jit(solution)/shard_map/ppermute | solution.py:255
  48.7 9.9 %collective-permute-start.13 = (f32[32,512]{1,0:T(8,128)S(1)}, f32[32,512]{1,0:T(8,128)S(1)}, u32[]{:S(2)}, u32[]{:S(2)}) collective-permute-start(f32[32,512]{1,0:T(8,128)S(1)} %add_add_fusion), channel_id=1, source_target_pairs={{0,12},{1,13},{2,14},{3,15},{4,8},{5,9},{6,10},{7,11},{8,4},{9,5},... | collective-permute-start | bytes 196616 | tf_op jit(solution)/shard_map/ppermute | solution.py:255
  50.5 7.3 %collective-permute-start.12 = (f32[32,512]{1,0:T(8,128)S(1)}, f32[32,512]{1,0:T(8,128)S(1)}, u32[]{:S(2)}, u32[]{:S(2)}) collective-permute-start(f32[32,512]{1,0:T(8,128)S(1)} %add_add_fusion), channel_id=1, source_target_pairs={{0,8},{1,9},{2,10},{3,11},{4,12},{5,13},{6,14},{7,15},{8,0},{9,1},... | collective-permute-start | bytes 196616 | tf_op jit(solution)/shard_map/ppermute | solution.py:255
  50.5 6.4 %collective-permute-start.11 = (f32[32,512]{1,0:T(8,128)S(1)}, f32[32,512]{1,0:T(8,128)S(1)}, u32[]{:S(2)}, u32[]{:S(2)}) collective-permute-start(f32[32,512]{1,0:T(8,128)S(1)} %add_add_fusion), channel_id=1, source_target_pairs={{0,4},{1,5},{2,6},{3,7},{4,0},{5,1},{6,2},{7,3},{8,12},{9,13},{10,... | collective-permute-start | bytes 196616 | tf_op jit(solution)/shard_map/ppermute | solution.py:255
  53.2 5.1 %collective-permute-start.20 = (f32[64,512]{1,0:T(8,128)S(1)}, f32[64,512]{1,0:T(8,128)S(1)}, u32[]{:S(2)}, u32[]{:S(2)}) collective-permute-start(f32[64,512]{1,0:T(8,128)S(1)} %add.68), channel_id=1, source_target_pairs={{0,2},{1,3},{2,0},{3,1},{4,6},{5,7},{6,4},{7,5},{8,10},{9,11},{10,... | collective-permute-start | bytes 393224 | tf_op jit(solution)/shard_map/ppermute | solution.py:255
  58.3 5.1 %collective-permute-start.21 = (f32[64,512]{1,0:T(8,128)S(1)}, f32[64,512]{1,0:T(8,128)S(1)}, u32[]{:S(2)}, u32[]{:S(2)}) collective-permute-start(f32[64,512]{1,0:T(8,128)S(1)} %add.69), channel_id=1, source_target_pairs={{0,4},{1,5},{2,6},{3,7},{4,0},{5,1},{6,2},{7,3},{8,12},{9,13},{10,... | collective-permute-start | bytes 393224 | tf_op jit(solution)/shard_map/ppermute | solution.py:255
  58.6 7.6 %collective-permute-start.14 = (f32[128,512]{1,0:T(8,128)S(1)}, f32[128,512]{1,0:T(8,128)S(1)}, u32[]{:S(2)}, u32[]{:S(2)}) collective-permute-start(f32[128,512]{1,0:T(8,128)S(1)} %constant_dynamic-update-slice_fusion.refs_1_), channel_id=1, source_target_pairs={{0,2},{1,3},{2,0},{3,1},{4,6},{5,7},{6,4},{7,5},{8,10},{9,11},{10,... | collective-permute-start | bytes 786440 | tf_op jit(solution)/shard_map/ppermute | solution.py:255
  63.4 7.3 %collective-permute-start.22 = (f32[64,512]{1,0:T(8,128)S(1)}, f32[64,512]{1,0:T(8,128)S(1)}, u32[]{:S(2)}, u32[]{:S(2)}) collective-permute-start(f32[64,512]{1,0:T(8,128)S(1)} %add.70), channel_id=1, source_target_pairs={{0,8},{1,9},{2,10},{3,11},{4,12},{5,13},{6,14},{7,15},{8,0},{9,1},... | collective-permute-start | bytes 393224 | tf_op jit(solution)/shard_map/ppermute | solution.py:255
  64.0 7.3 %collective-permute-start.15 = (f32[128,512]{1,0:T(8,128)S(1)}, f32[128,512]{1,0:T(8,128)S(1)}, u32[]{:S(2)}, u32[]{:S(2)}) collective-permute-start(f32[128,512]{1,0:T(8,128)S(1)} %constant_dynamic-update-slice_fusion.refs_1_), channel_id=1, source_target_pairs={{0,1},{1,0},{2,3},{3,2},{4,5},{5,4},{6,7},{7,6},{8,9},{9,8},{10,11... | collective-permute-start | bytes 786440 | tf_op jit(solution)/shard_map/ppermute | solution.py:255
  66.3 5.1 %collective-permute-start.16 = (f32[128,512]{1,0:T(8,128)S(1)}, f32[128,512]{1,0:T(8,128)S(1)}, u32[]{:S(2)}, u32[]{:S(2)}) collective-permute-start(f32[128,512]{1,0:T(8,128)S(1)} %collective-permute-done.14.refs_2_), channel_id=1, source_target_pairs={{0,1},{1,0},{2,3},{3,2},{4,5},{5,4},{6,7},{7,6},{8,9},{9,8},{10,11... | collective-permute-start | bytes 786440 | tf_op jit(solution)/shard_map/ppermute | solution.py:255

commit v3 on v2

v3 whole, which is shorter than its diff:
```python
import functools
import math

import jax
import jax.numpy as jnp
from jax import lax
from jax.experimental import pallas as pl
from jax.experimental.pallas import tpu as pltpu
from jax.sharding import PartitionSpec as P

LINES = 64
TAIL = 16
CHUNK = 512
LOG2E = 1.4426950408889634
BF = jnp.bfloat16
F32 = jnp.float32
HALF = jnp.float16
VMEM = 24 * 2**20


def params(limit=VMEM):
    return pltpu.CompilerParams(vmem_limit_bytes=limit)


def parts_of(x, count):
    parts = []
    for _ in range(count):
        parts.append(x.astype(BF).astype(F32))
        x = x - parts[-1]
    return parts


def pack_kernel(*refs):
    points, scens = refs[6:8]
    held, sems = refs[8:14], refs[14]
    loads = [pltpu.make_async_copy(refs[i], held[i], sems.at[i]) for i in range(6)]
    for load in loads:
        load.start()
    for load in loads:
        load.wait()
    exposures, guarantees, kinds, lines, returns, drivers = held
    factors = exposures.shape[0]
    points[:factors, :] = exposures[...]
    level = guarantees[...] * (1.0 + 0.15 * kinds[...].astype(F32))
    rows = [*parts_of(level, 3), lines[...].astype(F32)]
    rows.append(jnp.zeros((TAIL - 4, level.shape[1]), F32))
    points[factors:, :] = jnp.concatenate(rows, axis=0).astype(BF)
    scens[:factors, :] = returns[...]
    scens[factors:, :] = jnp.concatenate(parts_of(drivers[...], 2), axis=0).astype(BF)


def packs_of(exposures, guarantees, kinds, lines, returns, drivers):
    points, factors = exposures.shape
    row = (1, points)
    args = (
        exposures.T,
        guarantees.reshape(row),
        kinds.reshape(row),
        lines.reshape(row),
        returns,
        drivers,
    )
    return pl.pallas_call(
        pack_kernel,
        in_specs=[pl.BlockSpec(memory_space=pltpu.HBM)] * len(args),
        out_shape=[
            jax.ShapeDtypeStruct((factors + TAIL, points), BF),
            jax.ShapeDtypeStruct((factors + 2 * drivers.shape[0], returns.shape[1]), BF),
        ],
        scratch_shapes=[pltpu.VMEM(a.shape, a.dtype) for a in args]
        + [pltpu.SemaphoreType.DMA((len(args),))],
        compiler_params=params(58 * 2**20),
        cost_estimate=pl.CostEstimate(flops=2**20, bytes_accessed=2**20, transcendentals=0),
    )(*args)


def value_kernel(plan, count, earlier, scale, *refs):
    blocks = len(plan)
    rts, refs = refs[:blocks], refs[blocks:]
    stacks, refs = refs[:count], refs[count:]
    if scale:
        before, refs = refs[: len(earlier)], refs[len(earlier) :]
        basis, refs = refs[: 2 * blocks], refs[2 * blocks :]
        core, keep, send, w, oh, lev, whole = refs
    else:
        outs, (w, oh, lev) = refs[:blocks], refs[blocks:]
    own, double = rts[0].shape
    factors = double // 2
    points = stacks[0].shape[1]
    lines = oh.shape[0]
    height = factors + TAIL
    packs = [s.at[k : k + height] for s in stacks for k in range(0, s.shape[0], height)]
    for i in range(len(packs)):
        at = slice(i * points, (i + 1) * points)
        e = packs[i][:factors, :].astype(F32) * LOG2E
        high = e.astype(BF)
        w[:factors, at] = high
        w[factors:, at] = (e - high.astype(F32)).astype(BF)
        tail = packs[i][factors:, :].astype(F32)
        lev[:, at] = tail[0:1] + tail[1:2] + tail[2:3]
        label = lax.broadcasted_iota(jnp.int32, (lines, points), 0).astype(F32)
        oh[:, at] = (label == tail[3:4]).astype(BF)
    sums = []
    for i in range(blocks):
        for s0 in range(0, own, CHUNK):
            r = rts[i][s0 : s0 + CHUNK, :]
            total = None
            for j in plan[i] or range(len(packs)):
                at = slice(j * points, (j + 1) * points)
                power = jnp.dot(r, w[:, at], preferred_element_type=F32)
                payoff = jnp.maximum(lev[:, at] - jnp.exp2(power), 0.0).astype(BF)
                part = lax.dot_general(
                    payoff, oh[:, at], (((1,), (1,)), ((), ())), preferred_element_type=F32
                )
                total = part if total is None else total + part
            if not scale:
                outs[i][s0 : s0 + CHUNK, :] = total
                continue
            for k, at in enumerate(earlier):
                if at == i:
                    total = total + before[k][s0 : s0 + CHUNK, :]
            sums.append((i, s0, total))
    if not scale:
        return
    result = None
    for i in range(blocks):
        v = jnp.concatenate([t for at, _, t in sums if at == i], axis=0)
        vh = v.astype(BF)
        vl = (v - vh.astype(F32)).astype(BF)
        both = jnp.concatenate([vh, vl], axis=1)
        a = jnp.dot(basis[2 * i][...], both, preferred_element_type=F32)
        b = jnp.dot(basis[2 * i + 1][...], vh, preferred_element_type=F32)
        part = a[:, :lines] + a[:, lines:] + b
        result = part if result is None else result + part
    whole[...] = (result * scale).T
    half = lines // 2
    keep[...] = whole[pl.ds(pl.multiple_of(core[0] * half, half), half), :]
    send[...] = whole[pl.ds(pl.multiple_of((1 - core[0]) * half, half), half), :]


def values_of(rts, packs, plan, lines, before=(), basis=(), scale=None, core=None):
    own, double = rts[0].shape
    points = packs[0].shape[1]
    count = sum(p.shape[0] for p in packs) // (double // 2 + TAIL)
    pairs = own * points * len(plan) * count
    scratch = [
        pltpu.VMEM((double, points * count), BF),
        pltpu.VMEM((lines, points * count), BF),
        pltpu.VMEM((1, points * count), F32),
    ]
    specs = [pl.BlockSpec(memory_space=pltpu.VMEM)] * (len(rts) + len(packs) + len(before))
    if scale:
        terms = basis[0].shape[0]
        specs += [pl.BlockSpec(memory_space=pltpu.VMEM)] * len(basis)
        specs.append(pl.BlockSpec(memory_space=pltpu.SMEM))
        scratch.append(pltpu.VMEM((lines, terms), F32))
        shape = [jax.ShapeDtypeStruct((lines // 2, terms), F32)] * 2
        basis = [*basis, core]
    else:
        shape = [jax.ShapeDtypeStruct((own, lines), F32)] * len(rts)
    kernel = functools.partial(value_kernel, plan, len(packs), [i for i, _ in before], scale)
    return pl.pallas_call(
        kernel,
        in_specs=specs,
        out_shape=shape,
        scratch_shapes=scratch,
        compiler_params=params(),
        cost_estimate=pl.CostEstimate(
            flops=1700 * pairs, bytes_accessed=2**20, transcendentals=pairs
        ),
    )(*rts, *packs, *[v for _, v in before], *basis)


def picks_of(exps):
    count = exps.shape[1]
    e = exps[...].astype(F32)
    row = lax.broadcasted_iota(jnp.int32, (count, count), 0)
    col = lax.broadcasted_iota(jnp.int32, (count, count), 1)
    upto = (row <= col).astype(BF)
    cum = jnp.dot(e.astype(BF), upto, preferred_element_type=F32)
    before = cum - e
    picks = [
        jnp.where((cum > t + 0.5) & (before < t + 0.5), 1.0, 0.0).astype(BF) for t in range(3)
    ]
    return [jnp.concatenate([p, p], axis=1) for p in picks]


def basis_kernel(exps, scens, high, low, rt):
    factors = rt.shape[1] // 2
    r = scens[:factors, :].astype(F32).T.astype(BF)
    rt[:, :factors] = r
    rt[:, factors:] = r
    picks = picks_of(exps)
    for c in range(0, scens.shape[1], CHUNK):
        part = scens[factors:, c : c + CHUNK]
        x = [jnp.dot(p, part, preferred_element_type=F32) for p in picks]
        b = x[0] * x[1] * x[2]
        h = b.astype(BF)
        high[:, c : c + CHUNK] = h
        low[:, c : c + CHUNK] = (b - h.astype(F32)).astype(BF)


def first_kernel(exps, scens, p0, p1, high, low, rt, out, w, oh, lev):
    basis_kernel(exps, scens, high, low, rt)
    value_kernel([None], 2, (), None, rt, p0, p1, out, w, oh, lev)


def gram_kernel(start, exps, scens, first, high, low, rt, keep, send):
    basis_kernel(exps, scens, high, low, rt)
    rows = keep.shape[0]
    for i, out in enumerate((keep, send)):
        r0 = pl.multiple_of(start[i] * rows, rows)
        out[...] = lax.dot_general(
            first[pl.ds(r0, rows), :],
            first[...],
            (((1,), (1,)), ((), ())),
            preferred_element_type=F32,
        ) + lax.dot_general(
            high[pl.ds(r0, rows), :],
            high[...],
            (((1,), (1,)), ((), ())),
            preferred_element_type=F32,
        )


def basis_of(exponents, scens, near=(), lines=0, start=None, first=None):
    terms, count = exponents.shape
    factors, own = scens.shape[0] - 2 * count, scens.shape[1]
    shapes = [jax.ShapeDtypeStruct((terms, own), BF)] * 2
    shapes.append(jax.ShapeDtypeStruct((own, 2 * factors), BF))
    vmem = pl.BlockSpec(memory_space=pltpu.VMEM)
    cost = pl.CostEstimate(flops=3 * 10**9, bytes_accessed=3 * 2**20, transcendentals=0)
    if start is None:
        points = near[0].shape[1] * len(near)
        shapes.append(jax.ShapeDtypeStruct((own, lines), F32))
        return pl.pallas_call(
            first_kernel,
            out_shape=shapes,
            scratch_shapes=[
                pltpu.VMEM((2 * factors, points), BF),
                pltpu.VMEM((lines, points), BF),
                pltpu.VMEM((1, points), F32),
            ],
            compiler_params=params(),
            cost_estimate=cost,
        )(exponents, scens, *near)
    shapes += [jax.ShapeDtypeStruct((terms // 4, terms), F32)] * 2
    return pl.pallas_call(
        gram_kernel,
        in_specs=[pl.BlockSpec(memory_space=pltpu.SMEM)] + [vmem] * 3,
        out_shape=shapes,
        compiler_params=params(),
        cost_estimate=cost,
    )(start, exponents, scens, first)


def place_kernel(blocks, *refs):
    order, pieces, out = refs[0], refs[1:-1], refs[-1]
    rows = out.shape[0] // blocks
    k = 0
    for piece in pieces:
        for i in range(piece.shape[0] // rows):
            at = pl.multiple_of(order[k] * rows, rows)
            out[pl.ds(at, rows), :] = piece[i * rows : (i + 1) * rows, :]
            k += 1


def placed(blocks, order, pieces, terms):
    return pl.pallas_call(
        functools.partial(place_kernel, blocks),
        in_specs=[pl.BlockSpec(memory_space=pltpu.SMEM)]
        + [pl.BlockSpec(memory_space=pltpu.VMEM)] * len(pieces),
        out_shape=jax.ShapeDtypeStruct((terms, terms), F32),
        compiler_params=params(),
        cost_estimate=pl.CostEstimate(
            flops=2**20, bytes_accessed=2 * 2**20, transcendentals=0
        ),
    )(order, *pieces)


def after(x, done):
    return lax.optimization_barrier((x, done))[0]


def local(n, returns, exposures, guarantees, guar_type, line_ids, drivers, exponents):
    lines = LINES
    scen_total = returns.shape[1] * n
    all_points = exposures.shape[0] * n
    terms = exponents.shape[0]
    me = lax.axis_index("scen").astype(jnp.int32)
    core, side = me & 1, (me >> 1) & 1

    def swap(x, mask):
        return lax.ppermute(x, "scen", [(i, i ^ mask) for i in range(n)])

    far = list(range(4, n, 4))
    deep = [4 << i for i in range((n // 4).bit_length() - 1)]
    scale = 1.0 / (math.sqrt(all_points / lines) * scen_total)
    pack, scens0 = packs_of(exposures, guarantees, guar_type, line_ids, returns, drivers)

    near = (pack, swap(pack, 1))
    scens1 = swap(scens0, 2)
    packs = {m: swap(pack, m) for m in deep}

    high0, low0, rt0, v = basis_of(exponents, scens0, near, lines)
    before = [(0, v)]
    packs = {m: after(p, v) for m, p in packs.items()}
    for m in far:
        top = max(h for h in deep if h <= m)
        if m not in packs:
            packs[m] = swap(packs[m ^ top], top)

    base = side * 2 + core
    start = jnp.stack([base, base ^ 1])
    high1, low1, rt1, keep, send = basis_of(
        exponents, after(scens1, v), start=start, first=high0
    )
    more = swap(send, 1)
    (v,) = values_of([rt1], near, [None], lines)
    before.append((1, v))
    keep, more = after((keep, more), v)
    gram = (keep + more) * (1.0 / scen_total)

    rts = [rt0, rt1]
    steps = list(deep)
    for i, m in enumerate(far):
        pair = [packs[m], swap(after(packs[m], v), 1)]
        if steps:
            mine = gram.astype(HALF)
            other = swap(mine, steps.pop(0))
        if m == far[-1]:
            break
        v0, v1 = values_of(rts, after(pair, gram), [None, None], lines)
        before += [(0, v0), (1, v1)]
        if i > 0:
            v = v0
        if steps:
            gram = mine.astype(F32) + after(other, v0).astype(F32)
        else:
            gram = after(gram, v0)
    basis = (high0, low0, high1, low1)
    keep, send = values_of(
        rts, after(pair, gram), [None, None], lines, before, basis, scale, core.reshape(1)
    )

    a = (mine.astype(F32) + after(other, keep).astype(F32)).astype(HALF)
    b = swap(a, 2)
    rhs = keep + swap(send, 1)
    for m in [2] + deep:
        mine = rhs.astype(HALF)
        other = swap(mine, m)
        if m == deep[-1]:
            c = swap(jnp.concatenate([a, b], axis=0), 1)
            order = jnp.stack([base ^ k for k in (0, 2, 1, 3)])
            gram = placed(4, order, [x.astype(F32) for x in (a, b, c)], terms)
            other = after(other, gram)
        rhs = mine.astype(F32) + other.astype(F32)
        if m == 2:
            b = after(b, rhs)
    other = swap(rhs, 1)
    first = jnp.where(core == 0, rhs, other)
    second = jnp.where(core == 0, other, rhs)
    return (gram, jnp.concatenate([first, second], axis=0).T)


def solution(mesh):
    spots = (
        P(None, ("grp", "scen")),
        P(("grp", "scen"), None),
        P(("grp", "scen")),
        P(("grp", "scen")),
        P(("grp", "scen")),
        P(None, ("grp", "scen")),
        P(),
    )
    return jax.shard_map(
        functools.partial(local, mesh.shape["scen"]),
        mesh=mesh,
        in_specs=spots,
        out_specs=(P("grp", None), P("grp", None)),
        check_vma=False,
    )
```

time: 73.2 us -> 70.3 us (0.960)
  starting transfers between devices: 21.6 us -> 14.2 us
  local copies, waits for them, and re-layouts: 2.84 us -> 5.44 us
  waiting for transfers between devices: 16.1 us -> 18 us
    ppermute x23 -> x18, starting transfers between devices: 21.6 us -> 14.2 us  [swap(): return lax.ppermute(x, 'scen', [(i, i ^ mask) for i in range(n)])]
    pallas_call x3, Pallas kernels: 3.38 us -> 7.71 us  [the longest x1 4.12 us: basis_of(): pl.pallas_call(first_kernel, out_shape=shapes, scratch_shapes=[pltpu.VMEM...]
    pallas_call x5 -> x4, Pallas kernels: 23.1 us -> 19.5 us  [values_of(): pl.pallas_call(kernel, in_specs=specs, out_shape=shape, scratch_shapes=sc...]
    unnamed x18 -> x27, local copies, waits for them, and re-layouts: 1.8 us -> 5.44 us
    ppermute x23 -> x18, waiting for transfers between devices: 16.1 us -> 18 us  [swap(): return lax.ppermute(x, 'scen', [(i, i ^ mask) for i in range(n)])]
    concatenate x4 -> x0, local copies, waits for them, and re-layouts: 1.02 us -> none  [the longest x3 1.01 us: local(): pack = jnp.concatenate([exposures.T, rows], axis=0)]
  transfers between devices with their start and end apart: 23 -> 18, of which waited for: 8 -> 9; matrix products, arithmetic and copies ran while one was open for 2% -> 1% of each run, Pallas kernels for 29% -> 40%
where the time goes in v3:
time: 70.3 us; the launch traced here: 70.1 us
  Pallas kernels  30.4 us (43%)
  waiting for transfers between devices  18 us (26%)
  starting transfers between devices  14.2 us (20%)
  local copies, waits for them, and re-layouts  5.44 us (8%)
  other arithmetic  1.15 us (2%)
  between operations  0.96 us (1%)
    pallas_call x4, Pallas kernels, values_of(): pl.pallas_call(kernel, in_specs=specs, out_shape=shape, scratch_shapes=sc...  19.5 us
    ppermute x18, waiting for transfers between devices, swap(): return lax.ppermute(x, 'scen', [(i, i ^ mask) for i in range(n)])  18 us
    ppermute x18, starting transfers between devices, swap(): return lax.ppermute(x, 'scen', [(i, i ^ mask) for i in range(n)])  14.2 us
    unnamed x27, local copies, waits for them, and re-layouts  5.44 us
    pallas_call x1, Pallas kernels, basis_of(): pl.pallas_call(first_kernel, out_shape=shapes, scratch_shapes=[pltpu.VMEM...  4.12 us
    pallas_call x1, Pallas kernels, basis_of(): pl.pallas_call(gram_kernel, in_specs=[pl.BlockSpec(memory_space=pltpu.SME...  3.19 us
    pallas_call x1, Pallas kernels, packs_of(): pl.pallas_call(pack_kernel, in_specs=[pl.BlockSpec(memory_space=pltpu.HBM...  2.01 us
    pallas_call x1, Pallas kernels, placed(): pl.pallas_call(functools.partial(place_kernel, blocks), in_specs=[pl.Bloc...  1.59 us
  transfers between devices with their start and end apart: 18, of which 9 were waited for; matrix products, arithmetic and copies ran while one was open for 1% of the time, Pallas kernels for 40%

profile of v3, /device:TPU:0, one launch (start us, length us, event | category | flops | bytes accessed | tf_op | source)
XLA Modules:
  0.0 70.1 jit_solution(6195870337592543270)
XLA Ops:
  0.6 2.0 %shard_map.86 = (bf16[80,1024]{1,0:T(8,128)(2,1)}, bf16[144,1024]{1,0:T(8,128)(2,1)}) custom-call(bf16[64,1024]{1,0:T(8,128)(2,1)} %bitcast.11, f32[1,1024]{1,0:T(1,128)} %bitcast.12, s32[1,1024]{1,0:T(1,128)} %bitcast.13, s32[1,1024]{1,0:T(1,128)} %bitcast.14, bf16[64,1024]{1,0:T(8,128)(2,1)} %refs_4_.1, f32[40,1024]{1,0:T(8,128)} %refs_5_.1), custom_call_target="tpu_custom_call" | custom-call | flops 1048576 | bytes 1048576 | tf_op jit(solution)/shard_map/pallas_call | solution.py:63
  2.7 0.5 collective-permute-start.1
  3.2 2.6 %collective-permute-start.4 = (bf16[80,1024]{1,0:T(8,128)(2,1)}, bf16[80,1024]{1,0:T(8,128)(2,1)S(1)}, u32[]{:S(2)}, u32[]{:S(2)}) collective-permute-start(bf16[80,1024]{1,0:T(8,128)(2,1)} %get-tuple-element.38.p0.refs_1_), channel_id=1, source_target_pairs={{0,4},{1,5},{2,6},{3,7},{4,0},{5,1},{6,2},{7,3},{8,12},{9,13},{10,... | collective-permute-start | bytes 491528 | tf_op jit(solution)/shard_map/ppermute | solution.py:294
  5.8 2.6 %collective-permute-start.8 = (bf16[80,1024]{1,0:T(8,128)(2,1)}, bf16[80,1024]{1,0:T(8,128)(2,1)S(1)}, u32[]{:S(2)}, u32[]{:S(2)}) collective-permute-start(bf16[80,1024]{1,0:T(8,128)(2,1)} %get-tuple-element.38.p0.refs_1_), channel_id=1, source_target_pairs={{0,8},{1,9},{2,10},{3,11},{4,12},{5,13},{6,14},{7,15},{8,0},{9,1},... | collective-permute-start | bytes 491528 | tf_op jit(solution)/shard_map/ppermute | solution.py:294
  8.4 1.5 %collective-permute-start = (bf16[144,1024]{1,0:T(8,128)(2,1)}, bf16[144,1024]{1,0:T(8,128)(2,1)S(1)}, u32[]{:S(2)}, u32[]{:S(2)}) collective-permute-start(bf16[144,1024]{1,0:T(8,128)(2,1)} %get-tuple-element.37.scens), channel_id=1, source_target_pairs={{0,2},{1,3},{2,0},{3,1},{4,6},{5,7},{6,4},{7,5},{8,10},{9,11},{10,... | collective-permute-start | bytes 884744 | tf_op jit(solution)/shard_map/ppermute | solution.py:294
  10.2 0.9 %copy-done.1 = bf16[80,1024]{1,0:T(8,128)(2,1)S(1)} copy-done((bf16[80,1024]{1,0:T(8,128)(2,1)S(1)}, bf16[80,1024]{1,0:T(8,128)(2,1)}, u32[]{:S(2)}) %copy-start.1) | copy-done | bytes 163864
  11.1 4.1 %shard_map.87 = (bf16[512,1024]{1,0:T(8,128)(2,1)S(1)}, bf16[512,1024]{1,0:T(8,128)(2,1)S(1)}, bf16[1024,128]{1,0:T(8,128)(2,1)S(1)}, f32[1024,64]{1,0:T(8,128)S(1)}) custom-call(s32[512,40]{1,0:T(8,128)S(1)} %copy.10.exps, bf16[144,1024]{1,0:T(8,128)(2,1)S(1)} %copy-done, bf16[80,1024]{1,0:T(8,128)(2,1)S(1)} %copy-done.1, ...), custom_call_target="tpu_custom_call" | custom-call | flops 3000000000 | bytes 3145728 | tf_op jit(solution)/shard_map/pallas_call | solution.py:236
  15.2 1.0 %copy-done.6 = bf16[512,1024]{1,0:T(8,128)(2,1)} copy-done((bf16[512,1024]{1,0:T(8,128)(2,1)}, bf16[512,1024]{1,0:T(8,128)(2,1)S(1)}, u32[]{:S(2)}) %copy-start.6) | copy-done | bytes 1048600
  16.2 0.7 copy-done.10
  16.9 0.5 collective-permute-done.scens
  17.4 3.2 %shard_map.88 = (bf16[512,1024]{1,0:T(8,128)(2,1)S(1)}, bf16[512,1024]{1,0:T(8,128)(2,1)S(1)}, bf16[1024,128]{1,0:T(8,128)(2,1)S(1)}, f32[128,512]{1,0:T(8,128)S(1)}, f32[128,512]{1,0:T(8,128)S(1)}) custom-call(s32[2]{0:T(128)S(1)} %pad_add_fusion.1.start, s32[512,40]{1,0:T(8,128)S(1)} %copy.10.exps, bf16[144,1024]{1,0:T(8,128)(2,1)S(1)} %collective-permute-done.scens, ...), custom_call_target="tpu_custom_call" | custom-call | flops 3000000000 | bytes 3145728 | tf_op jit(solution)/shard_map/pallas_call | solution.py:248
  20.6 1.0 %copy-done.2 = bf16[512,1024]{1,0:T(8,128)(2,1)} copy-done((bf16[512,1024]{1,0:T(8,128)(2,1)}, bf16[512,1024]{1,0:T(8,128)(2,1)S(1)}, u32[]{:S(2)}) %copy-start.2) | copy-done | bytes 1048600
  21.6 3.0 %shard_map.89.refs_5_ = f32[1024,64]{1,0:T(8,128)S(1)} custom-call(bf16[1024,128]{1,0:T(8,128)(2,1)S(1)} %get-tuple-element.44.refs_0_.refs_1_, bf16[80,1024]{1,0:T(8,128)(2,1)S(1)} %copy-done.1, bf16[80,1024]{1,0:T(8,128)(2,1)S(1)} %collective-permute-done.1.p1.refs_2_), custom_call_target="tpu_custom_call" | custom-call | flops 3565158400 | bytes 1048576 | tf_op jit(solution)/shard_map/pallas_call | solution.py:162
  24.6 0.8 %copy-done.8 = f32[1024,64]{1,0:T(8,128)} copy-done((f32[1024,64]{1,0:T(8,128)}, f32[1024,64]{1,0:T(8,128)S(1)}, u32[]{:S(2)}) %copy-start.8) | copy-done | bytes 262168
  26.3 0.5 collective-permute-done.9.refs_3_
  26.8 0.9 %copy-done.11 = bf16[1024,128]{1,0:T(8,128)(2,1)S(1)} copy-done((bf16[1024,128]{1,0:T(8,128)(2,1)S(1)}, bf16[1024,128]{1,0:T(8,128)(2,1)}, u32[]{:S(2)}) %copy-start.11) | copy-done | bytes 262168
  27.8 5.4 %shard_map.91 = (f32[1024,64]{1,0:T(8,128)S(1)}, f32[1024,64]{1,0:T(8,128)S(1)}) custom-call(bf16[1024,128]{1,0:T(8,128)(2,1)S(1)} %copy-done.11, bf16[1024,128]{1,0:T(8,128)(2,1)S(1)} %get-tuple-element.44.refs_0_.refs_1_, bf16[80,1024]{1,0:T(8,128)(2,1)S(1)} %collective-permute-done.8.refs_2_, bf16[80,1024]{1,0:T(8,128)(2,1)S(1)} %collective-permute-done.9.refs_3_), custom_call_target="tpu_custom_call" | custom-call | flops 7130316800 | bytes 1048576 | tf_op jit(solution)/shard_map/pallas_call | solution.py:162
  33.1 3.2 %collective-permute-done.7.refs_2_ = bf16[80,1024]{1,0:T(8,128)(2,1)S(1)} collective-permute-done((bf16[80,1024]{1,0:T(8,128)(2,1)S(1)}, bf16[80,1024]{1,0:T(8,128)(2,1)S(1)}, u32[]{:S(2)}, u32[]{:S(2)}) %collective-permute-start.7) | collective-permute-done | bytes 163872 | tf_op jit(solution)/shard_map/ppermute | solution.py:294
  36.6 5.2 %shard_map.90 = (f32[1024,64]{1,0:T(8,128)S(1)}, f32[1024,64]{1,0:T(8,128)S(1)}) custom-call(bf16[1024,128]{1,0:T(8,128)(2,1)S(1)} %copy-done.11, bf16[1024,128]{1,0:T(8,128)(2,1)S(1)} %get-tuple-element.44.refs_0_.refs_1_, bf16[80,1024]{1,0:T(8,128)(2,1)S(1)} %collective-permute-done.4.refs_2_, bf16[80,1024]{1,0:T(8,128)(2,1)S(1)} %collective-permute-done.5.refs_3_), custom_call_target="tpu_custom_call" | custom-call | flops 7130316800 | bytes 1048576 | tf_op jit(solution)/shard_map/pallas_call | solution.py:162
  41.8 6.0 %shard_map.92 = (f32[32,512]{1,0:T(8,128)S(1)}, f32[32,512]{1,0:T(8,128)S(1)}) custom-call(bf16[1024,128]{1,0:T(8,128)(2,1)S(1)} %copy-done.11, bf16[1024,128]{1,0:T(8,128)(2,1)S(1)} %get-tuple-element.44.refs_0_.refs_1_, bf16[80,1024]{1,0:T(8,128)(2,1)S(1)} %collective-permute-done.7.refs_2_, bf16[80,1024]{1,0:T(8,128)(2,1)S(1)} %collective-permute-done.10.refs_3_, ...), custom_call_target="tpu_custom_call" | custom-call | flops 7130316800 | bytes 1048576 | tf_op jit(solution)/shard_map/pallas_call | solution.py:162
  47.8 0.5 collective-permute-start.12
  48.3 1.7 %collective-permute-start.6 = (f16[128,512]{1,0:T(8,128)(2,1)S(1)}, f16[128,512]{1,0:T(8,128)(2,1)S(1)}, u32[]{:S(2)}, u32[]{:S(2)}) collective-permute-start(f16[128,512]{1,0:T(8,128)(2,1)S(1)} %fusion.1), channel_id=1, source_target_pairs={{0,8},{1,9},{2,10},{3,11},{4,12},{5,13},{6,14},{7,15},{8,0},{9,1},... | collective-permute-start | bytes 393224 | tf_op jit(solution)/shard_map/ppermute | solution.py:294
  50.0 1.6 %collective-permute-start.13 = (f16[32,512]{1,0:T(8,128)(2,1)S(1)}, f16[32,512]{1,0:T(8,128)(2,1)S(1)}, u32[]{:S(2)}, u32[]{:S(2)}) collective-permute-start(f16[32,512]{1,0:T(8,128)(2,1)S(1)} %add_convert_fusion.2), channel_id=1, source_target_pairs={{0,2},{1,3},{2,0},{3,1},{4,6},{5,7},{6,4},{7,5},{8,10},{9,11},{10,... | collective-permute-start | bytes 98312 | tf_op jit(solution)/shard_map/ppermute | solution.py:294
  51.6 6.0 %collective-permute-done.6 = f16[128,512]{1,0:T(8,128)(2,1)S(1)} collective-permute-done((f16[128,512]{1,0:T(8,128)(2,1)S(1)}, f16[128,512]{1,0:T(8,128)(2,1)S(1)}, u32[]{:S(2)}, u32[]{:S(2)}) %collective-permute-start.6) | collective-permute-done | bytes 131104 | tf_op jit(solution)/shard_map/ppermute | solution.py:294
  57.6 1.6 %collective-permute-start.11 = (f16[128,512]{1,0:T(8,128)(2,1)S(1)}, f16[128,512]{1,0:T(8,128)(2,1)S(1)}, u32[]{:S(2)}, u32[]{:S(2)}) collective-permute-start(f16[128,512]{1,0:T(8,128)(2,1)S(1)} %get-tuple-element.73), channel_id=1, source_target_pairs={{0,2},{1,3},{2,0},{3,1},{4,6},{5,7},{6,4},{7,5},{8,10},{9,11},{10,... | collective-permute-start | bytes 393224 | tf_op jit(solution)/shard_map/ppermute | solution.py:294
  59.3 3.3 %collective-permute-done.11 = f16[128,512]{1,0:T(8,128)(2,1)S(1)} collective-permute-done((f16[128,512]{1,0:T(8,128)(2,1)S(1)}, f16[128,512]{1,0:T(8,128)(2,1)S(1)}, u32[]{:S(2)}, u32[]{:S(2)}) %collective-permute-start.11) | collective-permute-done | bytes 131104 | tf_op jit(solution)/shard_map/ppermute | solution.py:294
  62.8 0.4 collective-permute-done.15
  63.7 0.7 collective-permute-done.14
  64.4 1.6 %shard_map.93 = f32[512,512]{1,0:T(8,128)} custom-call(s32[4]{0:T(128)S(1)} %pad_add_fusion.refs_0_, f32[128,512]{1,0:T(8,128)S(1)} %get-tuple-element.72.refs_1_, f32[128,512]{1,0:T(8,128)S(1)} %convert_element_type.68.refs_2_, f32[256,512]{1,0:T(8,128)S(1)} %convert_element_type.69.refs_3_), custom_call_target="tpu_custom_call" | custom-call | flops 1048576 | bytes 2097152 | tf_op jit(solution)/shard_map/pallas_call | solution.py:269
  66.0 2.1 %collective-permute-done.16 = f16[32,512]{1,0:T(8,128)(2,1)S(1)} collective-permute-done((f16[32,512]{1,0:T(8,128)(2,1)S(1)}, f16[32,512]{1,0:T(8,128)(2,1)S(1)}, u32[]{:S(2)}, u32[]{:S(2)}) %collective-permute-start.16) | collective-permute-done | bytes 32800 | tf_op jit(solution)/shard_map/ppermute | solution.py:294
  68.2 1.2 %collective-permute-done.17 = f32[32,512]{1,0:T(8,128)S(1)} collective-permute-done((f32[32,512]{1,0:T(8,128)S(1)}, f32[32,512]{1,0:T(8,128)S(1)}, u32[]{:S(2)}, u32[]{:S(2)}) %collective-permute-start.17) | collective-permute-done | bytes 65568 | tf_op jit(solution)/shard_map/ppermute | solution.py:294
  69.5 0.7 maximum_bitcast_fusion
  (53 shorter events, 2.2 us)
Async XLA Ops:
  0.6 9.4 %copy-start.12 = (s32[512,40]{0,1:T(8,128)S(1)}, s32[512,40]{0,1:T(8,128)}, u32[]{:S(2)}) copy-start(s32[512,40]{0,1:T(8,128)} %param.13) | copy-start | bytes 245764
  2.7 7.5 %copy-start = (bf16[144,1024]{1,0:T(8,128)(2,1)S(1)}, bf16[144,1024]{1,0:T(8,128)(2,1)}, u32[]{:S(2)}) copy-start(bf16[144,1024]{1,0:T(8,128)(2,1)} %get-tuple-element.37.scens) | copy-start | bytes 884740
  2.7 7.5 %collective-permute-start.1 = (bf16[80,1024]{1,0:T(8,128)(2,1)}, bf16[80,1024]{1,0:T(8,128)(2,1)S(1)}, u32[]{:S(2)}, u32[]{:S(2)}) collective-permute-start(bf16[80,1024]{1,0:T(8,128)(2,1)} %get-tuple-element.38.p0.refs_1_), channel_id=1, source_target_pairs={{0,1},{1,0},{2,3},{3,2},{4,5},{5,4},{6,7},{7,6},{8,9},{9,8},{10,11... | collective-permute-start | bytes 491528 | tf_op jit(solution)/shard_map/ppermute | solution.py:294
  3.2 22.2 %collective-permute-start.4 = (bf16[80,1024]{1,0:T(8,128)(2,1)}, bf16[80,1024]{1,0:T(8,128)(2,1)S(1)}, u32[]{:S(2)}, u32[]{:S(2)}) collective-permute-start(bf16[80,1024]{1,0:T(8,128)(2,1)} %get-tuple-element.38.p0.refs_1_), channel_id=1, source_target_pairs={{0,4},{1,5},{2,6},{3,7},{4,0},{5,1},{6,2},{7,3},{8,12},{9,13},{10,... | collective-permute-start | bytes 491528 | tf_op jit(solution)/shard_map/ppermute | solution.py:294
  5.8 11.1 %collective-permute-start.8 = (bf16[80,1024]{1,0:T(8,128)(2,1)}, bf16[80,1024]{1,0:T(8,128)(2,1)S(1)}, u32[]{:S(2)}, u32[]{:S(2)}) collective-permute-start(bf16[80,1024]{1,0:T(8,128)(2,1)} %get-tuple-element.38.p0.refs_1_), channel_id=1, source_target_pairs={{0,8},{1,9},{2,10},{3,11},{4,12},{5,13},{6,14},{7,15},{8,0},{9,1},... | collective-permute-start | bytes 491528 | tf_op jit(solution)/shard_map/ppermute | solution.py:294
  8.4 9.0 %collective-permute-start = (bf16[144,1024]{1,0:T(8,128)(2,1)}, bf16[144,1024]{1,0:T(8,128)(2,1)S(1)}, u32[]{:S(2)}, u32[]{:S(2)}) collective-permute-start(bf16[144,1024]{1,0:T(8,128)(2,1)} %get-tuple-element.37.scens), channel_id=1, source_target_pairs={{0,2},{1,3},{2,0},{3,1},{4,6},{5,7},{6,4},{7,5},{8,10},{9,11},{10,... | collective-permute-start | bytes 884744 | tf_op jit(solution)/shard_map/ppermute | solution.py:294
  10.2 0.9 %copy-start.1 = (bf16[80,1024]{1,0:T(8,128)(2,1)S(1)}, bf16[80,1024]{1,0:T(8,128)(2,1)}, u32[]{:S(2)}) copy-start(bf16[80,1024]{1,0:T(8,128)(2,1)} %get-tuple-element.38.p0.refs_1_) | copy-start | bytes 491524
  15.2 1.0 %copy-start.6 = (bf16[512,1024]{1,0:T(8,128)(2,1)}, bf16[512,1024]{1,0:T(8,128)(2,1)S(1)}, u32[]{:S(2)}) copy-start(bf16[512,1024]{1,0:T(8,128)(2,1)S(1)} %get-tuple-element.64.refs_11_) | copy-start | bytes 3145732
  16.2 0.7 copy-start.10
  20.6 1.0 %copy-start.2 = (bf16[512,1024]{1,0:T(8,128)(2,1)}, bf16[512,1024]{1,0:T(8,128)(2,1)S(1)}, u32[]{:S(2)}) copy-start(bf16[512,1024]{1,0:T(8,128)(2,1)S(1)} %get-tuple-element.65.refs_12_) | copy-start | bytes 3145732
  21.6 3.0 %copy-start.4 = (bf16[512,1024]{1,0:T(8,128)(2,1)}, bf16[512,1024]{1,0:T(8,128)(2,1)S(1)}, u32[]{:S(2)}) copy-start(bf16[512,1024]{1,0:T(8,128)(2,1)S(1)} %get-tuple-element.66.refs_13_) | copy-start | bytes 3145732
  24.6 0.8 %copy-start.8 = (f32[1024,64]{1,0:T(8,128)}, f32[1024,64]{1,0:T(8,128)S(1)}, u32[]{:S(2)}) copy-start(f32[1024,64]{1,0:T(8,128)S(1)} %shard_map.89.refs_5_) | copy-start | bytes 786436
  25.4 1.4 %collective-permute-start.9 = (bf16[80,1024]{1,0:T(8,128)(2,1)S(1)}, bf16[80,1024]{1,0:T(8,128)(2,1)S(1)}, u32[]{:S(2)}, u32[]{:S(2)}) collective-permute-start(bf16[80,1024]{1,0:T(8,128)(2,1)S(1)} %collective-permute-done.8.refs_2_), channel_id=1, source_target_pairs={{0,1},{1,0},{2,3},{3,2},{4,5},{5,4},{6,7},{7,6},{8,9},{9,8},{10,11... | collective-permute-start | bytes 491528 | tf_op jit(solution)/shard_map/ppermute | solution.py:294
  25.4 10.9 %collective-permute-start.7 = (bf16[80,1024]{1,0:T(8,128)(2,1)S(1)}, bf16[80,1024]{1,0:T(8,128)(2,1)S(1)}, u32[]{:S(2)}, u32[]{:S(2)}) collective-permute-start(bf16[80,1024]{1,0:T(8,128)(2,1)S(1)} %collective-permute-done.4.refs_2_), channel_id=1, source_target_pairs={{0,8},{1,9},{2,10},{3,11},{4,12},{5,13},{6,14},{7,15},{8,0},{9,1},... | collective-permute-start | bytes 491528 | tf_op jit(solution)/shard_map/ppermute | solution.py:294
  25.8 10.6 %collective-permute-start.2 = (f32[128,512]{1,0:T(8,128)S(1)}, f32[128,512]{1,0:T(8,128)S(1)}, u32[]{:S(2)}, u32[]{:S(2)}) collective-permute-start(f32[128,512]{1,0:T(8,128)S(1)} %get-tuple-element.43), channel_id=1, source_target_pairs={{0,1},{1,0},{2,3},{3,2},{4,5},{5,4},{6,7},{7,6},{8,9},{9,8},{10,11... | collective-permute-start | bytes 786440 | tf_op jit(solution)/shard_map/ppermute | solution.py:294
  26.0 10.6 %collective-permute-start.5 = (bf16[80,1024]{1,0:T(8,128)(2,1)S(1)}, bf16[80,1024]{1,0:T(8,128)(2,1)S(1)}, u32[]{:S(2)}, u32[]{:S(2)}) collective-permute-start(bf16[80,1024]{1,0:T(8,128)(2,1)S(1)} %collective-permute-done.4.refs_2_), channel_id=1, source_target_pairs={{0,1},{1,0},{2,3},{3,2},{4,5},{5,4},{6,7},{7,6},{8,9},{9,8},{10,11... | collective-permute-start | bytes 491528 | tf_op jit(solution)/shard_map/ppermute | solution.py:294
  26.8 1.0 %copy-start.11 = (bf16[1024,128]{1,0:T(8,128)(2,1)S(1)}, bf16[1024,128]{1,0:T(8,128)(2,1)}, u32[]{:S(2)}) copy-start(bf16[1024,128]{1,0:T(8,128)(2,1)} %copy-done.10) | copy-start | bytes 786436
  36.3 5.4 %collective-permute-start.10 = (bf16[80,1024]{1,0:T(8,128)(2,1)S(1)}, bf16[80,1024]{1,0:T(8,128)(2,1)S(1)}, u32[]{:S(2)}, u32[]{:S(2)}) collective-permute-start(bf16[80,1024]{1,0:T(8,128)(2,1)S(1)} %collective-permute-done.7.refs_2_), channel_id=1, source_target_pairs={{0,1},{1,0},{2,3},{3,2},{4,5},{5,4},{6,7},{7,6},{8,9},{9,8},{10,11... | collective-permute-start | bytes 491528 | tf_op jit(solution)/shard_map/ppermute | solution.py:294
  36.4 5.3 %copy-start.3 = (bf16[512,1024]{1,0:T(8,128)(2,1)S(1)}, bf16[512,1024]{1,0:T(8,128)(2,1)}, u32[]{:S(2)}) copy-start(bf16[512,1024]{1,0:T(8,128)(2,1)} %copy-done.2) | copy-start | bytes 3145732
  36.5 5.3 %copy-start.5 = (bf16[512,1024]{1,0:T(8,128)(2,1)S(1)}, bf16[512,1024]{1,0:T(8,128)(2,1)}, u32[]{:S(2)}) copy-start(bf16[512,1024]{1,0:T(8,128)(2,1)} %copy-done.4) | copy-start | bytes 3145732
  36.5 5.3 %copy-start.7 = (bf16[512,1024]{1,0:T(8,128)(2,1)S(1)}, bf16[512,1024]{1,0:T(8,128)(2,1)}, u32[]{:S(2)}) copy-start(bf16[512,1024]{1,0:T(8,128)(2,1)} %copy-done.6) | copy-start | bytes 3145732
  36.5 5.3 %copy-start.9 = (f32[1024,64]{1,0:T(8,128)S(1)}, f32[1024,64]{1,0:T(8,128)}, u32[]{:S(2)}) copy-start(f32[1024,64]{1,0:T(8,128)} %copy-done.8) | copy-start | bytes 786436
  36.5 11.8 %collective-permute-start.3 = (f16[128,512]{1,0:T(8,128)(2,1)S(1)}, f16[128,512]{1,0:T(8,128)(2,1)S(1)}, u32[]{:S(2)}, u32[]{:S(2)}) collective-permute-start(f16[128,512]{1,0:T(8,128)(2,1)S(1)} %fusion.3), channel_id=1, source_target_pairs={{0,4},{1,5},{2,6},{3,7},{4,0},{5,1},{6,2},{7,3},{8,12},{9,13},{10,... | collective-permute-start | bytes 393224 | tf_op jit(solution)/shard_map/ppermute | solution.py:294
  47.8 2.2 %collective-permute-start.12 = (f32[32,512]{1,0:T(8,128)S(1)}, f32[32,512]{1,0:T(8,128)S(1)}, u32[]{:S(2)}, u32[]{:S(2)}) collective-permute-start(f32[32,512]{1,0:T(8,128)S(1)} %get-tuple-element.69), channel_id=1, source_target_pairs={{0,1},{1,0},{2,3},{3,2},{4,5},{5,4},{6,7},{7,6},{8,9},{9,8},{10,11... | collective-permute-start | bytes 196616 | tf_op jit(solution)/shard_map/ppermute | solution.py:294
  48.3 9.3 %collective-permute-start.6 = (f16[128,512]{1,0:T(8,128)(2,1)S(1)}, f16[128,512]{1,0:T(8,128)(2,1)S(1)}, u32[]{:S(2)}, u32[]{:S(2)}) collective-permute-start(f16[128,512]{1,0:T(8,128)(2,1)S(1)} %fusion.1), channel_id=1, source_target_pairs={{0,8},{1,9},{2,10},{3,11},{4,12},{5,13},{6,14},{7,15},{8,0},{9,1},... | collective-permute-start | bytes 393224 | tf_op jit(solution)/shard_map/ppermute | solution.py:294
  50.0 9.2 %collective-permute-start.13 = (f16[32,512]{1,0:T(8,128)(2,1)S(1)}, f16[32,512]{1,0:T(8,128)(2,1)S(1)}, u32[]{:S(2)}, u32[]{:S(2)}) collective-permute-start(f16[32,512]{1,0:T(8,128)(2,1)S(1)} %add_convert_fusion.2), channel_id=1, source_target_pairs={{0,2},{1,3},{2,0},{3,1},{4,6},{5,7},{6,4},{7,5},{8,10},{9,11},{10,... | collective-permute-start | bytes 98312 | tf_op jit(solution)/shard_map/ppermute | solution.py:294
  57.6 5.0 %collective-permute-start.11 = (f16[128,512]{1,0:T(8,128)(2,1)S(1)}, f16[128,512]{1,0:T(8,128)(2,1)S(1)}, u32[]{:S(2)}, u32[]{:S(2)}) collective-permute-start(f16[128,512]{1,0:T(8,128)(2,1)S(1)} %get-tuple-element.73), channel_id=1, source_target_pairs={{0,2},{1,3},{2,0},{3,1},{4,6},{5,7},{6,4},{7,5},{8,10},{9,11},{10,... | collective-permute-start | bytes 393224 | tf_op jit(solution)/shard_map/ppermute | solution.py:294
  59.2 4.0 %collective-permute-start.15 = (f16[32,512]{1,0:T(8,128)(2,1)S(1)}, f16[32,512]{1,0:T(8,128)(2,1)S(1)}, u32[]{:S(2)}, u32[]{:S(2)}) collective-permute-start(f16[32,512]{1,0:T(8,128)(2,1)S(1)} %fusion), channel_id=1, source_target_pairs={{0,4},{1,5},{2,6},{3,7},{4,0},{5,1},{6,2},{7,3},{8,12},{9,13},{10,... | collective-permute-start | bytes 98312 | tf_op jit(solution)/shard_map/ppermute | solution.py:294
  62.7 1.6 %collective-permute-start.14 = (f16[256,512]{1,0:T(8,128)(2,1)S(1)}, f16[256,512]{1,0:T(8,128)(2,1)S(1)}, u32[]{:S(2)}, u32[]{:S(2)}) collective-permute-start(f16[256,512]{1,0:T(8,128)(2,1)S(1)} %pad_maximum_fusion), channel_id=1, source_target_pairs={{0,1},{1,0},{2,3},{3,2},{4,5},{5,4},{6,7},{7,6},{8,9},{9,8},{10,11... | collective-permute-start | bytes 786440 | tf_op jit(solution)/shard_map/ppermute | solution.py:294
  63.2 4.9 %collective-permute-start.16 = (f16[32,512]{1,0:T(8,128)(2,1)S(1)}, f16[32,512]{1,0:T(8,128)(2,1)S(1)}, u32[]{:S(2)}, u32[]{:S(2)}) collective-permute-start(f16[32,512]{1,0:T(8,128)(2,1)S(1)} %add_convert_fusion.1), channel_id=1, source_target_pairs={{0,8},{1,9},{2,10},{3,11},{4,12},{5,13},{6,14},{7,15},{8,0},{9,1},... | collective-permute-start | bytes 98312 | tf_op jit(solution)/shard_map/ppermute | solution.py:294
  68.1 1.3 %collective-permute-start.17 = (f32[32,512]{1,0:T(8,128)S(1)}, f32[32,512]{1,0:T(8,128)S(1)}, u32[]{:S(2)}, u32[]{:S(2)}) collective-permute-start(f32[32,512]{1,0:T(8,128)S(1)} %convert_add_fusion.1), channel_id=1, source_target_pairs={{0,1},{1,0},{2,3},{3,2},{4,5},{5,4},{6,7},{7,6},{8,9},{9,8},{10,11... | collective-permute-start | bytes 196616 | tf_op jit(solution)/shard_map/ppermute | solution.py:294

commit v4 on v3

--- a/solution.py
+++ b/solution.py
@@ -74,57 +74,81 @@
     )(*args)
 
 
-def value_kernel(plan, count, earlier, scale, *refs):
-    blocks = len(plan)
+def prepare(packs, w, oh, lev):
+    factors = w.shape[0] // 2
+    points = packs[0].shape[1]
+    for i, pack in enumerate(packs):
+        at = slice(i * points, (i + 1) * points)
+        e = pack[:factors, :].astype(F32) * LOG2E
+        high = e.astype(BF)
+        w[:factors, at] = high
+        w[factors:, at] = (e - high.astype(F32)).astype(BF)
+        tail = pack[factors:, :].astype(F32)
+        lev[:, at] = tail[0:1] + tail[1:2] + tail[2:3]
+        label = lax.broadcasted_iota(jnp.int32, (oh.shape[0], points), 0).astype(F32)
+        oh[:, at] = (label == tail[3:4]).astype(BF)
+
+
+def chunk_values(r, w, oh, lev, step):
+    total = None
+    for j in range(0, w.shape[1], step):
+        at = slice(j, j + step)
+        power = jnp.dot(r, w[:, at], preferred_element_type=F32)
+        payoff = jnp.maximum(lev[:, at] - jnp.exp2(power), 0.0).astype(BF)
+        part = lax.dot_general(
+            payoff, oh[:, at], (((1,), (1,)), ((), ())), preferred_element_type=F32
+        )
+        total = part if total is None else total + part
+    return total
+
+
+def value_kernel(blocks, count, earlier, scale, *refs):
     rts, refs = refs[:blocks], refs[blocks:]
-    stacks, refs = refs[:count], refs[count:]
+    packs, refs = refs[:count], refs[count:]
+    sources = list(rts)
     if scale:
         before, refs = refs[: len(earlier)], refs[len(earlier) :]
         basis, refs = refs[: 2 * blocks], refs[2 * blocks :]
-        core, keep, send, w, oh, lev, whole = refs
+        core, keep, send, w, oh, lev, sems, *held = refs
+        whole, held = held[0], held[1:]
+        sources += [*before, *basis]
     else:
-        outs, (w, oh, lev) = refs[:blocks], refs[blocks:]
+        outs, (w, oh, lev, sems, *held) = refs[:blocks], refs[blocks:]
+        sums, held = held[:blocks], held[blocks:]
+    loads = [pltpu.make_async_copy(a, b, sems.at[i]) for i, (a, b) in enumerate(zip(sources, held))]
+    for load in loads:
+        load.start()
     own, double = rts[0].shape
-    factors = double // 2
-    points = stacks[0].shape[1]
+    points = packs[0].shape[1]
+    prepare(packs, w, oh, lev)
+    for load in loads[:blocks]:
+        load.wait()
+    totals = [
+        [
+            chunk_values(held[i][s0 : s0 + CHUNK, :], w, oh, lev, points)
+            for s0 in range(0, own, CHUNK)
+        ]
+        for i in range(blocks)
+    ]
+    if not scale:
+        stores = []
+        for i in range(blocks):
+            sums[i][...] = jnp.concatenate(totals[i], axis=0)
+            stores.append(pltpu.make_async_copy(sums[i], outs[i], sems.at[len(sources) + i]))
+            stores[-1].start()
+        for store in stores:
+            store.wait()
+        return
+    for load in loads[blocks:]:
+        load.wait()
+    before, basis = held[blocks : blocks + len(before)], held[blocks + len(before) :]
     lines = oh.shape[0]
-    height = factors + TAIL
-    packs = [s.at[k : k + height] for s in stacks for k in range(0, s.shape[0], height)]
-    for i in range(len(packs)):
-        at = slice(i * points, (i + 1) * points)
-        e = packs[i][:factors, :].astype(F32) * LOG2E
-        high = e.astype(BF)
-        w[:factors, at] = high
-        w[factors:, at] = (e - high.astype(F32)).astype(BF)
-        tail = packs[i][factors:, :].astype(F32)
-        lev[:, at] = tail[0:1] + tail[1:2] + tail[2:3]
-        label = lax.broadcasted_iota(jnp.int32, (lines, points), 0).astype(F32)
-        oh[:, at] = (label == tail[3:4]).astype(BF)
-    sums = []
-    for i in range(blocks):
-        for s0 in range(0, own, CHUNK):
-            r = rts[i][s0 : s0 + CHUNK, :]
-            total = None
-            for j in plan[i] or range(len(packs)):
-                at = slice(j * points, (j + 1) * points)
-                power = jnp.dot(r, w[:, at], preferred_element_type=F32)
-                payoff = jnp.maximum(lev[:, at] - jnp.exp2(power), 0.0).astype(BF)
-                part = lax.dot_general(
-                    payoff, oh[:, at], (((1,), (1,)), ((), ())), preferred_element_type=F32
-                )
-                total = part if total is None else total + part
-            if not scale:
-                outs[i][s0 : s0 + CHUNK, :] = total
-                continue
-            for k, at in enumerate(earlier):
-                if at == i:
-                    total = total + before[k][s0 : s0 + CHUNK, :]
-            sums.append((i, s0, total))
-    if not scale:
-        return
     result = None
     for i in range(blocks):
-        v = jnp.concatenate([t for at, _, t in sums if at == i], axis=0)
+        v = jnp.concatenate(totals[i], axis=0)
+        for k, at in enumerate(earlier):
+            if at == i:
+                v = v + before[k][...]
         vh = v.astype(BF)
         vl = (v - vh.astype(F32)).astype(BF)
         both = jnp.concatenate([vh, vl], axis=1)
@@ -138,32 +162,49 @@
     send[...] = whole[pl.ds(pl.multiple_of((1 - core[0]) * half, half), half), :]
 
 
-def values_of(rts, packs, plan, lines, before=(), basis=(), scale=None, core=None):
+VSPEC = pl.BlockSpec(memory_space=pltpu.VMEM)
+SSPEC = pl.BlockSpec(memory_space=pltpu.SMEM)
+HSPEC = pl.BlockSpec(memory_space=pltpu.HBM)
+
+
+def like(arrays):
+    return [pltpu.VMEM(a.shape, a.dtype) for a in arrays]
+
+
+def point_scratch(double, lines, points):
+    return [
+        pltpu.VMEM((double, points), BF),
+        pltpu.VMEM((lines, points), BF),
+        pltpu.VMEM((1, points), F32),
+    ]
+
+
+def values_of(rts, packs, lines, before=(), basis=(), scale=None, core=None):
     own, double = rts[0].shape
     points = packs[0].shape[1]
-    count = sum(p.shape[0] for p in packs) // (double // 2 + TAIL)
-    pairs = own * points * len(plan) * count
-    scratch = [
-        pltpu.VMEM((double, points * count), BF),
-        pltpu.VMEM((lines, points * count), BF),
-        pltpu.VMEM((1, points * count), F32),
-    ]
-    specs = [pl.BlockSpec(memory_space=pltpu.VMEM)] * (len(rts) + len(packs) + len(before))
+    pairs = own * points * len(rts) * len(packs)
+    held = [*rts, *[v for _, v in before], *basis]
+    scratch = point_scratch(double, lines, points * len(packs))
+    scratch.append(pltpu.SemaphoreType.DMA((len(held) + len(rts),)))
+    specs = [HSPEC] * len(rts) + [VSPEC] * len(packs)
     if scale:
         terms = basis[0].shape[0]
-        specs += [pl.BlockSpec(memory_space=pltpu.VMEM)] * len(basis)
-        specs.append(pl.BlockSpec(memory_space=pltpu.SMEM))
+        specs += [HSPEC] * (len(before) + len(basis)) + [SSPEC]
         scratch.append(pltpu.VMEM((lines, terms), F32))
         shape = [jax.ShapeDtypeStruct((lines // 2, terms), F32)] * 2
+        outs = [VSPEC] * 2
         basis = [*basis, core]
     else:
         shape = [jax.ShapeDtypeStruct((own, lines), F32)] * len(rts)
-    kernel = functools.partial(value_kernel, plan, len(packs), [i for i, _ in before], scale)
+        outs = [HSPEC] * len(rts)
+        scratch += like(shape)
+    kernel = functools.partial(value_kernel, len(rts), len(packs), [i for i, _ in before], scale)
     return pl.pallas_call(
         kernel,
         in_specs=specs,
+        out_specs=outs,
         out_shape=shape,
-        scratch_shapes=scratch,
+        scratch_shapes=scratch + like(held),
         compiler_params=params(),
         cost_estimate=pl.CostEstimate(
             flops=1700 * pairs, bytes_accessed=2**20, transcendentals=pairs
@@ -200,27 +241,50 @@
         low[:, c : c + CHUNK] = (b - h.astype(F32)).astype(BF)
 
 
-def first_kernel(exps, scens, p0, p1, high, low, rt, out, w, oh, lev):
-    basis_kernel(exps, scens, high, low, rt)
-    value_kernel([None], 2, (), None, rt, p0, p1, out, w, oh, lev)
-
-
-def gram_kernel(start, exps, scens, first, high, low, rt, keep, send):
-    basis_kernel(exps, scens, high, low, rt)
+def first_kernel(exps, scens, p0, p1, *refs):
+    outs, (w, oh, lev, sems, packs, *held) = refs[:4], refs[4:]
+    loads = [pltpu.make_async_copy(p, packs.at[i], sems.at[4 + i]) for i, p in enumerate((p0, p1))]
+    for load in loads:
+        load.start()
+    stores = [pltpu.make_async_copy(a, b, sems.at[i]) for i, (a, b) in enumerate(zip(held, outs))]
+    basis_kernel(exps, scens, *held[:3])
+    for store in stores[:3]:
+        store.start()
+    for load in loads:
+        load.wait()
+    prepare([packs.at[0], packs.at[1]], w, oh, lev)
+    points = packs.shape[2]
+    for s0 in range(0, held[2].shape[0], CHUNK):
+        held[3][s0 : s0 + CHUNK, :] = chunk_values(
+            held[2][s0 : s0 + CHUNK, :], w, oh, lev, points
+        )
+    stores[3].start()
+    for store in stores:
+        store.wait()
+
+
+def gram_kernel(start, exps, scens, earlier, *refs):
+    outs, keep, send, (sems, first, *held) = refs[:3], refs[3], refs[4], refs[5:]
+    load = pltpu.make_async_copy(earlier, first, sems.at[3])
+    load.start()
+    stores = [pltpu.make_async_copy(a, b, sems.at[i]) for i, (a, b) in enumerate(zip(held, outs))]
+    high = held[0]
+    basis_kernel(exps, scens, *held)
+    for store in stores:
+        store.start()
+    load.wait()
     rows = keep.shape[0]
     for i, out in enumerate((keep, send)):
         r0 = pl.multiple_of(start[i] * rows, rows)
-        out[...] = lax.dot_general(
-            first[pl.ds(r0, rows), :],
-            first[...],
-            (((1,), (1,)), ((), ())),
-            preferred_element_type=F32,
-        ) + lax.dot_general(
-            high[pl.ds(r0, rows), :],
-            high[...],
-            (((1,), (1,)), ((), ())),
-            preferred_element_type=F32,
-        )
+        total = None
+        for b in (first, high):
+            part = lax.dot_general(
+                b[pl.ds(r0, rows), :], b[...], (((1,), (1,)), ((), ())), preferred_element_type=F32
+            )
+            total = part if total is None else total + part
+        out[...] = total
+    for store in stores:
+        store.wait()
 
 
 def basis_of(exponents, scens, near=(), lines=0, start=None, first=None):
@@ -228,27 +292,29 @@
     factors, own = scens.shape[0] - 2 * count, scens.shape[1]
     shapes = [jax.ShapeDtypeStruct((terms, own), BF)] * 2
     shapes.append(jax.ShapeDtypeStruct((own, 2 * factors), BF))
-    vmem = pl.BlockSpec(memory_space=pltpu.VMEM)
     cost = pl.CostEstimate(flops=3 * 10**9, bytes_accessed=3 * 2**20, transcendentals=0)
     if start is None:
-        points = near[0].shape[1] * len(near)
+        points = near[0].shape[1]
         shapes.append(jax.ShapeDtypeStruct((own, lines), F32))
         return pl.pallas_call(
             first_kernel,
+            in_specs=[VSPEC] * 2 + [HSPEC] * 2,
+            out_specs=[HSPEC] * 4,
             out_shape=shapes,
-            scratch_shapes=[
-                pltpu.VMEM((2 * factors, points), BF),
-                pltpu.VMEM((lines, points), BF),
-                pltpu.VMEM((1, points), F32),
-            ],
+            scratch_shapes=point_scratch(2 * factors, lines, 2 * points)
+            + [pltpu.SemaphoreType.DMA((6,)), pltpu.VMEM((2, *near[0].shape), BF)]
+            + like(shapes),
             compiler_params=params(),
             cost_estimate=cost,
         )(exponents, scens, *near)
+    scratch = [pltpu.SemaphoreType.DMA((4,)), *like([first]), *like(shapes)]
     shapes += [jax.ShapeDtypeStruct((terms // 4, terms), F32)] * 2
     return pl.pallas_call(
         gram_kernel,
-        in_specs=[pl.BlockSpec(memory_space=pltpu.SMEM)] + [vmem] * 3,
+        in_specs=[SSPEC, VSPEC, VSPEC, HSPEC],
+        out_specs=[HSPEC] * 3 + [VSPEC] * 2,
         out_shape=shapes,
+        scratch_shapes=scratch,
         compiler_params=params(),
         cost_estimate=cost,
     )(start, exponents, scens, first)
@@ -304,7 +370,7 @@
 
     high0, low0, rt0, v = basis_of(exponents, scens0, near, lines)
     before = [(0, v)]
-    packs = {m: after(p, v) for m, p in packs.items()}
+    packs[4] = after(packs[4], v)
     for m in far:
         top = max(h for h in deep if h <= m)
         if m not in packs:
@@ -316,7 +382,7 @@
         exponents, after(scens1, v), start=start, first=high0
     )
     more = swap(send, 1)
-    (v,) = values_of([rt1], near, [None], lines)
+    (v,) = values_of([rt1], near, lines)
     before.append((1, v))
     keep, more = after((keep, more), v)
     gram = (keep + more) * (1.0 / scen_total)
@@ -330,20 +396,21 @@
             other = swap(mine, steps.pop(0))
         if m == far[-1]:
             break
-        v0, v1 = values_of(rts, after(pair, gram), [None, None], lines)
+        v0, v1 = values_of(rts, after(pair, gram), lines)
         before += [(0, v0), (1, v1)]
         if i > 0:
             v = v0
-        if steps:
+        if other is not None:
             gram = mine.astype(F32) + after(other, v0).astype(F32)
+            other = None
         else:
             gram = after(gram, v0)
     basis = (high0, low0, high1, low1)
     keep, send = values_of(
-        rts, after(pair, gram), [None, None], lines, before, basis, scale, core.reshape(1)
+        rts, after(pair, gram), lines, before, basis, scale, core.reshape(1)
     )
 
-    a = (mine.astype(F32) + after(other, keep).astype(F32)).astype(HALF)
+    a = after(gram, keep).astype(HALF)
     b = swap(a, 2)
     rhs = keep + swap(send, 1)
     for m in [2] + deep:

time: 70.3 us -> 65.7 us (0.935)
  waiting for transfers between devices: 18 us -> 12.4 us
  local copies, waits for them, and re-layouts: 5.44 us -> 1.04 us
  Pallas kernels: 30.4 us -> 33.6 us
  starting transfers between devices: 14.2 us -> 16.4 us
    ppermute x18, waiting for transfers between devices: 18 us -> 12.4 us  [swap(): return lax.ppermute(x, 'scen', [(i, i ^ mask) for i in range(n)])]
    unnamed x27 -> x7, local copies, waits for them, and re-layouts: 5.44 us -> 1.04 us
    pallas_call x6, Pallas kernels: 26.8 us -> 30.1 us  [the longest x4 21.4 us: values_of(): pl.pallas_call(kernel, in_specs=specs, out_specs=outs, out_shape=shape, s...]
    ppermute x18, starting transfers between devices: 14.2 us -> 16.4 us  [swap(): return lax.ppermute(x, 'scen', [(i, i ^ mask) for i in range(n)])]
  transfers between devices with their start and end apart: 18 -> 18, of which waited for: 9 -> 12; matrix products, arithmetic and copies ran while one was open for 1% -> 1% of each run, Pallas kernels for 40% -> 38%
where the time goes in v4:
time: 65.7 us; the launch traced here: 65.5 us
  Pallas kernels  33.6 us (51%)
  starting transfers between devices  16.4 us (25%)
  waiting for transfers between devices  12.4 us (19%)
  other arithmetic  1.17 us (2%)
  local copies, waits for them, and re-layouts  1.04 us (2%)
  between operations  0.87 us (1%)
    pallas_call x4, Pallas kernels, values_of(): pl.pallas_call(kernel, in_specs=specs, out_specs=outs, out_shape=shape, s...  21.4 us
    ppermute x18, starting transfers between devices, swap(): return lax.ppermute(x, 'scen', [(i, i ^ mask) for i in range(n)])  16.4 us
    ppermute x18, waiting for transfers between devices, swap(): return lax.ppermute(x, 'scen', [(i, i ^ mask) for i in range(n)])  12.4 us
    pallas_call x1, Pallas kernels, basis_of(): pl.pallas_call(first_kernel, in_specs=[VSPEC] * 2 + [HSPEC] * 2, out_spec...  5.18 us
    pallas_call x1, Pallas kernels, basis_of(): pl.pallas_call(gram_kernel, in_specs=[SSPEC, VSPEC, VSPEC, HSPEC], out_sp...  3.53 us
    pallas_call x1, Pallas kernels, packs_of(): pl.pallas_call(pack_kernel, in_specs=[pl.BlockSpec(memory_space=pltpu.HBM...  1.99 us
    pallas_call x1, Pallas kernels, placed(): pl.pallas_call(functools.partial(place_kernel, blocks), in_specs=[pl.Bloc...  1.59 us
  transfers between devices with their start and end apart: 18, of which 12 were waited for; matrix products, arithmetic and copies ran while one was open for 1% of the time, Pallas kernels for 38%

profile of v4, /device:TPU:0, one launch (start us, length us, event | category | flops | bytes accessed | tf_op | source)
XLA Modules:
  0.0 65.5 jit_solution(6033713363296722419)
XLA Ops:
  0.6 2.0 %shard_map.86 = (bf16[80,1024]{1,0:T(8,128)(2,1)}, bf16[144,1024]{1,0:T(8,128)(2,1)}) custom-call(bf16[64,1024]{1,0:T(8,128)(2,1)} %bitcast.11, f32[1,1024]{1,0:T(1,128)} %bitcast.12, s32[1,1024]{1,0:T(1,128)} %bitcast.13, s32[1,1024]{1,0:T(1,128)} %bitcast.14, bf16[64,1024]{1,0:T(8,128)(2,1)} %refs_4_.1, f32[40,1024]{1,0:T(8,128)} %refs_5_.1), custom_call_target="tpu_custom_call" | custom-call | flops 1048576 | bytes 1048576 | tf_op jit(solution)/shard_map/pallas_call | solution.py:63
  2.7 0.5 collective-permute-start.1
  3.2 2.6 %collective-permute-start.4 = (bf16[80,1024]{1,0:T(8,128)(2,1)}, bf16[80,1024]{1,0:T(8,128)(2,1)S(1)}, u32[]{:S(2)}, u32[]{:S(2)}) collective-permute-start(bf16[80,1024]{1,0:T(8,128)(2,1)} %get-tuple-element.38.p0.refs_1_), channel_id=1, source_target_pairs={{0,4},{1,5},{2,6},{3,7},{4,0},{5,1},{6,2},{7,3},{8,12},{9,13},{10,... | collective-permute-start | bytes 491528 | tf_op jit(solution)/shard_map/ppermute | solution.py:360
  5.8 2.6 %collective-permute-start.7 = (bf16[80,1024]{1,0:T(8,128)(2,1)}, bf16[80,1024]{1,0:T(8,128)(2,1)S(1)}, u32[]{:S(2)}, u32[]{:S(2)}) collective-permute-start(bf16[80,1024]{1,0:T(8,128)(2,1)} %get-tuple-element.38.p0.refs_1_), channel_id=1, source_target_pairs={{0,8},{1,9},{2,10},{3,11},{4,12},{5,13},{6,14},{7,15},{8,0},{9,1},... | collective-permute-start | bytes 491528 | tf_op jit(solution)/shard_map/ppermute | solution.py:360
  8.4 1.5 %collective-permute-start = (bf16[144,1024]{1,0:T(8,128)(2,1)}, bf16[144,1024]{1,0:T(8,128)(2,1)S(1)}, u32[]{:S(2)}, u32[]{:S(2)}) collective-permute-start(bf16[144,1024]{1,0:T(8,128)(2,1)} %get-tuple-element.37.scens), channel_id=1, source_target_pairs={{0,2},{1,3},{2,0},{3,1},{4,6},{5,7},{6,4},{7,5},{8,10},{9,11},{10,... | collective-permute-start | bytes 884744 | tf_op jit(solution)/shard_map/ppermute | solution.py:360
  10.2 0.9 %copy-done.1 = bf16[80,1024]{1,0:T(8,128)(2,1)S(1)} copy-done((bf16[80,1024]{1,0:T(8,128)(2,1)S(1)}, bf16[80,1024]{1,0:T(8,128)(2,1)}, u32[]{:S(2)}) %copy-start.1) | copy-done | bytes 163864
  11.1 5.2 %shard_map.87 = (bf16[512,1024]{1,0:T(8,128)(2,1)S(1)}, bf16[512,1024]{1,0:T(8,128)(2,1)S(1)}, bf16[1024,128]{1,0:T(8,128)(2,1)S(1)}, f32[1024,64]{1,0:T(8,128)S(1)}) custom-call(s32[512,40]{1,0:T(8,128)S(1)} %copy.10.exps, bf16[144,1024]{1,0:T(8,128)(2,1)S(1)} %copy-done, bf16[80,1024]{1,0:T(8,128)(2,1)S(1)} %copy-done.1, ...), custom_call_target="tpu_custom_call" | custom-call | flops 3000000000 | bytes 3145728 | tf_op jit(solution)/shard_map/pallas_call | solution.py:299
  16.3 1.2 %collective-permute-done.scens = bf16[144,1024]{1,0:T(8,128)(2,1)S(1)} collective-permute-done((bf16[144,1024]{1,0:T(8,128)(2,1)}, bf16[144,1024]{1,0:T(8,128)(2,1)S(1)}, u32[]{:S(2)}, u32[]{:S(2)}) %collective-permute-start) | collective-permute-done | bytes 294944 | tf_op jit(solution)/shard_map/ppermute | solution.py:360
  17.4 3.5 %shard_map.88 = (bf16[512,1024]{1,0:T(8,128)(2,1)S(1)}, bf16[512,1024]{1,0:T(8,128)(2,1)S(1)}, bf16[1024,128]{1,0:T(8,128)(2,1)S(1)}, f32[128,512]{1,0:T(8,128)S(1)}, f32[128,512]{1,0:T(8,128)S(1)}) custom-call(s32[2]{0:T(128)S(1)} %pad_add_fusion.1.start, s32[512,40]{1,0:T(8,128)S(1)} %copy.10.exps, bf16[144,1024]{1,0:T(8,128)(2,1)S(1)} %collective-permute-done.scens, ...), custom_call_target="tpu_custom_call" | custom-call | flops 3000000000 | bytes 3145728 | tf_op jit(solution)/shard_map/pallas_call | solution.py:312
  21.0 3.2 %shard_map.89.refs_5_ = f32[1024,64]{1,0:T(8,128)S(1)} custom-call(bf16[1024,128]{1,0:T(8,128)(2,1)S(1)} %get-tuple-element.44.refs_0_.refs_1_, bf16[80,1024]{1,0:T(8,128)(2,1)S(1)} %copy-done.1, bf16[80,1024]{1,0:T(8,128)(2,1)S(1)} %collective-permute-done.1.p1.refs_2_), custom_call_target="tpu_custom_call" | custom-call | flops 3565158400 | bytes 1048576 | tf_op jit(solution)/shard_map/pallas_call | solution.py:202
  24.2 0.6 collective-permute-start.8
  24.8 0.3 collective-permute-start.9
  25.1 0.7 %collective-permute-done.8.refs_3_ = bf16[80,1024]{1,0:T(8,128)(2,1)S(1)} collective-permute-done((bf16[80,1024]{1,0:T(8,128)(2,1)S(1)}, bf16[80,1024]{1,0:T(8,128)(2,1)S(1)}, u32[]{:S(2)}, u32[]{:S(2)}) %collective-permute-start.8) | collective-permute-done | bytes 163872 | tf_op jit(solution)/shard_map/ppermute | solution.py:360
  25.9 0.5 collective-permute-start.3
  26.5 5.7 %shard_map.90 = (f32[1024,64]{1,0:T(8,128)S(1)}, f32[1024,64]{1,0:T(8,128)S(1)}) custom-call(bf16[1024,128]{1,0:T(8,128)(2,1)S(1)} %get-tuple-element.47.refs_0_, bf16[1024,128]{1,0:T(8,128)(2,1)S(1)} %get-tuple-element.44.refs_0_.refs_1_, bf16[80,1024]{1,0:T(8,128)(2,1)S(1)} %collective-permute-done.4.refs_2_, ...), custom_call_target="tpu_custom_call" | custom-call | flops 7130316800 | bytes 1048576 | tf_op jit(solution)/shard_map/pallas_call | solution.py:202
  32.5 2.8 %collective-permute-start.6 = (f16[128,512]{1,0:T(8,128)(2,1)S(1)}, f16[128,512]{1,0:T(8,128)(2,1)S(1)}, u32[]{:S(2)}, u32[]{:S(2)}) collective-permute-start(f16[128,512]{1,0:T(8,128)(2,1)S(1)} %fusion.1), channel_id=1, source_target_pairs={{0,8},{1,9},{2,10},{3,11},{4,12},{5,13},{6,14},{7,15},{8,0},{9,1},... | collective-permute-start | bytes 393224 | tf_op jit(solution)/shard_map/ppermute | solution.py:360
  35.3 5.5 %shard_map.91 = (f32[1024,64]{1,0:T(8,128)S(1)}, f32[1024,64]{1,0:T(8,128)S(1)}) custom-call(bf16[1024,128]{1,0:T(8,128)(2,1)S(1)} %get-tuple-element.47.refs_0_, bf16[1024,128]{1,0:T(8,128)(2,1)S(1)} %get-tuple-element.44.refs_0_.refs_1_, bf16[80,1024]{1,0:T(8,128)(2,1)S(1)} %collective-permute-done.7.refs_2_, ...), custom_call_target="tpu_custom_call" | custom-call | flops 7130316800 | bytes 1048576 | tf_op jit(solution)/shard_map/pallas_call | solution.py:202
  40.9 0.7 %collective-permute-done.6 = f16[128,512]{1,0:T(8,128)(2,1)S(1)} collective-permute-done((f16[128,512]{1,0:T(8,128)(2,1)S(1)}, f16[128,512]{1,0:T(8,128)(2,1)S(1)}, u32[]{:S(2)}, u32[]{:S(2)}) %collective-permute-start.6) | collective-permute-done | bytes 131104 | tf_op jit(solution)/shard_map/ppermute | solution.py:360
  41.6 0.6 collective-permute-done.10.refs_3_
  42.3 7.0 %shard_map.92 = (f32[32,512]{1,0:T(8,128)S(1)}, f32[32,512]{1,0:T(8,128)S(1)}) custom-call(bf16[1024,128]{1,0:T(8,128)(2,1)S(1)} %get-tuple-element.47.refs_0_, bf16[1024,128]{1,0:T(8,128)(2,1)S(1)} %get-tuple-element.44.refs_0_.refs_1_, bf16[80,1024]{1,0:T(8,128)(2,1)S(1)} %collective-permute-done.9.refs_2_, ...), custom_call_target="tpu_custom_call" | custom-call | flops 7130316800 | bytes 1048576 | tf_op jit(solution)/shard_map/pallas_call | solution.py:202
  49.5 1.1 %collective-permute-done.12 = f32[32,512]{1,0:T(8,128)S(1)} collective-permute-done((f32[32,512]{1,0:T(8,128)S(1)}, f32[32,512]{1,0:T(8,128)S(1)}, u32[]{:S(2)}, u32[]{:S(2)}) %collective-permute-start.12) | collective-permute-done | bytes 65568 | tf_op jit(solution)/shard_map/ppermute | solution.py:360
  50.6 1.6 %collective-permute-start.13 = (f16[32,512]{1,0:T(8,128)(2,1)S(1)}, f16[32,512]{1,0:T(8,128)(2,1)S(1)}, u32[]{:S(2)}, u32[]{:S(2)}) collective-permute-start(f16[32,512]{1,0:T(8,128)(2,1)S(1)} %add_convert_fusion.1), channel_id=1, source_target_pairs={{0,2},{1,3},{2,0},{3,1},{4,6},{5,7},{6,4},{7,5},{8,10},{9,11},{10,... | collective-permute-start | bytes 98312 | tf_op jit(solution)/shard_map/ppermute | solution.py:360
  52.3 0.6 collective-permute-start.11
  52.8 1.8 %collective-permute-done.13 = f16[32,512]{1,0:T(8,128)(2,1)S(1)} collective-permute-done((f16[32,512]{1,0:T(8,128)(2,1)S(1)}, f16[32,512]{1,0:T(8,128)(2,1)S(1)}, u32[]{:S(2)}, u32[]{:S(2)}) %collective-permute-start.13) | collective-permute-done | bytes 32800 | tf_op jit(solution)/shard_map/ppermute | solution.py:360
  54.6 1.4 %collective-permute-start.15 = (f16[32,512]{1,0:T(8,128)(2,1)S(1)}, f16[32,512]{1,0:T(8,128)(2,1)S(1)}, u32[]{:S(2)}, u32[]{:S(2)}) collective-permute-start(f16[32,512]{1,0:T(8,128)(2,1)S(1)} %fusion), channel_id=1, source_target_pairs={{0,4},{1,5},{2,6},{3,7},{4,0},{5,1},{6,2},{7,3},{8,12},{9,13},{10,... | collective-permute-start | bytes 98312 | tf_op jit(solution)/shard_map/ppermute | solution.py:360
  56.1 1.5 %collective-permute-done.11 = f16[128,512]{1,0:T(8,128)(2,1)S(1)} collective-permute-done((f16[128,512]{1,0:T(8,128)(2,1)S(1)}, f16[128,512]{1,0:T(8,128)(2,1)S(1)}, u32[]{:S(2)}, u32[]{:S(2)}) %collective-permute-start.11) | collective-permute-done | bytes 131104 | tf_op jit(solution)/shard_map/ppermute | solution.py:360
  57.7 0.9 %collective-permute-done.15 = f16[32,512]{1,0:T(8,128)(2,1)S(1)} collective-permute-done((f16[32,512]{1,0:T(8,128)(2,1)S(1)}, f16[32,512]{1,0:T(8,128)(2,1)S(1)}, u32[]{:S(2)}, u32[]{:S(2)}) %collective-permute-start.15) | collective-permute-done | bytes 32800 | tf_op jit(solution)/shard_map/ppermute | solution.py:360
  58.6 0.9 %collective-permute-start.16 = (f16[32,512]{1,0:T(8,128)(2,1)S(1)}, f16[32,512]{1,0:T(8,128)(2,1)S(1)}, u32[]{:S(2)}, u32[]{:S(2)}) collective-permute-start(f16[32,512]{1,0:T(8,128)(2,1)S(1)} %add_convert_fusion), channel_id=1, source_target_pairs={{0,8},{1,9},{2,10},{3,11},{4,12},{5,13},{6,14},{7,15},{8,0},{9,1},... | collective-permute-start | bytes 98312 | tf_op jit(solution)/shard_map/ppermute | solution.py:360
  59.7 1.6 %shard_map.93 = f32[512,512]{1,0:T(8,128)} custom-call(s32[4]{0:T(128)S(1)} %pad_add_fusion.refs_0_, f32[128,512]{1,0:T(8,128)S(1)} %get-tuple-element.72.refs_1_, f32[128,512]{1,0:T(8,128)S(1)} %convert_element_type.68.refs_2_, f32[256,512]{1,0:T(8,128)S(1)} %convert_element_type.69.refs_3_), custom_call_target="tpu_custom_call" | custom-call | flops 1048576 | bytes 2097152 | tf_op jit(solution)/shard_map/pallas_call | solution.py:335
  61.3 2.3 %collective-permute-done.16 = f16[32,512]{1,0:T(8,128)(2,1)S(1)} collective-permute-done((f16[32,512]{1,0:T(8,128)(2,1)S(1)}, f16[32,512]{1,0:T(8,128)(2,1)S(1)}, u32[]{:S(2)}, u32[]{:S(2)}) %collective-permute-start.16) | collective-permute-done | bytes 32800 | tf_op jit(solution)/shard_map/ppermute | solution.py:360
  63.6 1.2 %collective-permute-done.17 = f32[32,512]{1,0:T(8,128)S(1)} collective-permute-done((f32[32,512]{1,0:T(8,128)S(1)}, f32[32,512]{1,0:T(8,128)S(1)}, u32[]{:S(2)}, u32[]{:S(2)}) %collective-permute-start.17) | collective-permute-done | bytes 65568 | tf_op jit(solution)/shard_map/ppermute | solution.py:360
  64.9 0.7 %maximum_bitcast_fusion = f32[512,64]{0,1:T(8,128)} fusion(f32[32,512]{1,0:T(8,128)S(1)} %get-tuple-element.77, f32[32,512]{1,0:T(8,128)S(1)} %get-tuple-element.76), kind=kLoop, calls=%fused_computation.4 | loop fusion | flops 32768 | bytes 262144 | tf_op jit(solution)/shard_map/transpose | solution.py:430
  (34 shorter events, 1.5 us)
Async XLA Ops:
  0.6 9.4 %copy-start.2 = (s32[512,40]{0,1:T(8,128)S(1)}, s32[512,40]{0,1:T(8,128)}, u32[]{:S(2)}) copy-start(s32[512,40]{0,1:T(8,128)} %param.13) | copy-start | bytes 245764
  2.6 7.5 %copy-start = (bf16[144,1024]{1,0:T(8,128)(2,1)S(1)}, bf16[144,1024]{1,0:T(8,128)(2,1)}, u32[]{:S(2)}) copy-start(bf16[144,1024]{1,0:T(8,128)(2,1)} %get-tuple-element.37.scens) | copy-start | bytes 884740
  2.7 7.5 %collective-permute-start.1 = (bf16[80,1024]{1,0:T(8,128)(2,1)}, bf16[80,1024]{1,0:T(8,128)(2,1)S(1)}, u32[]{:S(2)}, u32[]{:S(2)}) collective-permute-start(bf16[80,1024]{1,0:T(8,128)(2,1)} %get-tuple-element.38.p0.refs_1_), channel_id=1, source_target_pairs={{0,1},{1,0},{2,3},{3,2},{4,5},{5,4},{6,7},{7,6},{8,9},{9,8},{10,11... | collective-permute-start | bytes 491528 | tf_op jit(solution)/shard_map/ppermute | solution.py:360
  3.2 21.6 %collective-permute-start.4 = (bf16[80,1024]{1,0:T(8,128)(2,1)}, bf16[80,1024]{1,0:T(8,128)(2,1)S(1)}, u32[]{:S(2)}, u32[]{:S(2)}) collective-permute-start(bf16[80,1024]{1,0:T(8,128)(2,1)} %get-tuple-element.38.p0.refs_1_), channel_id=1, source_target_pairs={{0,4},{1,5},{2,6},{3,7},{4,0},{5,1},{6,2},{7,3},{8,12},{9,13},{10,... | collective-permute-start | bytes 491528 | tf_op jit(solution)/shard_map/ppermute | solution.py:360
  5.8 18.4 %collective-permute-start.7 = (bf16[80,1024]{1,0:T(8,128)(2,1)}, bf16[80,1024]{1,0:T(8,128)(2,1)S(1)}, u32[]{:S(2)}, u32[]{:S(2)}) collective-permute-start(bf16[80,1024]{1,0:T(8,128)(2,1)} %get-tuple-element.38.p0.refs_1_), channel_id=1, source_target_pairs={{0,8},{1,9},{2,10},{3,11},{4,12},{5,13},{6,14},{7,15},{8,0},{9,1},... | collective-permute-start | bytes 491528 | tf_op jit(solution)/shard_map/ppermute | solution.py:360
  8.4 9.0 %collective-permute-start = (bf16[144,1024]{1,0:T(8,128)(2,1)}, bf16[144,1024]{1,0:T(8,128)(2,1)S(1)}, u32[]{:S(2)}, u32[]{:S(2)}) collective-permute-start(bf16[144,1024]{1,0:T(8,128)(2,1)} %get-tuple-element.37.scens), channel_id=1, source_target_pairs={{0,2},{1,3},{2,0},{3,1},{4,6},{5,7},{6,4},{7,5},{8,10},{9,11},{10,... | collective-permute-start | bytes 884744 | tf_op jit(solution)/shard_map/ppermute | solution.py:360
  10.2 0.9 %copy-start.1 = (bf16[80,1024]{1,0:T(8,128)(2,1)S(1)}, bf16[80,1024]{1,0:T(8,128)(2,1)}, u32[]{:S(2)}) copy-start(bf16[80,1024]{1,0:T(8,128)(2,1)} %get-tuple-element.38.p0.refs_1_) | copy-start | bytes 491524
  21.0 4.9 %collective-permute-start.2 = (f32[128,512]{1,0:T(8,128)S(1)}, f32[128,512]{1,0:T(8,128)S(1)}, u32[]{:S(2)}, u32[]{:S(2)}) collective-permute-start(f32[128,512]{1,0:T(8,128)S(1)} %get-tuple-element.43), channel_id=1, source_target_pairs={{0,1},{1,0},{2,3},{3,2},{4,5},{5,4},{6,7},{7,6},{8,9},{9,8},{10,11... | collective-permute-start | bytes 786440 | tf_op jit(solution)/shard_map/ppermute | solution.py:360
  24.2 1.6 %collective-permute-start.8 = (bf16[80,1024]{1,0:T(8,128)(2,1)S(1)}, bf16[80,1024]{1,0:T(8,128)(2,1)S(1)}, u32[]{:S(2)}, u32[]{:S(2)}) collective-permute-start(bf16[80,1024]{1,0:T(8,128)(2,1)S(1)} %collective-permute-done.7.refs_2_), channel_id=1, source_target_pairs={{0,1},{1,0},{2,3},{3,2},{4,5},{5,4},{6,7},{7,6},{8,9},{9,8},{10,11... | collective-permute-start | bytes 491528 | tf_op jit(solution)/shard_map/ppermute | solution.py:360
  24.8 16.0 %collective-permute-start.9 = (bf16[80,1024]{1,0:T(8,128)(2,1)S(1)}, bf16[80,1024]{1,0:T(8,128)(2,1)S(1)}, u32[]{:S(2)}, u32[]{:S(2)}) collective-permute-start(bf16[80,1024]{1,0:T(8,128)(2,1)S(1)} %collective-permute-done.4.refs_2_), channel_id=1, source_target_pairs={{0,8},{1,9},{2,10},{3,11},{4,12},{5,13},{6,14},{7,15},{8,0},{9,1},... | collective-permute-start | bytes 491528 | tf_op jit(solution)/shard_map/ppermute | solution.py:360
  25.1 1.4 %collective-permute-start.5 = (bf16[80,1024]{1,0:T(8,128)(2,1)S(1)}, bf16[80,1024]{1,0:T(8,128)(2,1)S(1)}, u32[]{:S(2)}, u32[]{:S(2)}) collective-permute-start(bf16[80,1024]{1,0:T(8,128)(2,1)S(1)} %collective-permute-done.4.refs_2_), channel_id=1, source_target_pairs={{0,1},{1,0},{2,3},{3,2},{4,5},{5,4},{6,7},{7,6},{8,9},{9,8},{10,11... | collective-permute-start | bytes 491528 | tf_op jit(solution)/shard_map/ppermute | solution.py:360
  25.9 6.6 %collective-permute-start.3 = (f16[128,512]{1,0:T(8,128)(2,1)S(1)}, f16[128,512]{1,0:T(8,128)(2,1)S(1)}, u32[]{:S(2)}, u32[]{:S(2)}) collective-permute-start(f16[128,512]{1,0:T(8,128)(2,1)S(1)} %fusion.3), channel_id=1, source_target_pairs={{0,4},{1,5},{2,6},{3,7},{4,0},{5,1},{6,2},{7,3},{8,12},{9,13},{10,... | collective-permute-start | bytes 393224 | tf_op jit(solution)/shard_map/ppermute | solution.py:360
  32.5 9.1 %collective-permute-start.6 = (f16[128,512]{1,0:T(8,128)(2,1)S(1)}, f16[128,512]{1,0:T(8,128)(2,1)S(1)}, u32[]{:S(2)}, u32[]{:S(2)}) collective-permute-start(f16[128,512]{1,0:T(8,128)(2,1)S(1)} %fusion.1), channel_id=1, source_target_pairs={{0,8},{1,9},{2,10},{3,11},{4,12},{5,13},{6,14},{7,15},{8,0},{9,1},... | collective-permute-start | bytes 393224 | tf_op jit(solution)/shard_map/ppermute | solution.py:360
  40.8 1.5 %collective-permute-start.10 = (bf16[80,1024]{1,0:T(8,128)(2,1)S(1)}, bf16[80,1024]{1,0:T(8,128)(2,1)S(1)}, u32[]{:S(2)}, u32[]{:S(2)}) collective-permute-start(bf16[80,1024]{1,0:T(8,128)(2,1)S(1)} %collective-permute-done.9.refs_2_), channel_id=1, source_target_pairs={{0,1},{1,0},{2,3},{3,2},{4,5},{5,4},{6,7},{7,6},{8,9},{9,8},{10,11... | collective-permute-start | bytes 491528 | tf_op jit(solution)/shard_map/ppermute | solution.py:360
  49.3 1.3 %collective-permute-start.12 = (f32[32,512]{1,0:T(8,128)S(1)}, f32[32,512]{1,0:T(8,128)S(1)}, u32[]{:S(2)}, u32[]{:S(2)}) collective-permute-start(f32[32,512]{1,0:T(8,128)S(1)} %get-tuple-element.69), channel_id=1, source_target_pairs={{0,1},{1,0},{2,3},{3,2},{4,5},{5,4},{6,7},{7,6},{8,9},{9,8},{10,11... | collective-permute-start | bytes 196616 | tf_op jit(solution)/shard_map/ppermute | solution.py:360
  50.6 4.0 %collective-permute-start.13 = (f16[32,512]{1,0:T(8,128)(2,1)S(1)}, f16[32,512]{1,0:T(8,128)(2,1)S(1)}, u32[]{:S(2)}, u32[]{:S(2)}) collective-permute-start(f16[32,512]{1,0:T(8,128)(2,1)S(1)} %add_convert_fusion.1), channel_id=1, source_target_pairs={{0,2},{1,3},{2,0},{3,1},{4,6},{5,7},{6,4},{7,5},{8,10},{9,11},{10,... | collective-permute-start | bytes 98312 | tf_op jit(solution)/shard_map/ppermute | solution.py:360
  52.3 5.3 %collective-permute-start.11 = (f16[128,512]{1,0:T(8,128)(2,1)S(1)}, f16[128,512]{1,0:T(8,128)(2,1)S(1)}, u32[]{:S(2)}, u32[]{:S(2)}) collective-permute-start(f16[128,512]{1,0:T(8,128)(2,1)S(1)} %get-tuple-element.73), channel_id=1, source_target_pairs={{0,2},{1,3},{2,0},{3,1},{4,6},{5,7},{6,4},{7,5},{8,10},{9,11},{10,... | collective-permute-start | bytes 393224 | tf_op jit(solution)/shard_map/ppermute | solution.py:360
  54.6 4.0 %collective-permute-start.15 = (f16[32,512]{1,0:T(8,128)(2,1)S(1)}, f16[32,512]{1,0:T(8,128)(2,1)S(1)}, u32[]{:S(2)}, u32[]{:S(2)}) collective-permute-start(f16[32,512]{1,0:T(8,128)(2,1)S(1)} %fusion), channel_id=1, source_target_pairs={{0,4},{1,5},{2,6},{3,7},{4,0},{5,1},{6,2},{7,3},{8,12},{9,13},{10,... | collective-permute-start | bytes 98312 | tf_op jit(solution)/shard_map/ppermute | solution.py:360
  57.7 1.9 %collective-permute-start.14 = (f16[256,512]{1,0:T(8,128)(2,1)S(1)}, f16[256,512]{1,0:T(8,128)(2,1)S(1)}, u32[]{:S(2)}, u32[]{:S(2)}) collective-permute-start(f16[256,512]{1,0:T(8,128)(2,1)S(1)} %pad_maximum_fusion), channel_id=1, source_target_pairs={{0,1},{1,0},{2,3},{3,2},{4,5},{5,4},{6,7},{7,6},{8,9},{9,8},{10,11... | collective-permute-start | bytes 786440 | tf_op jit(solution)/shard_map/ppermute | solution.py:360
  58.6 4.9 %collective-permute-start.16 = (f16[32,512]{1,0:T(8,128)(2,1)S(1)}, f16[32,512]{1,0:T(8,128)(2,1)S(1)}, u32[]{:S(2)}, u32[]{:S(2)}) collective-permute-start(f16[32,512]{1,0:T(8,128)(2,1)S(1)} %add_convert_fusion), channel_id=1, source_target_pairs={{0,8},{1,9},{2,10},{3,11},{4,12},{5,13},{6,14},{7,15},{8,0},{9,1},... | collective-permute-start | bytes 98312 | tf_op jit(solution)/shard_map/ppermute | solution.py:360
  63.5 1.3 %collective-permute-start.17 = (f32[32,512]{1,0:T(8,128)S(1)}, f32[32,512]{1,0:T(8,128)S(1)}, u32[]{:S(2)}, u32[]{:S(2)}) collective-permute-start(f32[32,512]{1,0:T(8,128)S(1)} %convert_add_fusion.2), channel_id=1, source_target_pairs={{0,1},{1,0},{2,3},{3,2},{4,5},{5,4},{6,7},{7,6},{8,9},{9,8},{10,11... | collective-permute-start | bytes 196616 | tf_op jit(solution)/shard_map/ppermute | solution.py:360

commit v5 on v4

--- a/solution.py
+++ b/solution.py
@@ -105,21 +105,20 @@
 def value_kernel(blocks, count, earlier, scale, *refs):
     rts, refs = refs[:blocks], refs[blocks:]
     packs, refs = refs[:count], refs[count:]
-    sources = list(rts)
+    before, refs = refs[:earlier], refs[earlier:]
+    sources = [*rts, *before]
     if scale:
-        before, refs = refs[: len(earlier)], refs[len(earlier) :]
         basis, refs = refs[: 2 * blocks], refs[2 * blocks :]
-        core, keep, send, w, oh, lev, sems, *held = refs
-        whole, held = held[0], held[1:]
-        sources += [*before, *basis]
+        out, w, oh, lev, sems, *held = refs
+        sources += basis
     else:
-        outs, (w, oh, lev, sems, *held) = refs[:blocks], refs[blocks:]
-        sums, held = held[:blocks], held[blocks:]
+        out, w, oh, lev, sems, sums, *held = refs
     loads = [pltpu.make_async_copy(a, b, sems.at[i]) for i, (a, b) in enumerate(zip(sources, held))]
     for load in loads:
         load.start()
-    own, double = rts[0].shape
+    own = rts[0].shape[0]
     points = packs[0].shape[1]
+    lines = oh.shape[0]
     prepare(packs, w, oh, lev)
     for load in loads[:blocks]:
         load.wait()
@@ -130,25 +129,20 @@
         ]
         for i in range(blocks)
     ]
-    if not scale:
-        stores = []
-        for i in range(blocks):
-            sums[i][...] = jnp.concatenate(totals[i], axis=0)
-            stores.append(pltpu.make_async_copy(sums[i], outs[i], sems.at[len(sources) + i]))
-            stores[-1].start()
-        for store in stores:
-            store.wait()
-        return
     for load in loads[blocks:]:
         load.wait()
-    before, basis = held[blocks : blocks + len(before)], held[blocks + len(before) :]
-    lines = oh.shape[0]
+    before, basis = held[blocks : blocks + earlier], held[blocks + earlier :]
+    totals = [jnp.concatenate(t, axis=0) for t in totals]
+    if not scale:
+        sums[:, :lines] = totals[0] + before[0][:, :lines]
+        sums[:, lines:] = totals[1] + before[-1][:, -lines:]
+        store = pltpu.make_async_copy(sums, out, sems.at[len(sources)])
+        store.start()
+        store.wait()
+        return
     result = None
     for i in range(blocks):
-        v = jnp.concatenate(totals[i], axis=0)
-        for k, at in enumerate(earlier):
-            if at == i:
-                v = v + before[k][...]
+        v = totals[i] + before[0][:, i * lines : (i + 1) * lines]
         vh = v.astype(BF)
         vl = (v - vh.astype(F32)).astype(BF)
         both = jnp.concatenate([vh, vl], axis=1)
@@ -156,10 +150,22 @@
         b = jnp.dot(basis[2 * i + 1][...], vh, preferred_element_type=F32)
         part = a[:, :lines] + a[:, lines:] + b
         result = part if result is None else result + part
-    whole[...] = (result * scale).T
-    half = lines // 2
-    keep[...] = whole[pl.ds(pl.multiple_of(core[0] * half, half), half), :]
-    send[...] = whole[pl.ds(pl.multiple_of((1 - core[0]) * half, half), half), :]
+    out[...] = (result * scale).T
+
+
+def plain_kernel(rt, *refs):
+    packs, (out, w, oh, lev, sems, sums, held) = refs[:-7], refs[-7:]
+    load = pltpu.make_async_copy(rt, held, sems.at[0])
+    load.start()
+    prepare(packs, w, oh, lev)
+    load.wait()
+    for s0 in range(0, rt.shape[0], CHUNK):
+        sums[s0 : s0 + CHUNK, :] = chunk_values(
+            held[s0 : s0 + CHUNK, :], w, oh, lev, packs[0].shape[1]
+        )
+    store = pltpu.make_async_copy(sums, out, sems.at[1])
+    store.start()
+    store.wait()
 
 
 VSPEC = pl.BlockSpec(memory_space=pltpu.VMEM)
@@ -179,37 +185,36 @@
     ]
 
 
-def values_of(rts, packs, lines, before=(), basis=(), scale=None, core=None):
+def values_of(rts, packs, lines, before=(), basis=(), scale=None):
     own, double = rts[0].shape
     points = packs[0].shape[1]
     pairs = own * points * len(rts) * len(packs)
-    held = [*rts, *[v for _, v in before], *basis]
+    held = [*rts, *before, *basis]
     scratch = point_scratch(double, lines, points * len(packs))
-    scratch.append(pltpu.SemaphoreType.DMA((len(held) + len(rts),)))
-    specs = [HSPEC] * len(rts) + [VSPEC] * len(packs)
+    scratch.append(pltpu.SemaphoreType.DMA((len(held) + 1,)))
+    kernel = functools.partial(value_kernel, len(rts), len(packs), len(before), scale)
+    out = HSPEC
     if scale:
-        terms = basis[0].shape[0]
-        specs += [HSPEC] * (len(before) + len(basis)) + [SSPEC]
-        scratch.append(pltpu.VMEM((lines, terms), F32))
-        shape = [jax.ShapeDtypeStruct((lines // 2, terms), F32)] * 2
-        outs = [VSPEC] * 2
-        basis = [*basis, core]
+        shape = jax.ShapeDtypeStruct((lines, basis[0].shape[0]), F32)
+        out = VSPEC
     else:
-        shape = [jax.ShapeDtypeStruct((own, lines), F32)] * len(rts)
-        outs = [HSPEC] * len(rts)
-        scratch += like(shape)
-    kernel = functools.partial(value_kernel, len(rts), len(packs), [i for i, _ in before], scale)
+        shape = jax.ShapeDtypeStruct((own, lines * len(rts)), F32)
+        scratch += like([shape])
+    if not before:
+        kernel = plain_kernel
     return pl.pallas_call(
         kernel,
-        in_specs=specs,
-        out_specs=outs,
+        in_specs=[HSPEC] * len(rts)
+        + [VSPEC] * len(packs)
+        + [HSPEC] * (len(before) + len(basis)),
+        out_specs=out,
         out_shape=shape,
         scratch_shapes=scratch + like(held),
         compiler_params=params(),
         cost_estimate=pl.CostEstimate(
             flops=1700 * pairs, bytes_accessed=2**20, transcendentals=pairs
         ),
-    )(*rts, *packs, *[v for _, v in before], *basis)
+    )(*rts, *packs, *before, *basis)
 
 
 def picks_of(exps):
@@ -369,7 +374,7 @@
     packs = {m: swap(pack, m) for m in deep}
 
     high0, low0, rt0, v = basis_of(exponents, scens0, near, lines)
-    before = [(0, v)]
+    before = [v]
     packs[4] = after(packs[4], v)
     for m in far:
         top = max(h for h in deep if h <= m)
@@ -382,8 +387,8 @@
         exponents, after(scens1, v), start=start, first=high0
     )
     more = swap(send, 1)
-    (v,) = values_of([rt1], near, lines)
-    before.append((1, v))
+    v = values_of([rt1], near, lines)
+    before.append(v)
     keep, more = after((keep, more), v)
     gram = (keep + more) * (1.0 / scen_total)
 
@@ -396,8 +401,8 @@
             other = swap(mine, steps.pop(0))
         if m == far[-1]:
             break
-        v0, v1 = values_of(rts, after(pair, gram), lines)
-        before += [(0, v0), (1, v1)]
+        v0 = values_of(rts, after(pair, gram), lines, before)
+        before = [v0]
         if i > 0:
             v = v0
         if other is not None:
@@ -406,13 +411,9 @@
         else:
             gram = after(gram, v0)
     basis = (high0, low0, high1, low1)
-    keep, send = values_of(
-        rts, after(pair, gram), lines, before, basis, scale, core.reshape(1)
-    )
-
-    a = after(gram, keep).astype(HALF)
-    b = swap(a, 2)
-    rhs = keep + swap(send, 1)
+    rhs = values_of(rts, after(pair, gram), lines, before, basis, scale)
+
+    rhs = rhs + swap(rhs, 1)
     for m in [2] + deep:
         mine = rhs.astype(HALF)
         other = swap(mine, m)
@@ -423,11 +424,9 @@
             other = after(other, gram)
         rhs = mine.astype(F32) + other.astype(F32)
         if m == 2:
-            b = after(b, rhs)
-    other = swap(rhs, 1)
-    first = jnp.where(core == 0, rhs, other)
-    second = jnp.where(core == 0, other, rhs)
-    return (gram, jnp.concatenate([first, second], axis=0).T)
+            a = after(gram, rhs).astype(HALF)
+            b = swap(a, 2)
+    return (gram, rhs.T)
 
 
 def solution(mesh):

time: 65.7 us -> 65.5 us (level)
  waiting for transfers between devices: 12.4 us -> 13.5 us
  Pallas kernels: 33.6 us -> 32.6 us
    ppermute x18 -> x17, waiting for transfers between devices: 12.4 us -> 13.5 us  [swap(): return lax.ppermute(x, 'scen', [(i, i ^ mask) for i in range(n)])]
    pallas_call x4, Pallas kernels: 21.4 us -> 20.3 us  [values_of(): pl.pallas_call(kernel, in_specs=[HSPEC] * len(rts) + [VSPEC] * len(packs)...]
    ppermute x18 -> x17, starting transfers between devices: 16.4 us -> 16.2 us  [swap(): return lax.ppermute(x, 'scen', [(i, i ^ mask) for i in range(n)])]
  transfers between devices with their start and end apart: 18 -> 17, of which waited for: 12 -> 11; matrix products, arithmetic and copies ran while one was open for 1% -> 1% of each run, Pallas kernels for 38% -> 36%
where the time goes in v5:
time: 65.5 us; the launch traced here: 65.3 us
  Pallas kernels  32.6 us (50%)
  starting transfers between devices  16.2 us (25%)
  waiting for transfers between devices  13.5 us (21%)
  other arithmetic  1.18 us (2%)
  local copies, waits for them, and re-layouts  1.04 us (2%)
  between operations  0.85 us (1%)
    pallas_call x4, Pallas kernels, values_of(): pl.pallas_call(kernel, in_specs=[HSPEC] * len(rts) + [VSPEC] * len(packs)...  20.3 us
    ppermute x17, starting transfers between devices, swap(): return lax.ppermute(x, 'scen', [(i, i ^ mask) for i in range(n)])  16.2 us
    ppermute x17, waiting for transfers between devices, swap(): return lax.ppermute(x, 'scen', [(i, i ^ mask) for i in range(n)])  13.5 us
    pallas_call x1, Pallas kernels, basis_of(): pl.pallas_call(first_kernel, in_specs=[VSPEC] * 2 + [HSPEC] * 2, out_spec...  5.18 us
    pallas_call x1, Pallas kernels, basis_of(): pl.pallas_call(gram_kernel, in_specs=[SSPEC, VSPEC, VSPEC, HSPEC], out_sp...  3.53 us
    pallas_call x1, Pallas kernels, packs_of(): pl.pallas_call(pack_kernel, in_specs=[pl.BlockSpec(memory_space=pltpu.HBM...  1.99 us
    pallas_call x1, Pallas kernels, placed(): pl.pallas_call(functools.partial(place_kernel, blocks), in_specs=[pl.Bloc...  1.59 us
  transfers between devices with their start and end apart: 17, of which 11 were waited for; matrix products, arithmetic and copies ran while one was open for 1% of the time, Pallas kernels for 36%

profile of v5, /device:TPU:0, one launch (start us, length us, event | category | flops | bytes accessed | tf_op | source)
XLA Modules:
  0.0 65.3 jit_solution(8797511993176600214)
XLA Ops:
  0.6 2.0 %shard_map.86 = (bf16[80,1024]{1,0:T(8,128)(2,1)}, bf16[144,1024]{1,0:T(8,128)(2,1)}) custom-call(bf16[64,1024]{1,0:T(8,128)(2,1)} %bitcast.10, f32[1,1024]{1,0:T(1,128)} %bitcast.11, s32[1,1024]{1,0:T(1,128)} %bitcast.12, s32[1,1024]{1,0:T(1,128)} %bitcast.13, bf16[64,1024]{1,0:T(8,128)(2,1)} %refs_4_.1, f32[40,1024]{1,0:T(8,128)} %refs_5_.1), custom_call_target="tpu_custom_call" | custom-call | flops 1048576 | bytes 1048576 | tf_op jit(solution)/shard_map/pallas_call | solution.py:63
  2.7 0.5 collective-permute-start.1
  3.2 2.6 %collective-permute-start.4 = (bf16[80,1024]{1,0:T(8,128)(2,1)}, bf16[80,1024]{1,0:T(8,128)(2,1)S(1)}, u32[]{:S(2)}, u32[]{:S(2)}) collective-permute-start(bf16[80,1024]{1,0:T(8,128)(2,1)} %get-tuple-element.31.p0.refs_0_), channel_id=1, source_target_pairs={{0,4},{1,5},{2,6},{3,7},{4,0},{5,1},{6,2},{7,3},{8,12},{9,13},{10,... | collective-permute-start | bytes 491528 | tf_op jit(solution)/shard_map/ppermute | solution.py:365
  5.8 2.6 %collective-permute-start.7 = (bf16[80,1024]{1,0:T(8,128)(2,1)}, bf16[80,1024]{1,0:T(8,128)(2,1)S(1)}, u32[]{:S(2)}, u32[]{:S(2)}) collective-permute-start(bf16[80,1024]{1,0:T(8,128)(2,1)} %get-tuple-element.31.p0.refs_0_), channel_id=1, source_target_pairs={{0,8},{1,9},{2,10},{3,11},{4,12},{5,13},{6,14},{7,15},{8,0},{9,1},... | collective-permute-start | bytes 491528 | tf_op jit(solution)/shard_map/ppermute | solution.py:365
  8.4 1.5 %collective-permute-start = (bf16[144,1024]{1,0:T(8,128)(2,1)}, bf16[144,1024]{1,0:T(8,128)(2,1)S(1)}, u32[]{:S(2)}, u32[]{:S(2)}) collective-permute-start(bf16[144,1024]{1,0:T(8,128)(2,1)} %get-tuple-element.30.scens), channel_id=1, source_target_pairs={{0,2},{1,3},{2,0},{3,1},{4,6},{5,7},{6,4},{7,5},{8,10},{9,11},{10,... | collective-permute-start | bytes 884744 | tf_op jit(solution)/shard_map/ppermute | solution.py:365
  10.2 0.9 %copy-done.1 = bf16[80,1024]{1,0:T(8,128)(2,1)S(1)} copy-done((bf16[80,1024]{1,0:T(8,128)(2,1)S(1)}, bf16[80,1024]{1,0:T(8,128)(2,1)}, u32[]{:S(2)}) %copy-start.1) | copy-done | bytes 163864
  11.1 5.2 %shard_map.87 = (bf16[512,1024]{1,0:T(8,128)(2,1)S(1)}, bf16[512,1024]{1,0:T(8,128)(2,1)S(1)}, bf16[1024,128]{1,0:T(8,128)(2,1)S(1)}, f32[1024,64]{1,0:T(8,128)S(1)}) custom-call(s32[512,40]{1,0:T(8,128)S(1)} %copy.10.exps, bf16[144,1024]{1,0:T(8,128)(2,1)S(1)} %copy-done, bf16[80,1024]{1,0:T(8,128)(2,1)S(1)} %copy-done.1, ...), custom_call_target="tpu_custom_call" | custom-call | flops 3000000000 | bytes 3145728 | tf_op jit(solution)/shard_map/pallas_call | solution.py:304
  16.3 1.2 %collective-permute-done.scens = bf16[144,1024]{1,0:T(8,128)(2,1)S(1)} collective-permute-done((bf16[144,1024]{1,0:T(8,128)(2,1)}, bf16[144,1024]{1,0:T(8,128)(2,1)S(1)}, u32[]{:S(2)}, u32[]{:S(2)}) %collective-permute-start) | collective-permute-done | bytes 294944 | tf_op jit(solution)/shard_map/ppermute | solution.py:365
  17.4 3.5 %shard_map.88 = (bf16[512,1024]{1,0:T(8,128)(2,1)S(1)}, bf16[512,1024]{1,0:T(8,128)(2,1)S(1)}, bf16[1024,128]{1,0:T(8,128)(2,1)S(1)}, f32[128,512]{1,0:T(8,128)S(1)}, f32[128,512]{1,0:T(8,128)S(1)}) custom-call(s32[2]{0:T(128)S(1)} %pad_add_fusion.1.start, s32[512,40]{1,0:T(8,128)S(1)} %copy.10.exps, bf16[144,1024]{1,0:T(8,128)(2,1)S(1)} %collective-permute-done.scens, ...), custom_call_target="tpu_custom_call" | custom-call | flops 3000000000 | bytes 3145728 | tf_op jit(solution)/shard_map/pallas_call | solution.py:317
  21.0 3.2 %shard_map.89.refs_5_ = f32[1024,64]{1,0:T(8,128)S(1)} custom-call(bf16[1024,128]{1,0:T(8,128)(2,1)S(1)} %get-tuple-element.37.rt.refs_1_, bf16[80,1024]{1,0:T(8,128)(2,1)S(1)} %copy-done.1, bf16[80,1024]{1,0:T(8,128)(2,1)S(1)} %collective-permute-done.1.p1.refs_1_), custom_call_target="tpu_custom_call" | custom-call | flops 3565158400 | bytes 1048576 | tf_op jit(solution)/shard_map/pallas_call | solution.py:205
  24.2 0.6 collective-permute-start.8
  24.8 0.3 collective-permute-start.9
  25.1 0.7 %collective-permute-done.8.refs_3_ = bf16[80,1024]{1,0:T(8,128)(2,1)S(1)} collective-permute-done((bf16[80,1024]{1,0:T(8,128)(2,1)S(1)}, bf16[80,1024]{1,0:T(8,128)(2,1)S(1)}, u32[]{:S(2)}, u32[]{:S(2)}) %collective-permute-start.8) | collective-permute-done | bytes 163872 | tf_op jit(solution)/shard_map/ppermute | solution.py:365
  25.9 0.6 collective-permute-done.5.refs_3_
  26.5 0.4 collective-permute-start.3
  26.9 5.2 %shard_map.90.refs_4_ = f32[1024,128]{1,0:T(8,128)S(1)} custom-call(bf16[1024,128]{1,0:T(8,128)(2,1)S(1)} %get-tuple-element.40.refs_0_, bf16[1024,128]{1,0:T(8,128)(2,1)S(1)} %get-tuple-element.37.rt.refs_1_, bf16[80,1024]{1,0:T(8,128)(2,1)S(1)} %collective-permute-done.4.refs_2_, bf16[80,1024]{1,0:T(8,128)(2,1)S(1)} %collective-permute-done.5.refs_3_, ...), custom_call_target="tpu_custom_call" | custom-call | flops 7130316800 | bytes 1048576 | tf_op jit(solution)/shard_map/pallas_call | solution.py:205
  32.1 3.4 %collective-permute-done.3 = f16[128,512]{1,0:T(8,128)(2,1)S(1)} collective-permute-done((f16[128,512]{1,0:T(8,128)(2,1)S(1)}, f16[128,512]{1,0:T(8,128)(2,1)S(1)}, u32[]{:S(2)}, u32[]{:S(2)}) %collective-permute-start.3) | collective-permute-done | bytes 131104 | tf_op jit(solution)/shard_map/ppermute | solution.py:365
  35.6 5.1 %shard_map.91.refs_4_ = f32[1024,128]{1,0:T(8,128)S(1)} custom-call(bf16[1024,128]{1,0:T(8,128)(2,1)S(1)} %get-tuple-element.40.refs_0_, bf16[1024,128]{1,0:T(8,128)(2,1)S(1)} %get-tuple-element.37.rt.refs_1_, bf16[80,1024]{1,0:T(8,128)(2,1)S(1)} %collective-permute-done.7.refs_2_, bf16[80,1024]{1,0:T(8,128)(2,1)S(1)} %collective-permute-done.8.refs_3_, ...), custom_call_target="tpu_custom_call" | custom-call | flops 7130316800 | bytes 1048576 | tf_op jit(solution)/shard_map/pallas_call | solution.py:205
  40.8 0.6 collective-permute-done.6
  41.5 0.7 %collective-permute-done.10.refs_3_ = bf16[80,1024]{1,0:T(8,128)(2,1)S(1)} collective-permute-done((bf16[80,1024]{1,0:T(8,128)(2,1)S(1)}, bf16[80,1024]{1,0:T(8,128)(2,1)S(1)}, u32[]{:S(2)}, u32[]{:S(2)}) %collective-permute-start.10) | collective-permute-done | bytes 163872 | tf_op jit(solution)/shard_map/ppermute | solution.py:365
  42.2 6.8 %shard_map.92 = f32[64,512]{1,0:T(8,128)S(1)} custom-call(bf16[1024,128]{1,0:T(8,128)(2,1)S(1)} %get-tuple-element.40.refs_0_, bf16[1024,128]{1,0:T(8,128)(2,1)S(1)} %get-tuple-element.37.rt.refs_1_, bf16[80,1024]{1,0:T(8,128)(2,1)S(1)} %collective-permute-done.9.refs_2_, bf16[80,1024]{1,0:T(8,128)(2,1)S(1)} %collective-permute-done.10.refs_3_, ...), custom_call_target="tpu_custom_call" | custom-call | flops 7130316800 | bytes 1048576 | tf_op jit(solution)/shard_map/pallas_call | solution.py:205
  49.2 1.2 %collective-permute-done.11 = f32[64,512]{1,0:T(8,128)S(1)} collective-permute-done((f32[64,512]{1,0:T(8,128)S(1)}, f32[64,512]{1,0:T(8,128)S(1)}, u32[]{:S(2)}, u32[]{:S(2)}) %collective-permute-start.11) | collective-permute-done | bytes 131104 | tf_op jit(solution)/shard_map/ppermute | solution.py:365
  50.4 1.6 %collective-permute-start.12 = (f16[64,512]{1,0:T(8,128)(2,1)S(1)}, f16[64,512]{1,0:T(8,128)(2,1)S(1)}, u32[]{:S(2)}, u32[]{:S(2)}) collective-permute-start(f16[64,512]{1,0:T(8,128)(2,1)S(1)} %add_convert_fusion.1), channel_id=1, source_target_pairs={{0,2},{1,3},{2,0},{3,1},{4,6},{5,7},{6,4},{7,5},{8,10},{9,11},{10,... | collective-permute-start | bytes 196616 | tf_op jit(solution)/shard_map/ppermute | solution.py:365
  52.1 0.6 collective-permute-start.13
  52.6 2.4 %collective-permute-done.12 = f16[64,512]{1,0:T(8,128)(2,1)S(1)} collective-permute-done((f16[64,512]{1,0:T(8,128)(2,1)S(1)}, f16[64,512]{1,0:T(8,128)(2,1)S(1)}, u32[]{:S(2)}, u32[]{:S(2)}) %collective-permute-start.12) | collective-permute-done | bytes 65568 | tf_op jit(solution)/shard_map/ppermute | solution.py:365
  55.0 2.0 %collective-permute-start.15 = (f16[64,512]{1,0:T(8,128)(2,1)S(1)}, f16[64,512]{1,0:T(8,128)(2,1)S(1)}, u32[]{:S(2)}, u32[]{:S(2)}) collective-permute-start(f16[64,512]{1,0:T(8,128)(2,1)S(1)} %fusion), channel_id=1, source_target_pairs={{0,4},{1,5},{2,6},{3,7},{4,0},{5,1},{6,2},{7,3},{8,12},{9,13},{10,... | collective-permute-start | bytes 196616 | tf_op jit(solution)/shard_map/ppermute | solution.py:365
  57.0 0.6 collective-permute-done.13
  57.7 1.6 %collective-permute-done.15 = f16[64,512]{1,0:T(8,128)(2,1)S(1)} collective-permute-done((f16[64,512]{1,0:T(8,128)(2,1)S(1)}, f16[64,512]{1,0:T(8,128)(2,1)S(1)}, u32[]{:S(2)}, u32[]{:S(2)}) %collective-permute-start.15) | collective-permute-done | bytes 65568 | tf_op jit(solution)/shard_map/ppermute | solution.py:365
  59.4 3.0 %collective-permute-start.16 = (f16[64,512]{1,0:T(8,128)(2,1)S(1)}, f16[64,512]{1,0:T(8,128)(2,1)S(1)}, u32[]{:S(2)}, u32[]{:S(2)}) collective-permute-start(f16[64,512]{1,0:T(8,128)(2,1)S(1)} %add_convert_fusion), channel_id=1, source_target_pairs={{0,8},{1,9},{2,10},{3,11},{4,12},{5,13},{6,14},{7,15},{8,0},{9,1},... | collective-permute-start | bytes 196616 | tf_op jit(solution)/shard_map/ppermute | solution.py:365
  62.5 1.6 %shard_map.93 = f32[512,512]{1,0:T(8,128)} custom-call(s32[4]{0:T(128)S(1)} %pad_add_fusion.refs_0_, f32[128,512]{1,0:T(8,128)S(1)} %get-tuple-element.58.refs_1_, f32[128,512]{1,0:T(8,128)S(1)} %convert_element_type.68.refs_2_, f32[256,512]{1,0:T(8,128)S(1)} %convert_element_type.69.refs_3_), custom_call_target="tpu_custom_call" | custom-call | flops 1048576 | bytes 2097152 | tf_op jit(solution)/shard_map/pallas_call | solution.py:340
  64.1 0.5 collective-permute-done.16
  64.6 0.7 %add_bitcast_fusion = f32[512,64]{0,1:T(8,128)} fusion(f16[64,512]{1,0:T(8,128)(2,1)S(1)} %collective-permute-done.16, f16[64,512]{1,0:T(8,128)(2,1)S(1)} %add_convert_fusion), kind=kLoop, calls=%fused_computation.4 | loop fusion | flops 98304 | bytes 262144 | tf_op jit(solution)/shard_map/transpose | solution.py:429
  (30 shorter events, 1.2 us)
Async XLA Ops:
  0.6 9.4 %copy-start.2 = (s32[512,40]{0,1:T(8,128)S(1)}, s32[512,40]{0,1:T(8,128)}, u32[]{:S(2)}) copy-start(s32[512,40]{0,1:T(8,128)} %param.13) | copy-start | bytes 245764
  2.6 7.5 %copy-start = (bf16[144,1024]{1,0:T(8,128)(2,1)S(1)}, bf16[144,1024]{1,0:T(8,128)(2,1)}, u32[]{:S(2)}) copy-start(bf16[144,1024]{1,0:T(8,128)(2,1)} %get-tuple-element.30.scens) | copy-start | bytes 884740
  2.7 7.5 %collective-permute-start.1 = (bf16[80,1024]{1,0:T(8,128)(2,1)}, bf16[80,1024]{1,0:T(8,128)(2,1)S(1)}, u32[]{:S(2)}, u32[]{:S(2)}) collective-permute-start(bf16[80,1024]{1,0:T(8,128)(2,1)} %get-tuple-element.31.p0.refs_0_), channel_id=1, source_target_pairs={{0,1},{1,0},{2,3},{3,2},{4,5},{5,4},{6,7},{7,6},{8,9},{9,8},{10,11... | collective-permute-start | bytes 491528 | tf_op jit(solution)/shard_map/ppermute | solution.py:365
  3.2 21.6 %collective-permute-start.4 = (bf16[80,1024]{1,0:T(8,128)(2,1)}, bf16[80,1024]{1,0:T(8,128)(2,1)S(1)}, u32[]{:S(2)}, u32[]{:S(2)}) collective-permute-start(bf16[80,1024]{1,0:T(8,128)(2,1)} %get-tuple-element.31.p0.refs_0_), channel_id=1, source_target_pairs={{0,4},{1,5},{2,6},{3,7},{4,0},{5,1},{6,2},{7,3},{8,12},{9,13},{10,... | collective-permute-start | bytes 491528 | tf_op jit(solution)/shard_map/ppermute | solution.py:365
  5.8 18.4 %collective-permute-start.7 = (bf16[80,1024]{1,0:T(8,128)(2,1)}, bf16[80,1024]{1,0:T(8,128)(2,1)S(1)}, u32[]{:S(2)}, u32[]{:S(2)}) collective-permute-start(bf16[80,1024]{1,0:T(8,128)(2,1)} %get-tuple-element.31.p0.refs_0_), channel_id=1, source_target_pairs={{0,8},{1,9},{2,10},{3,11},{4,12},{5,13},{6,14},{7,15},{8,0},{9,1},... | collective-permute-start | bytes 491528 | tf_op jit(solution)/shard_map/ppermute | solution.py:365
  8.4 9.0 %collective-permute-start = (bf16[144,1024]{1,0:T(8,128)(2,1)}, bf16[144,1024]{1,0:T(8,128)(2,1)S(1)}, u32[]{:S(2)}, u32[]{:S(2)}) collective-permute-start(bf16[144,1024]{1,0:T(8,128)(2,1)} %get-tuple-element.30.scens), channel_id=1, source_target_pairs={{0,2},{1,3},{2,0},{3,1},{4,6},{5,7},{6,4},{7,5},{8,10},{9,11},{10,... | collective-permute-start | bytes 884744 | tf_op jit(solution)/shard_map/ppermute | solution.py:365
  10.2 0.9 %copy-start.1 = (bf16[80,1024]{1,0:T(8,128)(2,1)S(1)}, bf16[80,1024]{1,0:T(8,128)(2,1)}, u32[]{:S(2)}) copy-start(bf16[80,1024]{1,0:T(8,128)(2,1)} %get-tuple-element.31.p0.refs_0_) | copy-start | bytes 491524
  21.0 4.9 %collective-permute-start.2 = (f32[128,512]{1,0:T(8,128)S(1)}, f32[128,512]{1,0:T(8,128)S(1)}, u32[]{:S(2)}, u32[]{:S(2)}) collective-permute-start(f32[128,512]{1,0:T(8,128)S(1)} %get-tuple-element.36), channel_id=1, source_target_pairs={{0,1},{1,0},{2,3},{3,2},{4,5},{5,4},{6,7},{7,6},{8,9},{9,8},{10,11... | collective-permute-start | bytes 786440 | tf_op jit(solution)/shard_map/ppermute | solution.py:365
  24.2 1.6 %collective-permute-start.8 = (bf16[80,1024]{1,0:T(8,128)(2,1)S(1)}, bf16[80,1024]{1,0:T(8,128)(2,1)S(1)}, u32[]{:S(2)}, u32[]{:S(2)}) collective-permute-start(bf16[80,1024]{1,0:T(8,128)(2,1)S(1)} %collective-permute-done.7.refs_2_), channel_id=1, source_target_pairs={{0,1},{1,0},{2,3},{3,2},{4,5},{5,4},{6,7},{7,6},{8,9},{9,8},{10,11... | collective-permute-start | bytes 491528 | tf_op jit(solution)/shard_map/ppermute | solution.py:365
  24.8 16.0 %collective-permute-start.9 = (bf16[80,1024]{1,0:T(8,128)(2,1)S(1)}, bf16[80,1024]{1,0:T(8,128)(2,1)S(1)}, u32[]{:S(2)}, u32[]{:S(2)}) collective-permute-start(bf16[80,1024]{1,0:T(8,128)(2,1)S(1)} %collective-permute-done.4.refs_2_), channel_id=1, source_target_pairs={{0,8},{1,9},{2,10},{3,11},{4,12},{5,13},{6,14},{7,15},{8,0},{9,1},... | collective-permute-start | bytes 491528 | tf_op jit(solution)/shard_map/ppermute | solution.py:365
  25.1 1.4 %collective-permute-start.5 = (bf16[80,1024]{1,0:T(8,128)(2,1)S(1)}, bf16[80,1024]{1,0:T(8,128)(2,1)S(1)}, u32[]{:S(2)}, u32[]{:S(2)}) collective-permute-start(bf16[80,1024]{1,0:T(8,128)(2,1)S(1)} %collective-permute-done.4.refs_2_), channel_id=1, source_target_pairs={{0,1},{1,0},{2,3},{3,2},{4,5},{5,4},{6,7},{7,6},{8,9},{9,8},{10,11... | collective-permute-start | bytes 491528 | tf_op jit(solution)/shard_map/ppermute | solution.py:365
  26.5 9.0 %collective-permute-start.3 = (f16[128,512]{1,0:T(8,128)(2,1)S(1)}, f16[128,512]{1,0:T(8,128)(2,1)S(1)}, u32[]{:S(2)}, u32[]{:S(2)}) collective-permute-start(f16[128,512]{1,0:T(8,128)(2,1)S(1)} %fusion.3), channel_id=1, source_target_pairs={{0,4},{1,5},{2,6},{3,7},{4,0},{5,1},{6,2},{7,3},{8,12},{9,13},{10,... | collective-permute-start | bytes 393224 | tf_op jit(solution)/shard_map/ppermute | solution.py:365
  35.5 5.9 %collective-permute-start.6 = (f16[128,512]{1,0:T(8,128)(2,1)S(1)}, f16[128,512]{1,0:T(8,128)(2,1)S(1)}, u32[]{:S(2)}, u32[]{:S(2)}) collective-permute-start(f16[128,512]{1,0:T(8,128)(2,1)S(1)} %fusion.1), channel_id=1, source_target_pairs={{0,8},{1,9},{2,10},{3,11},{4,12},{5,13},{6,14},{7,15},{8,0},{9,1},... | collective-permute-start | bytes 393224 | tf_op jit(solution)/shard_map/ppermute | solution.py:365
  40.7 1.5 %collective-permute-start.10 = (bf16[80,1024]{1,0:T(8,128)(2,1)S(1)}, bf16[80,1024]{1,0:T(8,128)(2,1)S(1)}, u32[]{:S(2)}, u32[]{:S(2)}) collective-permute-start(bf16[80,1024]{1,0:T(8,128)(2,1)S(1)} %collective-permute-done.9.refs_2_), channel_id=1, source_target_pairs={{0,1},{1,0},{2,3},{3,2},{4,5},{5,4},{6,7},{7,6},{8,9},{9,8},{10,11... | collective-permute-start | bytes 491528 | tf_op jit(solution)/shard_map/ppermute | solution.py:365
  49.0 1.4 %collective-permute-start.11 = (f32[64,512]{1,0:T(8,128)S(1)}, f32[64,512]{1,0:T(8,128)S(1)}, u32[]{:S(2)}, u32[]{:S(2)}) collective-permute-start(f32[64,512]{1,0:T(8,128)S(1)} %shard_map.92), channel_id=1, source_target_pairs={{0,1},{1,0},{2,3},{3,2},{4,5},{5,4},{6,7},{7,6},{8,9},{9,8},{10,11... | collective-permute-start | bytes 393224 | tf_op jit(solution)/shard_map/ppermute | solution.py:365
  50.4 4.6 %collective-permute-start.12 = (f16[64,512]{1,0:T(8,128)(2,1)S(1)}, f16[64,512]{1,0:T(8,128)(2,1)S(1)}, u32[]{:S(2)}, u32[]{:S(2)}) collective-permute-start(f16[64,512]{1,0:T(8,128)(2,1)S(1)} %add_convert_fusion.1), channel_id=1, source_target_pairs={{0,2},{1,3},{2,0},{3,1},{4,6},{5,7},{6,4},{7,5},{8,10},{9,11},{10,... | collective-permute-start | bytes 196616 | tf_op jit(solution)/shard_map/ppermute | solution.py:365
  52.1 5.5 %collective-permute-start.13 = (f16[128,512]{1,0:T(8,128)(2,1)S(1)}, f16[128,512]{1,0:T(8,128)(2,1)S(1)}, u32[]{:S(2)}, u32[]{:S(2)}) collective-permute-start(f16[128,512]{1,0:T(8,128)(2,1)S(1)} %get-tuple-element.59), channel_id=1, source_target_pairs={{0,2},{1,3},{2,0},{3,1},{4,6},{5,7},{6,4},{7,5},{8,10},{9,11},{10,... | collective-permute-start | bytes 393224 | tf_op jit(solution)/shard_map/ppermute | solution.py:365
  55.0 4.3 %collective-permute-start.15 = (f16[64,512]{1,0:T(8,128)(2,1)S(1)}, f16[64,512]{1,0:T(8,128)(2,1)S(1)}, u32[]{:S(2)}, u32[]{:S(2)}) collective-permute-start(f16[64,512]{1,0:T(8,128)(2,1)S(1)} %fusion), channel_id=1, source_target_pairs={{0,4},{1,5},{2,6},{3,7},{4,0},{5,1},{6,2},{7,3},{8,12},{9,13},{10,... | collective-permute-start | bytes 196616 | tf_op jit(solution)/shard_map/ppermute | solution.py:365
  57.6 4.8 %collective-permute-start.14 = (f16[256,512]{1,0:T(8,128)(2,1)S(1)}, f16[256,512]{1,0:T(8,128)(2,1)S(1)}, u32[]{:S(2)}, u32[]{:S(2)}) collective-permute-start(f16[256,512]{1,0:T(8,128)(2,1)S(1)} %pad_maximum_fusion), channel_id=1, source_target_pairs={{0,1},{1,0},{2,3},{3,2},{4,5},{5,4},{6,7},{7,6},{8,9},{9,8},{10,11... | collective-permute-start | bytes 786440 | tf_op jit(solution)/shard_map/ppermute | solution.py:365
  59.4 5.2 %collective-permute-start.16 = (f16[64,512]{1,0:T(8,128)(2,1)S(1)}, f16[64,512]{1,0:T(8,128)(2,1)S(1)}, u32[]{:S(2)}, u32[]{:S(2)}) collective-permute-start(f16[64,512]{1,0:T(8,128)(2,1)S(1)} %add_convert_fusion), channel_id=1, source_target_pairs={{0,8},{1,9},{2,10},{3,11},{4,12},{5,13},{6,14},{7,15},{8,0},{9,1},... | collective-permute-start | bytes 196616 | tf_op jit(solution)/shard_map/ppermute | solution.py:365

commit v6 on v5

--- a/solution.py
+++ b/solution.py
@@ -371,15 +371,10 @@
 
     near = (pack, swap(pack, 1))
     scens1 = swap(scens0, 2)
-    packs = {m: swap(pack, m) for m in deep}
+    packs = {m: swap(pack, m) for m in far}
 
     high0, low0, rt0, v = basis_of(exponents, scens0, near, lines)
     before = [v]
-    packs[4] = after(packs[4], v)
-    for m in far:
-        top = max(h for h in deep if h <= m)
-        if m not in packs:
-            packs[m] = swap(packs[m ^ top], top)
 
     base = side * 2 + core
     start = jnp.stack([base, base ^ 1])
@@ -387,31 +382,30 @@
         exponents, after(scens1, v), start=start, first=high0
     )
     more = swap(send, 1)
+    relays = {4: swap(after(packs[4], send), 1)}
     v = values_of([rt1], near, lines)
     before.append(v)
     keep, more = after((keep, more), v)
     gram = (keep + more) * (1.0 / scen_total)
 
+    for m in far[1:]:
+        relays[m] = swap(after(packs[m], v), 1)
+    calls = [[packs[m], relays[m]] for m in far[:-1]] + [[packs[far[-1]]], [relays[far[-1]]]]
     rts = [rt0, rt1]
-    steps = list(deep)
-    for i, m in enumerate(far):
-        pair = [packs[m], swap(after(packs[m], v), 1)]
+    steps, other = list(deep), None
+    for i, call in enumerate(calls):
+        last = i == len(calls) - 1
+        if other is not None and (steps or last):
+            gram = mine.astype(F32) + after(other, v).astype(F32)
+            other = None
         if steps:
             mine = gram.astype(HALF)
             other = swap(mine, steps.pop(0))
-        if m == far[-1]:
-            break
-        v0 = values_of(rts, after(pair, gram), lines, before)
-        before = [v0]
-        if i > 0:
-            v = v0
-        if other is not None:
-            gram = mine.astype(F32) + after(other, v0).astype(F32)
-            other = None
-        else:
-            gram = after(gram, v0)
-    basis = (high0, low0, high1, low1)
-    rhs = values_of(rts, after(pair, gram), lines, before, basis, scale)
+        call = after(call, gram)
+        if not last:
+            v = values_of(rts, call, lines, before)
+            before = [v]
+    rhs = values_of(rts, call, lines, before, (high0, low0, high1, low1), scale)
 
     rhs = rhs + swap(rhs, 1)
     for m in [2] + deep:

time: 65.5 us -> 64.4 us (0.983)
  waiting for transfers between devices: 13.5 us -> 12.3 us
    ppermute x17, waiting for transfers between devices: 13.5 us -> 12.3 us  [swap(): return lax.ppermute(x, 'scen', [(i, i ^ mask) for i in range(n)])]
    pallas_call x4 -> x5, Pallas kernels: 20.3 us -> 20.9 us  [values_of(): pl.pallas_call(kernel, in_specs=[HSPEC] * len(rts) + [VSPEC] * len(packs)...]
  transfers between devices with their start and end apart: 17 -> 17, of which waited for: 11 -> 6; matrix products, arithmetic and copies ran while one was open for 1% -> 1% of each run, Pallas kernels for 36% -> 42%
where the time goes in v6:
time: 64.4 us; the launch traced here: 64.2 us
  Pallas kernels  33.2 us (52%)
  starting transfers between devices  15.6 us (24%)
  waiting for transfers between devices  12.3 us (19%)
  other arithmetic  1.18 us (2%)
  local copies, waits for them, and re-layouts  1.04 us (2%)
  between operations  0.9 us (1%)
    pallas_call x5, Pallas kernels, values_of(): pl.pallas_call(kernel, in_specs=[HSPEC] * len(rts) + [VSPEC] * len(packs)...  20.9 us
    ppermute x17, starting transfers between devices, swap(): return lax.ppermute(x, 'scen', [(i, i ^ mask) for i in range(n)])  15.6 us
    ppermute x17, waiting for transfers between devices, swap(): return lax.ppermute(x, 'scen', [(i, i ^ mask) for i in range(n)])  12.3 us
    pallas_call x1, Pallas kernels, basis_of(): pl.pallas_call(first_kernel, in_specs=[VSPEC] * 2 + [HSPEC] * 2, out_spec...  5.18 us
    pallas_call x1, Pallas kernels, basis_of(): pl.pallas_call(gram_kernel, in_specs=[SSPEC, VSPEC, VSPEC, HSPEC], out_sp...  3.53 us
    pallas_call x1, Pallas kernels, packs_of(): pl.pallas_call(pack_kernel, in_specs=[pl.BlockSpec(memory_space=pltpu.HBM...  1.99 us
    pallas_call x1, Pallas kernels, placed(): pl.pallas_call(functools.partial(place_kernel, blocks), in_specs=[pl.Bloc...  1.59 us
  transfers between devices with their start and end apart: 17, of which 6 were waited for; matrix products, arithmetic and copies ran while one was open for 1% of the time, Pallas kernels for 42%

profile of v6, /device:TPU:0, one launch (start us, length us, event | category | flops | bytes accessed | tf_op | source)
XLA Modules:
  0.0 64.2 jit_solution(6198955059359894848)
XLA Ops:
  0.6 2.0 %shard_map.86 = (bf16[80,1024]{1,0:T(8,128)(2,1)}, bf16[144,1024]{1,0:T(8,128)(2,1)}) custom-call(bf16[64,1024]{1,0:T(8,128)(2,1)} %bitcast.10, f32[1,1024]{1,0:T(1,128)} %bitcast.11, s32[1,1024]{1,0:T(1,128)} %bitcast.12, s32[1,1024]{1,0:T(1,128)} %bitcast.13, bf16[64,1024]{1,0:T(8,128)(2,1)} %refs_4_.1, f32[40,1024]{1,0:T(8,128)} %refs_5_.1), custom_call_target="tpu_custom_call" | custom-call | flops 1048576 | bytes 1048576 | tf_op jit(solution)/shard_map/pallas_call | solution.py:63
  2.7 0.5 collective-permute-start.1
  3.2 2.6 %collective-permute-start.4 = (bf16[80,1024]{1,0:T(8,128)(2,1)}, bf16[80,1024]{1,0:T(8,128)(2,1)S(1)}, u32[]{:S(2)}, u32[]{:S(2)}) collective-permute-start(bf16[80,1024]{1,0:T(8,128)(2,1)} %get-tuple-element.30.p0.refs_0_), channel_id=1, source_target_pairs={{0,4},{1,5},{2,6},{3,7},{4,0},{5,1},{6,2},{7,3},{8,12},{9,13},{10,... | collective-permute-start | bytes 491528 | tf_op jit(solution)/shard_map/ppermute | solution.py:365
  5.8 2.6 %collective-permute-start.8 = (bf16[80,1024]{1,0:T(8,128)(2,1)}, bf16[80,1024]{1,0:T(8,128)(2,1)S(1)}, u32[]{:S(2)}, u32[]{:S(2)}) collective-permute-start(bf16[80,1024]{1,0:T(8,128)(2,1)} %get-tuple-element.30.p0.refs_0_), channel_id=1, source_target_pairs={{0,8},{1,9},{2,10},{3,11},{4,12},{5,13},{6,14},{7,15},{8,0},{9,1},... | collective-permute-start | bytes 491528 | tf_op jit(solution)/shard_map/ppermute | solution.py:365
  8.4 1.7 %collective-permute-start = (bf16[144,1024]{1,0:T(8,128)(2,1)}, bf16[144,1024]{1,0:T(8,128)(2,1)S(1)}, u32[]{:S(2)}, u32[]{:S(2)}) collective-permute-start(bf16[144,1024]{1,0:T(8,128)(2,1)} %get-tuple-element.29.scens), channel_id=1, source_target_pairs={{0,2},{1,3},{2,0},{3,1},{4,6},{5,7},{6,4},{7,5},{8,10},{9,11},{10,... | collective-permute-start | bytes 884744 | tf_op jit(solution)/shard_map/ppermute | solution.py:365
  10.2 0.1 copy.10.exps
  10.4 0.9 %copy-done.1 = bf16[80,1024]{1,0:T(8,128)(2,1)S(1)} copy-done((bf16[80,1024]{1,0:T(8,128)(2,1)S(1)}, bf16[80,1024]{1,0:T(8,128)(2,1)}, u32[]{:S(2)}) %copy-start.1) | copy-done | bytes 163864
  11.3 5.2 %shard_map.87 = (bf16[512,1024]{1,0:T(8,128)(2,1)S(1)}, bf16[512,1024]{1,0:T(8,128)(2,1)S(1)}, bf16[1024,128]{1,0:T(8,128)(2,1)S(1)}, f32[1024,64]{1,0:T(8,128)S(1)}) custom-call(s32[512,40]{1,0:T(8,128)S(1)} %copy.10.exps, bf16[144,1024]{1,0:T(8,128)(2,1)S(1)} %copy-done, bf16[80,1024]{1,0:T(8,128)(2,1)S(1)} %copy-done.1, ...), custom_call_target="tpu_custom_call" | custom-call | flops 3000000000 | bytes 3145728 | tf_op jit(solution)/shard_map/pallas_call | solution.py:304
  16.5 0.9 %collective-permute-done.scens = bf16[144,1024]{1,0:T(8,128)(2,1)S(1)} collective-permute-done((bf16[144,1024]{1,0:T(8,128)(2,1)}, bf16[144,1024]{1,0:T(8,128)(2,1)S(1)}, u32[]{:S(2)}, u32[]{:S(2)}) %collective-permute-start) | collective-permute-done | bytes 294944 | tf_op jit(solution)/shard_map/ppermute | solution.py:365
  17.4 3.5 %shard_map.88 = (bf16[512,1024]{1,0:T(8,128)(2,1)S(1)}, bf16[512,1024]{1,0:T(8,128)(2,1)S(1)}, bf16[1024,128]{1,0:T(8,128)(2,1)S(1)}, f32[128,512]{1,0:T(8,128)S(1)}, f32[128,512]{1,0:T(8,128)S(1)}) custom-call(s32[2]{0:T(128)S(1)} %pad_add_fusion.1.start, s32[512,40]{1,0:T(8,128)S(1)} %copy.10.exps, bf16[144,1024]{1,0:T(8,128)(2,1)S(1)} %collective-permute-done.scens, ...), custom_call_target="tpu_custom_call" | custom-call | flops 3000000000 | bytes 3145728 | tf_op jit(solution)/shard_map/pallas_call | solution.py:317
  21.1 0.5 collective-permute-start.5
  21.5 3.2 %shard_map.89.refs_5_ = f32[1024,64]{1,0:T(8,128)S(1)} custom-call(bf16[1024,128]{1,0:T(8,128)(2,1)S(1)} %get-tuple-element.36.rt.refs_1_, bf16[80,1024]{1,0:T(8,128)(2,1)S(1)} %copy-done.1, bf16[80,1024]{1,0:T(8,128)(2,1)S(1)} %collective-permute-done.1.p1.refs_1_), custom_call_target="tpu_custom_call" | custom-call | flops 3565158400 | bytes 1048576 | tf_op jit(solution)/shard_map/pallas_call | solution.py:205
  24.7 0.2 collective-permute-start.9
  24.9 0.4 collective-permute-start.10
  25.4 0.7 %collective-permute-start.3 = (f16[128,512]{1,0:T(8,128)(2,1)S(1)}, f16[128,512]{1,0:T(8,128)(2,1)S(1)}, u32[]{:S(2)}, u32[]{:S(2)}) collective-permute-start(f16[128,512]{1,0:T(8,128)(2,1)S(1)} %fusion.3), channel_id=1, source_target_pairs={{0,4},{1,5},{2,6},{3,7},{4,0},{5,1},{6,2},{7,3},{8,12},{9,13},{10,... | collective-permute-start | bytes 393224 | tf_op jit(solution)/shard_map/ppermute | solution.py:365
  26.0 5.2 %shard_map.90.refs_4_ = f32[1024,128]{1,0:T(8,128)S(1)} custom-call(bf16[1024,128]{1,0:T(8,128)(2,1)S(1)} %get-tuple-element.39.refs_0_, bf16[1024,128]{1,0:T(8,128)(2,1)S(1)} %get-tuple-element.36.rt.refs_1_, bf16[80,1024]{1,0:T(8,128)(2,1)S(1)} %collective-permute-done.4.refs_2_, bf16[80,1024]{1,0:T(8,128)(2,1)S(1)} %collective-permute-done.5.refs_3_, ...), custom_call_target="tpu_custom_call" | custom-call | flops 7130316800 | bytes 1048576 | tf_op jit(solution)/shard_map/pallas_call | solution.py:205
  31.3 3.5 %collective-permute-start.6 = (f16[128,512]{1,0:T(8,128)(2,1)S(1)}, f16[128,512]{1,0:T(8,128)(2,1)S(1)}, u32[]{:S(2)}, u32[]{:S(2)}) collective-permute-start(f16[128,512]{1,0:T(8,128)(2,1)S(1)} %fusion.1), channel_id=1, source_target_pairs={{0,8},{1,9},{2,10},{3,11},{4,12},{5,13},{6,14},{7,15},{8,0},{9,1},... | collective-permute-start | bytes 393224 | tf_op jit(solution)/shard_map/ppermute | solution.py:365
  34.9 5.1 %shard_map.91.refs_3_ = f32[1024,128]{1,0:T(8,128)S(1)} custom-call(bf16[1024,128]{1,0:T(8,128)(2,1)S(1)} %get-tuple-element.39.refs_0_, bf16[1024,128]{1,0:T(8,128)(2,1)S(1)} %get-tuple-element.36.rt.refs_1_, bf16[80,1024]{1,0:T(8,128)(2,1)S(1)} %collective-permute-done.8.refs_2_, bf16[80,1024]{1,0:T(8,128)(2,1)S(1)} %collective-permute-done.9.refs_3_, ...), custom_call_target="tpu_custom_call" | custom-call | flops 7130316800 | bytes 1048576 | tf_op jit(solution)/shard_map/pallas_call | solution.py:205
  40.0 3.1 %shard_map.92.refs_3_ = f32[1024,128]{1,0:T(8,128)S(1)} custom-call(bf16[1024,128]{1,0:T(8,128)(2,1)S(1)} %get-tuple-element.39.refs_0_, bf16[1024,128]{1,0:T(8,128)(2,1)S(1)} %get-tuple-element.36.rt.refs_1_, bf16[80,1024]{1,0:T(8,128)(2,1)S(1)} %collective-permute-done.7.refs_2_, f32[1024,128]{1,0:T(8,128)S(1)} %shard_map.91.refs_3_), custom_call_target="tpu_custom_call" | custom-call | flops 3565158400 | bytes 1048576 | tf_op jit(solution)/shard_map/pallas_call | solution.py:205
  43.2 4.3 %shard_map.93 = f32[64,512]{1,0:T(8,128)S(1)} custom-call(bf16[1024,128]{1,0:T(8,128)(2,1)S(1)} %get-tuple-element.39.refs_0_, bf16[1024,128]{1,0:T(8,128)(2,1)S(1)} %get-tuple-element.36.rt.refs_1_, bf16[80,1024]{1,0:T(8,128)(2,1)S(1)} %collective-permute-done.10.refs_2_, f32[1024,128]{1,0:T(8,128)S(1)} %shard_map.92.refs_3_, ...), custom_call_target="tpu_custom_call" | custom-call | flops 3565158400 | bytes 1048576 | tf_op jit(solution)/shard_map/pallas_call | solution.py:205
  47.6 1.3 %collective-permute-done.11 = f32[64,512]{1,0:T(8,128)S(1)} collective-permute-done((f32[64,512]{1,0:T(8,128)S(1)}, f32[64,512]{1,0:T(8,128)S(1)}, u32[]{:S(2)}, u32[]{:S(2)}) %collective-permute-start.11) | collective-permute-done | bytes 131104 | tf_op jit(solution)/shard_map/ppermute | solution.py:365
  48.9 1.6 %collective-permute-start.12 = (f16[64,512]{1,0:T(8,128)(2,1)S(1)}, f16[64,512]{1,0:T(8,128)(2,1)S(1)}, u32[]{:S(2)}, u32[]{:S(2)}) collective-permute-start(f16[64,512]{1,0:T(8,128)(2,1)S(1)} %add_convert_fusion.1), channel_id=1, source_target_pairs={{0,2},{1,3},{2,0},{3,1},{4,6},{5,7},{6,4},{7,5},{8,10},{9,11},{10,... | collective-permute-start | bytes 196616 | tf_op jit(solution)/shard_map/ppermute | solution.py:365
  50.6 0.6 collective-permute-start.13
  51.1 2.4 %collective-permute-done.12 = f16[64,512]{1,0:T(8,128)(2,1)S(1)} collective-permute-done((f16[64,512]{1,0:T(8,128)(2,1)S(1)}, f16[64,512]{1,0:T(8,128)(2,1)S(1)}, u32[]{:S(2)}, u32[]{:S(2)}) %collective-permute-start.12) | collective-permute-done | bytes 65568 | tf_op jit(solution)/shard_map/ppermute | solution.py:365
  53.6 0.3 collective-permute-start.15
  53.9 2.2 %collective-permute-done.13 = f16[128,512]{1,0:T(8,128)(2,1)S(1)} collective-permute-done((f16[128,512]{1,0:T(8,128)(2,1)S(1)}, f16[128,512]{1,0:T(8,128)(2,1)S(1)}, u32[]{:S(2)}, u32[]{:S(2)}) %collective-permute-start.13) | collective-permute-done | bytes 131104 | tf_op jit(solution)/shard_map/ppermute | solution.py:365
  56.2 1.6 %collective-permute-done.15 = f16[64,512]{1,0:T(8,128)(2,1)S(1)} collective-permute-done((f16[64,512]{1,0:T(8,128)(2,1)S(1)}, f16[64,512]{1,0:T(8,128)(2,1)S(1)}, u32[]{:S(2)}, u32[]{:S(2)}) %collective-permute-start.15) | collective-permute-done | bytes 65568 | tf_op jit(solution)/shard_map/ppermute | solution.py:365
  57.9 0.1 collective-permute-start.16
  58.0 0.1 pad_add_fusion.refs_0_
  58.2 1.6 %shard_map.94 = f32[512,512]{1,0:T(8,128)} custom-call(s32[4]{0:T(128)S(1)} %pad_add_fusion.refs_0_, f32[128,512]{1,0:T(8,128)S(1)} %get-tuple-element.56.refs_1_, f32[128,512]{1,0:T(8,128)S(1)} %convert_element_type.68.refs_2_, f32[256,512]{1,0:T(8,128)S(1)} %convert_element_type.69.refs_3_), custom_call_target="tpu_custom_call" | custom-call | flops 1048576 | bytes 2097152 | tf_op jit(solution)/shard_map/pallas_call | solution.py:340
  59.8 3.8 %collective-permute-done.16 = f16[64,512]{1,0:T(8,128)(2,1)S(1)} collective-permute-done((f16[64,512]{1,0:T(8,128)(2,1)S(1)}, f16[64,512]{1,0:T(8,128)(2,1)S(1)}, u32[]{:S(2)}, u32[]{:S(2)}) %collective-permute-start.16) | collective-permute-done | bytes 65568 | tf_op jit(solution)/shard_map/ppermute | solution.py:365
  63.6 0.7 %add_bitcast_fusion = f32[512,64]{0,1:T(8,128)} fusion(f16[64,512]{1,0:T(8,128)(2,1)S(1)} %collective-permute-done.16, f16[64,512]{1,0:T(8,128)(2,1)S(1)} %add_convert_fusion), kind=kLoop, calls=%fused_computation.4 | loop fusion | flops 98304 | bytes 262144 | tf_op jit(solution)/shard_map/transpose | solution.py:423
  (31 shorter events, 0.7 us)
Async XLA Ops:
  0.6 9.6 %copy-start.2 = (s32[512,40]{0,1:T(8,128)S(1)}, s32[512,40]{0,1:T(8,128)}, u32[]{:S(2)}) copy-start(s32[512,40]{0,1:T(8,128)} %param.13) | copy-start | bytes 245764
  2.6 7.7 %copy-start = (bf16[144,1024]{1,0:T(8,128)(2,1)S(1)}, bf16[144,1024]{1,0:T(8,128)(2,1)}, u32[]{:S(2)}) copy-start(bf16[144,1024]{1,0:T(8,128)(2,1)} %get-tuple-element.29.scens) | copy-start | bytes 884740
  2.7 7.7 %collective-permute-start.1 = (bf16[80,1024]{1,0:T(8,128)(2,1)}, bf16[80,1024]{1,0:T(8,128)(2,1)S(1)}, u32[]{:S(2)}, u32[]{:S(2)}) collective-permute-start(bf16[80,1024]{1,0:T(8,128)(2,1)} %get-tuple-element.30.p0.refs_0_), channel_id=1, source_target_pairs={{0,1},{1,0},{2,3},{3,2},{4,5},{5,4},{6,7},{7,6},{8,9},{9,8},{10,11... | collective-permute-start | bytes 491528 | tf_op jit(solution)/shard_map/ppermute | solution.py:365
  3.2 17.9 %collective-permute-start.4 = (bf16[80,1024]{1,0:T(8,128)(2,1)}, bf16[80,1024]{1,0:T(8,128)(2,1)S(1)}, u32[]{:S(2)}, u32[]{:S(2)}) collective-permute-start(bf16[80,1024]{1,0:T(8,128)(2,1)} %get-tuple-element.30.p0.refs_0_), channel_id=1, source_target_pairs={{0,4},{1,5},{2,6},{3,7},{4,0},{5,1},{6,2},{7,3},{8,12},{9,13},{10,... | collective-permute-start | bytes 491528 | tf_op jit(solution)/shard_map/ppermute | solution.py:365
  5.8 18.9 %collective-permute-start.8 = (bf16[80,1024]{1,0:T(8,128)(2,1)}, bf16[80,1024]{1,0:T(8,128)(2,1)S(1)}, u32[]{:S(2)}, u32[]{:S(2)}) collective-permute-start(bf16[80,1024]{1,0:T(8,128)(2,1)} %get-tuple-element.30.p0.refs_0_), channel_id=1, source_target_pairs={{0,8},{1,9},{2,10},{3,11},{4,12},{5,13},{6,14},{7,15},{8,0},{9,1},... | collective-permute-start | bytes 491528 | tf_op jit(solution)/shard_map/ppermute | solution.py:365
  8.4 16.5 %collective-permute-start.7 = (bf16[80,1024]{1,0:T(8,128)(2,1)}, bf16[80,1024]{1,0:T(8,128)(2,1)S(1)}, u32[]{:S(2)}, u32[]{:S(2)}) collective-permute-start(bf16[80,1024]{1,0:T(8,128)(2,1)} %get-tuple-element.30.p0.refs_0_), channel_id=1, source_target_pairs={{0,12},{1,13},{2,14},{3,15},{4,8},{5,9},{6,10},{7,11},{8,4},{9,5},... | collective-permute-start | bytes 491528 | tf_op jit(solution)/shard_map/ppermute | solution.py:365
  8.4 9.0 %collective-permute-start = (bf16[144,1024]{1,0:T(8,128)(2,1)}, bf16[144,1024]{1,0:T(8,128)(2,1)S(1)}, u32[]{:S(2)}, u32[]{:S(2)}) collective-permute-start(bf16[144,1024]{1,0:T(8,128)(2,1)} %get-tuple-element.29.scens), channel_id=1, source_target_pairs={{0,2},{1,3},{2,0},{3,1},{4,6},{5,7},{6,4},{7,5},{8,10},{9,11},{10,... | collective-permute-start | bytes 884744 | tf_op jit(solution)/shard_map/ppermute | solution.py:365
  10.4 0.9 %copy-start.1 = (bf16[80,1024]{1,0:T(8,128)(2,1)S(1)}, bf16[80,1024]{1,0:T(8,128)(2,1)}, u32[]{:S(2)}) copy-start(bf16[80,1024]{1,0:T(8,128)(2,1)} %get-tuple-element.30.p0.refs_0_) | copy-start | bytes 491524
  21.0 4.3 %collective-permute-start.2 = (f32[128,512]{1,0:T(8,128)S(1)}, f32[128,512]{1,0:T(8,128)S(1)}, u32[]{:S(2)}, u32[]{:S(2)}) collective-permute-start(f32[128,512]{1,0:T(8,128)S(1)} %get-tuple-element.35), channel_id=1, source_target_pairs={{0,1},{1,0},{2,3},{3,2},{4,5},{5,4},{6,7},{7,6},{8,9},{9,8},{10,11... | collective-permute-start | bytes 786440 | tf_op jit(solution)/shard_map/ppermute | solution.py:365
  21.1 4.3 %collective-permute-start.5 = (bf16[80,1024]{1,0:T(8,128)(2,1)S(1)}, bf16[80,1024]{1,0:T(8,128)(2,1)S(1)}, u32[]{:S(2)}, u32[]{:S(2)}) collective-permute-start(bf16[80,1024]{1,0:T(8,128)(2,1)S(1)} %collective-permute-done.4.refs_2_), channel_id=1, source_target_pairs={{0,1},{1,0},{2,3},{3,2},{4,5},{5,4},{6,7},{7,6},{8,9},{9,8},{10,11... | collective-permute-start | bytes 491528 | tf_op jit(solution)/shard_map/ppermute | solution.py:365
  24.7 6.6 %collective-permute-start.9 = (bf16[80,1024]{1,0:T(8,128)(2,1)S(1)}, bf16[80,1024]{1,0:T(8,128)(2,1)S(1)}, u32[]{:S(2)}, u32[]{:S(2)}) collective-permute-start(bf16[80,1024]{1,0:T(8,128)(2,1)S(1)} %collective-permute-done.8.refs_2_), channel_id=1, source_target_pairs={{0,1},{1,0},{2,3},{3,2},{4,5},{5,4},{6,7},{7,6},{8,9},{9,8},{10,11... | collective-permute-start | bytes 491528 | tf_op jit(solution)/shard_map/ppermute | solution.py:365
  24.9 18.3 %collective-permute-start.10 = (bf16[80,1024]{1,0:T(8,128)(2,1)S(1)}, bf16[80,1024]{1,0:T(8,128)(2,1)S(1)}, u32[]{:S(2)}, u32[]{:S(2)}) collective-permute-start(bf16[80,1024]{1,0:T(8,128)(2,1)S(1)} %collective-permute-done.7.refs_2_), channel_id=1, source_target_pairs={{0,1},{1,0},{2,3},{3,2},{4,5},{5,4},{6,7},{7,6},{8,9},{9,8},{10,11... | collective-permute-start | bytes 491528 | tf_op jit(solution)/shard_map/ppermute | solution.py:365
  25.4 5.9 %collective-permute-start.3 = (f16[128,512]{1,0:T(8,128)(2,1)S(1)}, f16[128,512]{1,0:T(8,128)(2,1)S(1)}, u32[]{:S(2)}, u32[]{:S(2)}) collective-permute-start(f16[128,512]{1,0:T(8,128)(2,1)S(1)} %fusion.3), channel_id=1, source_target_pairs={{0,4},{1,5},{2,6},{3,7},{4,0},{5,1},{6,2},{7,3},{8,12},{9,13},{10,... | collective-permute-start | bytes 393224 | tf_op jit(solution)/shard_map/ppermute | solution.py:365
  31.3 11.8 %collective-permute-start.6 = (f16[128,512]{1,0:T(8,128)(2,1)S(1)}, f16[128,512]{1,0:T(8,128)(2,1)S(1)}, u32[]{:S(2)}, u32[]{:S(2)}) collective-permute-start(f16[128,512]{1,0:T(8,128)(2,1)S(1)} %fusion.1), channel_id=1, source_target_pairs={{0,8},{1,9},{2,10},{3,11},{4,12},{5,13},{6,14},{7,15},{8,0},{9,1},... | collective-permute-start | bytes 393224 | tf_op jit(solution)/shard_map/ppermute | solution.py:365
  47.5 1.4 %collective-permute-start.11 = (f32[64,512]{1,0:T(8,128)S(1)}, f32[64,512]{1,0:T(8,128)S(1)}, u32[]{:S(2)}, u32[]{:S(2)}) collective-permute-start(f32[64,512]{1,0:T(8,128)S(1)} %shard_map.93), channel_id=1, source_target_pairs={{0,1},{1,0},{2,3},{3,2},{4,5},{5,4},{6,7},{7,6},{8,9},{9,8},{10,11... | collective-permute-start | bytes 393224 | tf_op jit(solution)/shard_map/ppermute | solution.py:365
  48.9 4.6 %collective-permute-start.12 = (f16[64,512]{1,0:T(8,128)(2,1)S(1)}, f16[64,512]{1,0:T(8,128)(2,1)S(1)}, u32[]{:S(2)}, u32[]{:S(2)}) collective-permute-start(f16[64,512]{1,0:T(8,128)(2,1)S(1)} %add_convert_fusion.1), channel_id=1, source_target_pairs={{0,2},{1,3},{2,0},{3,1},{4,6},{5,7},{6,4},{7,5},{8,10},{9,11},{10,... | collective-permute-start | bytes 196616 | tf_op jit(solution)/shard_map/ppermute | solution.py:365
  50.6 5.5 %collective-permute-start.13 = (f16[128,512]{1,0:T(8,128)(2,1)S(1)}, f16[128,512]{1,0:T(8,128)(2,1)S(1)}, u32[]{:S(2)}, u32[]{:S(2)}) collective-permute-start(f16[128,512]{1,0:T(8,128)(2,1)S(1)} %get-tuple-element.57), channel_id=1, source_target_pairs={{0,2},{1,3},{2,0},{3,1},{4,6},{5,7},{6,4},{7,5},{8,10},{9,11},{10,... | collective-permute-start | bytes 393224 | tf_op jit(solution)/shard_map/ppermute | solution.py:365
  53.6 4.3 %collective-permute-start.15 = (f16[64,512]{1,0:T(8,128)(2,1)S(1)}, f16[64,512]{1,0:T(8,128)(2,1)S(1)}, u32[]{:S(2)}, u32[]{:S(2)}) collective-permute-start(f16[64,512]{1,0:T(8,128)(2,1)S(1)} %fusion), channel_id=1, source_target_pairs={{0,4},{1,5},{2,6},{3,7},{4,0},{5,1},{6,2},{7,3},{8,12},{9,13},{10,... | collective-permute-start | bytes 196616 | tf_op jit(solution)/shard_map/ppermute | solution.py:365
  56.2 2.0 %collective-permute-start.14 = (f16[256,512]{1,0:T(8,128)(2,1)S(1)}, f16[256,512]{1,0:T(8,128)(2,1)S(1)}, u32[]{:S(2)}, u32[]{:S(2)}) collective-permute-start(f16[256,512]{1,0:T(8,128)(2,1)S(1)} %pad_maximum_fusion), channel_id=1, source_target_pairs={{0,1},{1,0},{2,3},{3,2},{4,5},{5,4},{6,7},{7,6},{8,9},{9,8},{10,11... | collective-permute-start | bytes 786440 | tf_op jit(solution)/shard_map/ppermute | solution.py:365
  57.9 5.6 %collective-permute-start.16 = (f16[64,512]{1,0:T(8,128)(2,1)S(1)}, f16[64,512]{1,0:T(8,128)(2,1)S(1)}, u32[]{:S(2)}, u32[]{:S(2)}) collective-permute-start(f16[64,512]{1,0:T(8,128)(2,1)S(1)} %add_convert_fusion), channel_id=1, source_target_pairs={{0,8},{1,9},{2,10},{3,11},{4,12},{5,13},{6,14},{7,15},{8,0},{9,1},... | collective-permute-start | bytes 196616 | tf_op jit(solution)/shard_map/ppermute | solution.py:365

commit v7 on v6

--- a/solution.py
+++ b/solution.py
@@ -102,9 +102,11 @@
     return total
 
 
-def value_kernel(blocks, count, earlier, scale, *refs):
+def value_kernel(blocks, count, rows, earlier, scale, *refs):
     rts, refs = refs[:blocks], refs[blocks:]
-    packs, refs = refs[:count], refs[count:]
+    height = rts[0].shape[1] // 2 + TAIL
+    packs = [refs[i].at[r : r + height] for i, r in rows]
+    refs = refs[count:]
     before, refs = refs[:earlier], refs[earlier:]
     sources = [*rts, *before]
     if scale:
@@ -185,14 +187,15 @@
     ]
 
 
-def values_of(rts, packs, lines, before=(), basis=(), scale=None):
+def values_of(rts, packs, lines, before=(), basis=(), scale=None, rows=None):
     own, double = rts[0].shape
     points = packs[0].shape[1]
-    pairs = own * points * len(rts) * len(packs)
+    rows = rows or [(i, 0) for i in range(len(packs))]
+    pairs = own * points * len(rts) * len(rows)
     held = [*rts, *before, *basis]
-    scratch = point_scratch(double, lines, points * len(packs))
+    scratch = point_scratch(double, lines, points * len(rows))
     scratch.append(pltpu.SemaphoreType.DMA((len(held) + 1,)))
-    kernel = functools.partial(value_kernel, len(rts), len(packs), len(before), scale)
+    kernel = functools.partial(value_kernel, len(rts), len(packs), rows, len(before), scale)
     out = HSPEC
     if scale:
         shape = jax.ShapeDtypeStruct((lines, basis[0].shape[0]), F32)
@@ -364,17 +367,23 @@
     def swap(x, mask):
         return lax.ppermute(x, "scen", [(i, i ^ mask) for i in range(n)])
 
-    far = list(range(4, n, 4))
     deep = [4 << i for i in range((n // 4).bit_length() - 1)]
     scale = 1.0 / (math.sqrt(all_points / lines) * scen_total)
     pack, scens0 = packs_of(exposures, guarantees, guar_type, line_ids, returns, drivers)
 
     near = (pack, swap(pack, 1))
     scens1 = swap(scens0, 2)
-    packs = {m: swap(pack, m) for m in far}
+    packs = {m: swap(pack, m) for m in deep}
 
     high0, low0, rt0, v = basis_of(exponents, scens0, near, lines)
     before = [v]
+    packs[4] = after(packs[4], v)
+    relay = swap(packs[4], 1)
+    far = range(8, n, 4)
+    for m in far:
+        if m not in packs:
+            top = max(h for h in deep if h <= m)
+            packs[m] = swap(packs[m ^ top], top)
 
     base = side * 2 + core
     start = jnp.stack([base, base ^ 1])
@@ -382,15 +391,14 @@
         exponents, after(scens1, v), start=start, first=high0
     )
     more = swap(send, 1)
-    relays = {4: swap(after(packs[4], send), 1)}
     v = values_of([rt1], near, lines)
     before.append(v)
     keep, more = after((keep, more), v)
     gram = (keep + more) * (1.0 / scen_total)
 
-    for m in far[1:]:
-        relays[m] = swap(after(packs[m], v), 1)
-    calls = [[packs[m], relays[m]] for m in far[:-1]] + [[packs[far[-1]]], [relays[far[-1]]]]
+    pairs = [(m, m + 4) for m in range(8, n, 8)]
+    calls = [(4,), *pairs, *[(m ^ 1, k ^ 1) for m, k in pairs[:-1]]]
+    calls += [(m ^ 1,) for m in pairs[-1]]
     rts = [rt0, rt1]
     steps, other = list(deep), None
     for i, call in enumerate(calls):
@@ -398,14 +406,19 @@
         if other is not None and (steps or last):
             gram = mine.astype(F32) + after(other, v).astype(F32)
             other = None
+        if i == 1:
+            for m in far:
+                packs[m ^ 1] = swap(after(packs[m], v), 1)
         if steps:
             mine = gram.astype(HALF)
             other = swap(mine, steps.pop(0))
+        call = [packs[m] for m in call] + ([relay] if i == 0 else [])
         call = after(call, gram)
         if not last:
             v = values_of(rts, call, lines, before)
             before = [v]
-    rhs = values_of(rts, call, lines, before, (high0, low0, high1, low1), scale)
+    basis = (high0, low0, high1, low1)
+    rhs = values_of(rts, call, lines, before, basis, scale)
 
     rhs = rhs + swap(rhs, 1)
     for m in [2] + deep:

time: 64.4 us -> 62.3 us (0.967)
  waiting for transfers between devices: 12.3 us -> 10.4 us
    ppermute x17, waiting for transfers between devices: 12.3 us -> 10.4 us  [swap(): return lax.ppermute(x, 'scen', [(i, i ^ mask) for i in range(n)])]
  transfers between devices with their start and end apart: 17 -> 17, of which waited for: 6 -> 6; matrix products, arithmetic and copies ran while one was open for 1% -> 1% of each run, Pallas kernels for 42% -> 43%
where the time goes in v7:
time: 62.3 us; the launch traced here: 62.2 us
  Pallas kernels  33.2 us (53%)
  starting transfers between devices  15.5 us (25%)
  waiting for transfers between devices  10.4 us (17%)
  other arithmetic  1.18 us (2%)
  local copies, waits for them, and re-layouts  1.04 us (2%)
  between operations  0.91 us (1%)
    pallas_call x5, Pallas kernels, values_of(): pl.pallas_call(kernel, in_specs=[HSPEC] * len(rts) + [VSPEC] * len(packs)...  20.9 us
    ppermute x17, starting transfers between devices, swap(): return lax.ppermute(x, 'scen', [(i, i ^ mask) for i in range(n)])  15.5 us
    ppermute x17, waiting for transfers between devices, swap(): return lax.ppermute(x, 'scen', [(i, i ^ mask) for i in range(n)])  10.4 us
    pallas_call x1, Pallas kernels, basis_of(): pl.pallas_call(first_kernel, in_specs=[VSPEC] * 2 + [HSPEC] * 2, out_spec...  5.18 us
    pallas_call x1, Pallas kernels, basis_of(): pl.pallas_call(gram_kernel, in_specs=[SSPEC, VSPEC, VSPEC, HSPEC], out_sp...  3.53 us
    pallas_call x1, Pallas kernels, packs_of(): pl.pallas_call(pack_kernel, in_specs=[pl.BlockSpec(memory_space=pltpu.HBM...  1.99 us
    pallas_call x1, Pallas kernels, placed(): pl.pallas_call(functools.partial(place_kernel, blocks), in_specs=[pl.Bloc...  1.59 us
  transfers between devices with their start and end apart: 17, of which 6 were waited for; matrix products, arithmetic and copies ran while one was open for 1% of the time, Pallas kernels for 43%

profile of v7, /device:TPU:0, one launch (start us, length us, event | category | flops | bytes accessed | tf_op | source)
XLA Modules:
  0.0 62.2 jit_solution(13880116517532525591)
XLA Ops:
  0.6 2.0 %shard_map.86 = (bf16[80,1024]{1,0:T(8,128)(2,1)}, bf16[144,1024]{1,0:T(8,128)(2,1)}) custom-call(bf16[64,1024]{1,0:T(8,128)(2,1)} %bitcast.10, f32[1,1024]{1,0:T(1,128)} %bitcast.11, s32[1,1024]{1,0:T(1,128)} %bitcast.12, s32[1,1024]{1,0:T(1,128)} %bitcast.13, bf16[64,1024]{1,0:T(8,128)(2,1)} %refs_4_.1, f32[40,1024]{1,0:T(8,128)} %refs_5_.1), custom_call_target="tpu_custom_call" | custom-call | flops 1048576 | bytes 1048576 | tf_op jit(solution)/shard_map/pallas_call | solution.py:63
  2.7 0.5 collective-permute-start.1
  3.2 2.6 %collective-permute-start.4 = (bf16[80,1024]{1,0:T(8,128)(2,1)}, bf16[80,1024]{1,0:T(8,128)(2,1)S(1)}, u32[]{:S(2)}, u32[]{:S(2)}) collective-permute-start(bf16[80,1024]{1,0:T(8,128)(2,1)} %get-tuple-element.30.p0.refs_0_), channel_id=1, source_target_pairs={{0,4},{1,5},{2,6},{3,7},{4,0},{5,1},{6,2},{7,3},{8,12},{9,13},{10,... | collective-permute-start | bytes 491528 | tf_op jit(solution)/shard_map/ppermute | solution.py:368
  5.8 2.6 %collective-permute-start.7 = (bf16[80,1024]{1,0:T(8,128)(2,1)}, bf16[80,1024]{1,0:T(8,128)(2,1)S(1)}, u32[]{:S(2)}, u32[]{:S(2)}) collective-permute-start(bf16[80,1024]{1,0:T(8,128)(2,1)} %get-tuple-element.30.p0.refs_0_), channel_id=1, source_target_pairs={{0,8},{1,9},{2,10},{3,11},{4,12},{5,13},{6,14},{7,15},{8,0},{9,1},... | collective-permute-start | bytes 491528 | tf_op jit(solution)/shard_map/ppermute | solution.py:368
  8.4 1.5 %collective-permute-start = (bf16[144,1024]{1,0:T(8,128)(2,1)}, bf16[144,1024]{1,0:T(8,128)(2,1)S(1)}, u32[]{:S(2)}, u32[]{:S(2)}) collective-permute-start(bf16[144,1024]{1,0:T(8,128)(2,1)} %get-tuple-element.29.scens), channel_id=1, source_target_pairs={{0,2},{1,3},{2,0},{3,1},{4,6},{5,7},{6,4},{7,5},{8,10},{9,11},{10,... | collective-permute-start | bytes 884744 | tf_op jit(solution)/shard_map/ppermute | solution.py:368
  10.0 0.1 copy.10.exps
  10.2 0.9 %copy-done.1 = bf16[80,1024]{1,0:T(8,128)(2,1)S(1)} copy-done((bf16[80,1024]{1,0:T(8,128)(2,1)S(1)}, bf16[80,1024]{1,0:T(8,128)(2,1)}, u32[]{:S(2)}) %copy-start.1) | copy-done | bytes 163864
  11.1 5.2 %shard_map.87 = (bf16[512,1024]{1,0:T(8,128)(2,1)S(1)}, bf16[512,1024]{1,0:T(8,128)(2,1)S(1)}, bf16[1024,128]{1,0:T(8,128)(2,1)S(1)}, f32[1024,64]{1,0:T(8,128)S(1)}) custom-call(s32[512,40]{1,0:T(8,128)S(1)} %copy.10.exps, bf16[144,1024]{1,0:T(8,128)(2,1)S(1)} %copy-done, bf16[80,1024]{1,0:T(8,128)(2,1)S(1)} %copy-done.1, ...), custom_call_target="tpu_custom_call" | custom-call | flops 3000000000 | bytes 3145728 | tf_op jit(solution)/shard_map/pallas_call | solution.py:307
  16.4 0.4 collective-permute-start.9
  16.8 0.7 %collective-permute-done.scens = bf16[144,1024]{1,0:T(8,128)(2,1)S(1)} collective-permute-done((bf16[144,1024]{1,0:T(8,128)(2,1)}, bf16[144,1024]{1,0:T(8,128)(2,1)S(1)}, u32[]{:S(2)}, u32[]{:S(2)}) %collective-permute-start) | collective-permute-done | bytes 294944 | tf_op jit(solution)/shard_map/ppermute | solution.py:368
  17.4 3.5 %shard_map.88 = (bf16[512,1024]{1,0:T(8,128)(2,1)S(1)}, bf16[512,1024]{1,0:T(8,128)(2,1)S(1)}, bf16[1024,128]{1,0:T(8,128)(2,1)S(1)}, f32[128,512]{1,0:T(8,128)S(1)}, f32[128,512]{1,0:T(8,128)S(1)}) custom-call(s32[2]{0:T(128)S(1)} %pad_add_fusion.1.start, s32[512,40]{1,0:T(8,128)S(1)} %copy.10.exps, bf16[144,1024]{1,0:T(8,128)(2,1)S(1)} %collective-permute-done.scens, ...), custom_call_target="tpu_custom_call" | custom-call | flops 3000000000 | bytes 3145728 | tf_op jit(solution)/shard_map/pallas_call | solution.py:320
  21.0 3.2 %shard_map.89.refs_5_ = f32[1024,64]{1,0:T(8,128)S(1)} custom-call(bf16[1024,128]{1,0:T(8,128)(2,1)S(1)} %get-tuple-element.36.rt.refs_1_, bf16[80,1024]{1,0:T(8,128)(2,1)S(1)} %copy-done.1, bf16[80,1024]{1,0:T(8,128)(2,1)S(1)} %collective-permute-done.1.p1.refs_1_), custom_call_target="tpu_custom_call" | custom-call | flops 3565158400 | bytes 1048576 | tf_op jit(solution)/shard_map/pallas_call | solution.py:208
  24.3 0.5 collective-permute-start.3
  24.8 5.2 %shard_map.90.refs_4_ = f32[1024,128]{1,0:T(8,128)S(1)} custom-call(bf16[1024,128]{1,0:T(8,128)(2,1)S(1)} %get-tuple-element.39.refs_0_, bf16[1024,128]{1,0:T(8,128)(2,1)S(1)} %get-tuple-element.36.rt.refs_1_, bf16[80,1024]{1,0:T(8,128)(2,1)S(1)} %collective-permute-done.4.refs_2_, bf16[80,1024]{1,0:T(8,128)(2,1)S(1)} %collective-permute-done.5.refs_3_, ...), custom_call_target="tpu_custom_call" | custom-call | flops 7130316800 | bytes 1048576 | tf_op jit(solution)/shard_map/pallas_call | solution.py:208
  30.0 0.3 collective-permute-start.10
  30.3 0.3 collective-permute-start.8
  30.6 2.1 %collective-permute-start.6 = (f16[128,512]{1,0:T(8,128)(2,1)S(1)}, f16[128,512]{1,0:T(8,128)(2,1)S(1)}, u32[]{:S(2)}, u32[]{:S(2)}) collective-permute-start(f16[128,512]{1,0:T(8,128)(2,1)S(1)} %fusion.1), channel_id=1, source_target_pairs={{0,8},{1,9},{2,10},{3,11},{4,12},{5,13},{6,14},{7,15},{8,0},{9,1},... | collective-permute-start | bytes 393224 | tf_op jit(solution)/shard_map/ppermute | solution.py:368
  32.8 5.1 %shard_map.91.refs_3_ = f32[1024,128]{1,0:T(8,128)S(1)} custom-call(bf16[1024,128]{1,0:T(8,128)(2,1)S(1)} %get-tuple-element.39.refs_0_, bf16[1024,128]{1,0:T(8,128)(2,1)S(1)} %get-tuple-element.36.rt.refs_1_, bf16[80,1024]{1,0:T(8,128)(2,1)S(1)} %collective-permute-done.7.refs_2_, bf16[80,1024]{1,0:T(8,128)(2,1)S(1)} %collective-permute-done.9.refs_3_, ...), custom_call_target="tpu_custom_call" | custom-call | flops 7130316800 | bytes 1048576 | tf_op jit(solution)/shard_map/pallas_call | solution.py:208
  37.9 3.1 %shard_map.92.refs_3_ = f32[1024,128]{1,0:T(8,128)S(1)} custom-call(bf16[1024,128]{1,0:T(8,128)(2,1)S(1)} %get-tuple-element.39.refs_0_, bf16[1024,128]{1,0:T(8,128)(2,1)S(1)} %get-tuple-element.36.rt.refs_1_, bf16[80,1024]{1,0:T(8,128)(2,1)S(1)} %collective-permute-done.8.refs_2_, f32[1024,128]{1,0:T(8,128)S(1)} %shard_map.91.refs_3_), custom_call_target="tpu_custom_call" | custom-call | flops 3565158400 | bytes 1048576 | tf_op jit(solution)/shard_map/pallas_call | solution.py:208
  41.1 4.3 %shard_map.93 = f32[64,512]{1,0:T(8,128)S(1)} custom-call(bf16[1024,128]{1,0:T(8,128)(2,1)S(1)} %get-tuple-element.39.refs_0_, bf16[1024,128]{1,0:T(8,128)(2,1)S(1)} %get-tuple-element.36.rt.refs_1_, bf16[80,1024]{1,0:T(8,128)(2,1)S(1)} %collective-permute-done.10.refs_2_, f32[1024,128]{1,0:T(8,128)S(1)} %shard_map.92.refs_3_, ...), custom_call_target="tpu_custom_call" | custom-call | flops 3565158400 | bytes 1048576 | tf_op jit(solution)/shard_map/pallas_call | solution.py:208
  45.5 1.3 %collective-permute-done.11 = f32[64,512]{1,0:T(8,128)S(1)} collective-permute-done((f32[64,512]{1,0:T(8,128)S(1)}, f32[64,512]{1,0:T(8,128)S(1)}, u32[]{:S(2)}, u32[]{:S(2)}) %collective-permute-start.11) | collective-permute-done | bytes 131104 | tf_op jit(solution)/shard_map/ppermute | solution.py:368
  46.9 0.6 collective-permute-start.12
  47.5 1.6 %collective-permute-start.13 = (f16[128,512]{1,0:T(8,128)(2,1)S(1)}, f16[128,512]{1,0:T(8,128)(2,1)S(1)}, u32[]{:S(2)}, u32[]{:S(2)}) collective-permute-start(f16[128,512]{1,0:T(8,128)(2,1)S(1)} %get-tuple-element.57), channel_id=1, source_target_pairs={{0,2},{1,3},{2,0},{3,1},{4,6},{5,7},{6,4},{7,5},{8,10},{9,11},{10,... | collective-permute-start | bytes 393224 | tf_op jit(solution)/shard_map/ppermute | solution.py:368
  49.1 2.8 %collective-permute-done.12 = f16[64,512]{1,0:T(8,128)(2,1)S(1)} collective-permute-done((f16[64,512]{1,0:T(8,128)(2,1)S(1)}, f16[64,512]{1,0:T(8,128)(2,1)S(1)}, u32[]{:S(2)}, u32[]{:S(2)}) %collective-permute-start.12) | collective-permute-done | bytes 65568 | tf_op jit(solution)/shard_map/ppermute | solution.py:368
  51.9 1.6 %collective-permute-start.15 = (f16[64,512]{1,0:T(8,128)(2,1)S(1)}, f16[64,512]{1,0:T(8,128)(2,1)S(1)}, u32[]{:S(2)}, u32[]{:S(2)}) collective-permute-start(f16[64,512]{1,0:T(8,128)(2,1)S(1)} %fusion), channel_id=1, source_target_pairs={{0,4},{1,5},{2,6},{3,7},{4,0},{5,1},{6,2},{7,3},{8,12},{9,13},{10,... | collective-permute-start | bytes 196616 | tf_op jit(solution)/shard_map/ppermute | solution.py:368
  53.5 0.3 collective-permute-done.13
  54.0 2.2 %collective-permute-done.15 = f16[64,512]{1,0:T(8,128)(2,1)S(1)} collective-permute-done((f16[64,512]{1,0:T(8,128)(2,1)S(1)}, f16[64,512]{1,0:T(8,128)(2,1)S(1)}, u32[]{:S(2)}, u32[]{:S(2)}) %collective-permute-start.15) | collective-permute-done | bytes 65568 | tf_op jit(solution)/shard_map/ppermute | solution.py:368
  56.3 0.5 collective-permute-start.16
  56.7 0.1 pad_add_fusion.refs_0_
  56.9 1.6 %shard_map.94 = f32[512,512]{1,0:T(8,128)} custom-call(s32[4]{0:T(128)S(1)} %pad_add_fusion.refs_0_, f32[128,512]{1,0:T(8,128)S(1)} %get-tuple-element.56.refs_1_, f32[128,512]{1,0:T(8,128)S(1)} %convert_element_type.68.refs_2_, f32[256,512]{1,0:T(8,128)S(1)} %convert_element_type.69.refs_3_), custom_call_target="tpu_custom_call" | custom-call | flops 1048576 | bytes 2097152 | tf_op jit(solution)/shard_map/pallas_call | solution.py:343
  58.5 3.0 %collective-permute-done.16 = f16[64,512]{1,0:T(8,128)(2,1)S(1)} collective-permute-done((f16[64,512]{1,0:T(8,128)(2,1)S(1)}, f16[64,512]{1,0:T(8,128)(2,1)S(1)}, u32[]{:S(2)}, u32[]{:S(2)}) %collective-permute-start.16) | collective-permute-done | bytes 65568 | tf_op jit(solution)/shard_map/ppermute | solution.py:368
  61.5 0.7 %add_bitcast_fusion = f32[512,64]{0,1:T(8,128)} fusion(f16[64,512]{1,0:T(8,128)(2,1)S(1)} %collective-permute-done.16, f16[64,512]{1,0:T(8,128)(2,1)S(1)} %add_convert_fusion), kind=kLoop, calls=%fused_computation.4 | loop fusion | flops 98304 | bytes 262144 | tf_op jit(solution)/shard_map/transpose | solution.py:436
  (31 shorter events, 0.8 us)
Async XLA Ops:
  0.6 9.4 %copy-start.2 = (s32[512,40]{0,1:T(8,128)S(1)}, s32[512,40]{0,1:T(8,128)}, u32[]{:S(2)}) copy-start(s32[512,40]{0,1:T(8,128)} %param.13) | copy-start | bytes 245764
  2.6 7.5 %copy-start = (bf16[144,1024]{1,0:T(8,128)(2,1)S(1)}, bf16[144,1024]{1,0:T(8,128)(2,1)}, u32[]{:S(2)}) copy-start(bf16[144,1024]{1,0:T(8,128)(2,1)} %get-tuple-element.29.scens) | copy-start | bytes 884740
  2.7 7.5 %collective-permute-start.1 = (bf16[80,1024]{1,0:T(8,128)(2,1)}, bf16[80,1024]{1,0:T(8,128)(2,1)S(1)}, u32[]{:S(2)}, u32[]{:S(2)}) collective-permute-start(bf16[80,1024]{1,0:T(8,128)(2,1)} %get-tuple-element.30.p0.refs_0_), channel_id=1, source_target_pairs={{0,1},{1,0},{2,3},{3,2},{4,5},{5,4},{6,7},{7,6},{8,9},{9,8},{10,11... | collective-permute-start | bytes 491528 | tf_op jit(solution)/shard_map/ppermute | solution.py:368
  3.2 13.1 %collective-permute-start.4 = (bf16[80,1024]{1,0:T(8,128)(2,1)}, bf16[80,1024]{1,0:T(8,128)(2,1)S(1)}, u32[]{:S(2)}, u32[]{:S(2)}) collective-permute-start(bf16[80,1024]{1,0:T(8,128)(2,1)} %get-tuple-element.30.p0.refs_0_), channel_id=1, source_target_pairs={{0,4},{1,5},{2,6},{3,7},{4,0},{5,1},{6,2},{7,3},{8,12},{9,13},{10,... | collective-permute-start | bytes 491528 | tf_op jit(solution)/shard_map/ppermute | solution.py:368
  5.8 24.5 %collective-permute-start.7 = (bf16[80,1024]{1,0:T(8,128)(2,1)}, bf16[80,1024]{1,0:T(8,128)(2,1)S(1)}, u32[]{:S(2)}, u32[]{:S(2)}) collective-permute-start(bf16[80,1024]{1,0:T(8,128)(2,1)} %get-tuple-element.30.p0.refs_0_), channel_id=1, source_target_pairs={{0,8},{1,9},{2,10},{3,11},{4,12},{5,13},{6,14},{7,15},{8,0},{9,1},... | collective-permute-start | bytes 491528 | tf_op jit(solution)/shard_map/ppermute | solution.py:368
  8.4 9.0 %collective-permute-start = (bf16[144,1024]{1,0:T(8,128)(2,1)}, bf16[144,1024]{1,0:T(8,128)(2,1)S(1)}, u32[]{:S(2)}, u32[]{:S(2)}) collective-permute-start(bf16[144,1024]{1,0:T(8,128)(2,1)} %get-tuple-element.29.scens), channel_id=1, source_target_pairs={{0,2},{1,3},{2,0},{3,1},{4,6},{5,7},{6,4},{7,5},{8,10},{9,11},{10,... | collective-permute-start | bytes 884744 | tf_op jit(solution)/shard_map/ppermute | solution.py:368
  10.2 0.9 %copy-start.1 = (bf16[80,1024]{1,0:T(8,128)(2,1)S(1)}, bf16[80,1024]{1,0:T(8,128)(2,1)}, u32[]{:S(2)}) copy-start(bf16[80,1024]{1,0:T(8,128)(2,1)} %get-tuple-element.30.p0.refs_0_) | copy-start | bytes 491524
  16.3 8.0 %collective-permute-start.5 = (bf16[80,1024]{1,0:T(8,128)(2,1)S(1)}, bf16[80,1024]{1,0:T(8,128)(2,1)S(1)}, u32[]{:S(2)}, u32[]{:S(2)}) collective-permute-start(bf16[80,1024]{1,0:T(8,128)(2,1)S(1)} %collective-permute-done.4.refs_2_), channel_id=1, source_target_pairs={{0,1},{1,0},{2,3},{3,2},{4,5},{5,4},{6,7},{7,6},{8,9},{9,8},{10,11... | collective-permute-start | bytes 491528 | tf_op jit(solution)/shard_map/ppermute | solution.py:368
  16.4 13.7 %collective-permute-start.9 = (bf16[80,1024]{1,0:T(8,128)(2,1)S(1)}, bf16[80,1024]{1,0:T(8,128)(2,1)S(1)}, u32[]{:S(2)}, u32[]{:S(2)}) collective-permute-start(bf16[80,1024]{1,0:T(8,128)(2,1)S(1)} %collective-permute-done.4.refs_2_), channel_id=1, source_target_pairs={{0,8},{1,9},{2,10},{3,11},{4,12},{5,13},{6,14},{7,15},{8,0},{9,1},... | collective-permute-start | bytes 491528 | tf_op jit(solution)/shard_map/ppermute | solution.py:368
  21.0 3.3 %collective-permute-start.2 = (f32[128,512]{1,0:T(8,128)S(1)}, f32[128,512]{1,0:T(8,128)S(1)}, u32[]{:S(2)}, u32[]{:S(2)}) collective-permute-start(f32[128,512]{1,0:T(8,128)S(1)} %get-tuple-element.35), channel_id=1, source_target_pairs={{0,1},{1,0},{2,3},{3,2},{4,5},{5,4},{6,7},{7,6},{8,9},{9,8},{10,11... | collective-permute-start | bytes 786440 | tf_op jit(solution)/shard_map/ppermute | solution.py:368
  24.3 6.3 %collective-permute-start.3 = (f16[128,512]{1,0:T(8,128)(2,1)S(1)}, f16[128,512]{1,0:T(8,128)(2,1)S(1)}, u32[]{:S(2)}, u32[]{:S(2)}) collective-permute-start(f16[128,512]{1,0:T(8,128)(2,1)S(1)} %fusion.3), channel_id=1, source_target_pairs={{0,4},{1,5},{2,6},{3,7},{4,0},{5,1},{6,2},{7,3},{8,12},{9,13},{10,... | collective-permute-start | bytes 393224 | tf_op jit(solution)/shard_map/ppermute | solution.py:368
  30.0 11.1 %collective-permute-start.10 = (bf16[80,1024]{1,0:T(8,128)(2,1)S(1)}, bf16[80,1024]{1,0:T(8,128)(2,1)S(1)}, u32[]{:S(2)}, u32[]{:S(2)}) collective-permute-start(bf16[80,1024]{1,0:T(8,128)(2,1)S(1)} %collective-permute-done.9.refs_3_), channel_id=1, source_target_pairs={{0,1},{1,0},{2,3},{3,2},{4,5},{5,4},{6,7},{7,6},{8,9},{9,8},{10,11... | collective-permute-start | bytes 491528 | tf_op jit(solution)/shard_map/ppermute | solution.py:368
  30.3 7.6 %collective-permute-start.8 = (bf16[80,1024]{1,0:T(8,128)(2,1)S(1)}, bf16[80,1024]{1,0:T(8,128)(2,1)S(1)}, u32[]{:S(2)}, u32[]{:S(2)}) collective-permute-start(bf16[80,1024]{1,0:T(8,128)(2,1)S(1)} %collective-permute-done.7.refs_2_), channel_id=1, source_target_pairs={{0,1},{1,0},{2,3},{3,2},{4,5},{5,4},{6,7},{7,6},{8,9},{9,8},{10,11... | collective-permute-start | bytes 491528 | tf_op jit(solution)/shard_map/ppermute | solution.py:368
  30.6 10.4 %collective-permute-start.6 = (f16[128,512]{1,0:T(8,128)(2,1)S(1)}, f16[128,512]{1,0:T(8,128)(2,1)S(1)}, u32[]{:S(2)}, u32[]{:S(2)}) collective-permute-start(f16[128,512]{1,0:T(8,128)(2,1)S(1)} %fusion.1), channel_id=1, source_target_pairs={{0,8},{1,9},{2,10},{3,11},{4,12},{5,13},{6,14},{7,15},{8,0},{9,1},... | collective-permute-start | bytes 393224 | tf_op jit(solution)/shard_map/ppermute | solution.py:368
  45.4 1.4 %collective-permute-start.11 = (f32[64,512]{1,0:T(8,128)S(1)}, f32[64,512]{1,0:T(8,128)S(1)}, u32[]{:S(2)}, u32[]{:S(2)}) collective-permute-start(f32[64,512]{1,0:T(8,128)S(1)} %shard_map.93), channel_id=1, source_target_pairs={{0,1},{1,0},{2,3},{3,2},{4,5},{5,4},{6,7},{7,6},{8,9},{9,8},{10,11... | collective-permute-start | bytes 393224 | tf_op jit(solution)/shard_map/ppermute | solution.py:368
  46.9 5.0 %collective-permute-start.12 = (f16[64,512]{1,0:T(8,128)(2,1)S(1)}, f16[64,512]{1,0:T(8,128)(2,1)S(1)}, u32[]{:S(2)}, u32[]{:S(2)}) collective-permute-start(f16[64,512]{1,0:T(8,128)(2,1)S(1)} %add_convert_fusion.1), channel_id=1, source_target_pairs={{0,2},{1,3},{2,0},{3,1},{4,6},{5,7},{6,4},{7,5},{8,10},{9,11},{10,... | collective-permute-start | bytes 196616 | tf_op jit(solution)/shard_map/ppermute | solution.py:368
  47.5 6.4 %collective-permute-start.13 = (f16[128,512]{1,0:T(8,128)(2,1)S(1)}, f16[128,512]{1,0:T(8,128)(2,1)S(1)}, u32[]{:S(2)}, u32[]{:S(2)}) collective-permute-start(f16[128,512]{1,0:T(8,128)(2,1)S(1)} %get-tuple-element.57), channel_id=1, source_target_pairs={{0,2},{1,3},{2,0},{3,1},{4,6},{5,7},{6,4},{7,5},{8,10},{9,11},{10,... | collective-permute-start | bytes 393224 | tf_op jit(solution)/shard_map/ppermute | solution.py:368
  51.9 4.3 %collective-permute-start.15 = (f16[64,512]{1,0:T(8,128)(2,1)S(1)}, f16[64,512]{1,0:T(8,128)(2,1)S(1)}, u32[]{:S(2)}, u32[]{:S(2)}) collective-permute-start(f16[64,512]{1,0:T(8,128)(2,1)S(1)} %fusion), channel_id=1, source_target_pairs={{0,4},{1,5},{2,6},{3,7},{4,0},{5,1},{6,2},{7,3},{8,12},{9,13},{10,... | collective-permute-start | bytes 196616 | tf_op jit(solution)/shard_map/ppermute | solution.py:368
  54.0 2.9 %collective-permute-start.14 = (f16[256,512]{1,0:T(8,128)(2,1)S(1)}, f16[256,512]{1,0:T(8,128)(2,1)S(1)}, u32[]{:S(2)}, u32[]{:S(2)}) collective-permute-start(f16[256,512]{1,0:T(8,128)(2,1)S(1)} %pad_maximum_fusion), channel_id=1, source_target_pairs={{0,1},{1,0},{2,3},{3,2},{4,5},{5,4},{6,7},{7,6},{8,9},{9,8},{10,11... | collective-permute-start | bytes 786440 | tf_op jit(solution)/shard_map/ppermute | solution.py:368
  56.3 5.2 %collective-permute-start.16 = (f16[64,512]{1,0:T(8,128)(2,1)S(1)}, f16[64,512]{1,0:T(8,128)(2,1)S(1)}, u32[]{:S(2)}, u32[]{:S(2)}) collective-permute-start(f16[64,512]{1,0:T(8,128)(2,1)S(1)} %add_convert_fusion), channel_id=1, source_target_pairs={{0,8},{1,9},{2,10},{3,11},{4,12},{5,13},{6,14},{7,15},{8,0},{9,1},... | collective-permute-start | bytes 196616 | tf_op jit(solution)/shard_map/ppermute | solution.py:368

commit v8 on v7

--- a/solution.py
+++ b/solution.py
@@ -11,6 +11,8 @@
 LINES = 64
 TAIL = 16
 CHUNK = 512
+ROWS = 256
+TILE = 2**18
 LOG2E = 1.4426950408889634
 BF = jnp.bfloat16
 F32 = jnp.float32
@@ -89,17 +91,12 @@
         oh[:, at] = (label == tail[3:4]).astype(BF)
 
 
-def chunk_values(r, w, oh, lev, step):
-    total = None
-    for j in range(0, w.shape[1], step):
-        at = slice(j, j + step)
-        power = jnp.dot(r, w[:, at], preferred_element_type=F32)
-        payoff = jnp.maximum(lev[:, at] - jnp.exp2(power), 0.0).astype(BF)
-        part = lax.dot_general(
-            payoff, oh[:, at], (((1,), (1,)), ((), ())), preferred_element_type=F32
-        )
-        total = part if total is None else total + part
-    return total
+def chunk_values(r, w, oh, lev):
+    power = jnp.dot(r, w[...], preferred_element_type=F32)
+    payoff = jnp.maximum(lev[...] - jnp.exp2(power), 0.0).astype(BF)
+    return lax.dot_general(
+        payoff, oh[...], (((1,), (1,)), ((), ())), preferred_element_type=F32
+    )
 
 
 def value_kernel(blocks, count, rows, earlier, scale, *refs):
@@ -108,39 +105,35 @@
     packs = [refs[i].at[r : r + height] for i, r in rows]
     refs = refs[count:]
     before, refs = refs[:earlier], refs[earlier:]
-    sources = [*rts, *before]
+    sources = list(rts)
     if scale:
         basis, refs = refs[: 2 * blocks], refs[2 * blocks :]
         out, w, oh, lev, sems, *held = refs
         sources += basis
     else:
-        out, w, oh, lev, sems, sums, *held = refs
+        out, w, oh, lev, sems, *held = refs
     loads = [pltpu.make_async_copy(a, b, sems.at[i]) for i, (a, b) in enumerate(zip(sources, held))]
     for load in loads:
         load.start()
     own = rts[0].shape[0]
-    points = packs[0].shape[1]
     lines = oh.shape[0]
     prepare(packs, w, oh, lev)
     for load in loads[:blocks]:
         load.wait()
     totals = [
         [
-            chunk_values(held[i][s0 : s0 + CHUNK, :], w, oh, lev, points)
-            for s0 in range(0, own, CHUNK)
+            chunk_values(held[i][s0 : s0 + ROWS, :], w, oh, lev)
+            for s0 in range(0, own, ROWS)
         ]
         for i in range(blocks)
     ]
     for load in loads[blocks:]:
         load.wait()
-    before, basis = held[blocks : blocks + earlier], held[blocks + earlier :]
+    basis = held[blocks:]
     totals = [jnp.concatenate(t, axis=0) for t in totals]
     if not scale:
-        sums[:, :lines] = totals[0] + before[0][:, :lines]
-        sums[:, lines:] = totals[1] + before[-1][:, -lines:]
-        store = pltpu.make_async_copy(sums, out, sems.at[len(sources)])
-        store.start()
-        store.wait()
+        out[:, :lines] = totals[0] + before[0][:, :lines]
+        out[:, lines:] = totals[1] + before[-1][:, -lines:]
         return
     result = None
     for i in range(blocks):
@@ -156,18 +149,14 @@
 
 
 def plain_kernel(rt, *refs):
-    packs, (out, w, oh, lev, sems, sums, held) = refs[:-7], refs[-7:]
+    packs, (out, w, oh, lev, sems, held) = refs[:-6], refs[-6:]
     load = pltpu.make_async_copy(rt, held, sems.at[0])
     load.start()
     prepare(packs, w, oh, lev)
     load.wait()
-    for s0 in range(0, rt.shape[0], CHUNK):
-        sums[s0 : s0 + CHUNK, :] = chunk_values(
-            held[s0 : s0 + CHUNK, :], w, oh, lev, packs[0].shape[1]
-        )
-    store = pltpu.make_async_copy(sums, out, sems.at[1])
-    store.start()
-    store.wait()
+    rows = TILE // w.shape[1]
+    for s0 in range(0, rt.shape[0], rows):
+        out[s0 : s0 + rows, :] = chunk_values(held[s0 : s0 + rows, :], w, oh, lev)
 
 
 VSPEC = pl.BlockSpec(memory_space=pltpu.VMEM)
@@ -192,25 +181,22 @@
     points = packs[0].shape[1]
     rows = rows or [(i, 0) for i in range(len(packs))]
     pairs = own * points * len(rts) * len(rows)
-    held = [*rts, *before, *basis]
+    held = [*rts, *basis]
     scratch = point_scratch(double, lines, points * len(rows))
-    scratch.append(pltpu.SemaphoreType.DMA((len(held) + 1,)))
+    scratch.append(pltpu.SemaphoreType.DMA((len(held),)))
     kernel = functools.partial(value_kernel, len(rts), len(packs), rows, len(before), scale)
-    out = HSPEC
     if scale:
         shape = jax.ShapeDtypeStruct((lines, basis[0].shape[0]), F32)
-        out = VSPEC
     else:
         shape = jax.ShapeDtypeStruct((own, lines * len(rts)), F32)
-        scratch += like([shape])
     if not before:
         kernel = plain_kernel
     return pl.pallas_call(
         kernel,
         in_specs=[HSPEC] * len(rts)
-        + [VSPEC] * len(packs)
-        + [HSPEC] * (len(before) + len(basis)),
-        out_specs=out,
+        + [VSPEC] * (len(packs) + len(before))
+        + [HSPEC] * len(basis),
+        out_specs=VSPEC,
         out_shape=shape,
         scratch_shapes=scratch + like(held),
         compiler_params=params(),
@@ -261,11 +247,9 @@
     for load in loads:
         load.wait()
     prepare([packs.at[0], packs.at[1]], w, oh, lev)
-    points = packs.shape[2]
-    for s0 in range(0, held[2].shape[0], CHUNK):
-        held[3][s0 : s0 + CHUNK, :] = chunk_values(
-            held[2][s0 : s0 + CHUNK, :], w, oh, lev, points
-        )
+    rows = TILE // w.shape[1]
+    for s0 in range(0, held[2].shape[0], rows):
+        held[3][s0 : s0 + rows, :] = chunk_values(held[2][s0 : s0 + rows, :], w, oh, lev)
     stores[3].start()
     for store in stores:
         store.wait()

time: 62.3 us -> 60 us (0.963)
  Pallas kernels: 33.2 us -> 30.9 us
    pallas_call x5, Pallas kernels: 20.9 us -> 19.4 us  [values_of(): pl.pallas_call(kernel, in_specs=[HSPEC] * len(rts) + [VSPEC] * (len(packs...]
    pallas_call x1, Pallas kernels: 5.18 us -> 4.41 us  [basis_of(): pl.pallas_call(first_kernel, in_specs=[VSPEC] * 2 + [HSPEC] * 2, out_spec...]
  transfers between devices with their start and end apart: 17 -> 17, of which waited for: 6 -> 7; matrix products, arithmetic and copies ran while one was open for 1% -> 1% of each run, Pallas kernels for 43% -> 41%
where the time goes in v8:
time: 60 us; the launch traced here: 59.9 us
  Pallas kernels  30.9 us (52%)
  starting transfers between devices  15.5 us (26%)
  waiting for transfers between devices  10.3 us (17%)
  other arithmetic  1.17 us (2%)
  local copies, waits for them, and re-layouts  1.04 us (2%)
  between operations  0.9 us (2%)
    pallas_call x5, Pallas kernels, values_of(): pl.pallas_call(kernel, in_specs=[HSPEC] * len(rts) + [VSPEC] * (len(packs...  19.4 us
    ppermute x17, starting transfers between devices, swap(): return lax.ppermute(x, 'scen', [(i, i ^ mask) for i in range(n)])  15.5 us
    ppermute x17, waiting for transfers between devices, swap(): return lax.ppermute(x, 'scen', [(i, i ^ mask) for i in range(n)])  10.3 us
    pallas_call x1, Pallas kernels, basis_of(): pl.pallas_call(first_kernel, in_specs=[VSPEC] * 2 + [HSPEC] * 2, out_spec...  4.41 us
    pallas_call x1, Pallas kernels, basis_of(): pl.pallas_call(gram_kernel, in_specs=[SSPEC, VSPEC, VSPEC, HSPEC], out_sp...  3.53 us
    pallas_call x1, Pallas kernels, packs_of(): pl.pallas_call(pack_kernel, in_specs=[pl.BlockSpec(memory_space=pltpu.HBM...  1.99 us
    pallas_call x1, Pallas kernels, placed(): pl.pallas_call(functools.partial(place_kernel, blocks), in_specs=[pl.Bloc...  1.59 us
  transfers between devices with their start and end apart: 17, of which 7 were waited for; matrix products, arithmetic and copies ran while one was open for 1% of the time, Pallas kernels for 41%

profile of v8, /device:TPU:0, one launch (start us, length us, event | category | flops | bytes accessed | tf_op | source)
XLA Modules:
  0.0 59.9 jit_solution(9365707633887882490)
XLA Ops:
  0.6 2.0 %shard_map.86 = (bf16[80,1024]{1,0:T(8,128)(2,1)}, bf16[144,1024]{1,0:T(8,128)(2,1)}) custom-call(bf16[64,1024]{1,0:T(8,128)(2,1)} %bitcast.10, f32[1,1024]{1,0:T(1,128)} %bitcast.11, s32[1,1024]{1,0:T(1,128)} %bitcast.12, s32[1,1024]{1,0:T(1,128)} %bitcast.13, bf16[64,1024]{1,0:T(8,128)(2,1)} %refs_4_.1, f32[40,1024]{1,0:T(8,128)} %refs_5_.1), custom_call_target="tpu_custom_call" | custom-call | flops 1048576 | bytes 1048576 | tf_op jit(solution)/shard_map/pallas_call | solution.py:65
  2.7 0.5 collective-permute-start.1
  3.2 2.6 %collective-permute-start.4 = (bf16[80,1024]{1,0:T(8,128)(2,1)}, bf16[80,1024]{1,0:T(8,128)(2,1)S(1)}, u32[]{:S(2)}, u32[]{:S(2)}) collective-permute-start(bf16[80,1024]{1,0:T(8,128)(2,1)} %get-tuple-element.30.p0.refs_0_), channel_id=1, source_target_pairs={{0,4},{1,5},{2,6},{3,7},{4,0},{5,1},{6,2},{7,3},{8,12},{9,13},{10,... | collective-permute-start | bytes 491528 | tf_op jit(solution)/shard_map/ppermute | solution.py:352
  5.8 2.6 %collective-permute-start.7 = (bf16[80,1024]{1,0:T(8,128)(2,1)}, bf16[80,1024]{1,0:T(8,128)(2,1)S(1)}, u32[]{:S(2)}, u32[]{:S(2)}) collective-permute-start(bf16[80,1024]{1,0:T(8,128)(2,1)} %get-tuple-element.30.p0.refs_0_), channel_id=1, source_target_pairs={{0,8},{1,9},{2,10},{3,11},{4,12},{5,13},{6,14},{7,15},{8,0},{9,1},... | collective-permute-start | bytes 491528 | tf_op jit(solution)/shard_map/ppermute | solution.py:352
  8.4 1.5 %collective-permute-start = (bf16[144,1024]{1,0:T(8,128)(2,1)}, bf16[144,1024]{1,0:T(8,128)(2,1)S(1)}, u32[]{:S(2)}, u32[]{:S(2)}) collective-permute-start(bf16[144,1024]{1,0:T(8,128)(2,1)} %get-tuple-element.29.scens), channel_id=1, source_target_pairs={{0,2},{1,3},{2,0},{3,1},{4,6},{5,7},{6,4},{7,5},{8,10},{9,11},{10,... | collective-permute-start | bytes 884744 | tf_op jit(solution)/shard_map/ppermute | solution.py:352
  10.0 0.1 copy.10.exps
  10.2 0.9 %copy-done.1 = bf16[80,1024]{1,0:T(8,128)(2,1)S(1)} copy-done((bf16[80,1024]{1,0:T(8,128)(2,1)S(1)}, bf16[80,1024]{1,0:T(8,128)(2,1)}, u32[]{:S(2)}) %copy-start.1) | copy-done | bytes 163864
  11.1 4.4 %shard_map.87 = (bf16[512,1024]{1,0:T(8,128)(2,1)S(1)}, bf16[512,1024]{1,0:T(8,128)(2,1)S(1)}, bf16[1024,128]{1,0:T(8,128)(2,1)S(1)}, f32[1024,64]{1,0:T(8,128)S(1)}) custom-call(s32[512,40]{1,0:T(8,128)S(1)} %copy.10.exps, bf16[144,1024]{1,0:T(8,128)(2,1)S(1)} %copy-done, bf16[80,1024]{1,0:T(8,128)(2,1)S(1)} %copy-done.1, ...), custom_call_target="tpu_custom_call" | custom-call | flops 3000000000 | bytes 3145728 | tf_op jit(solution)/shard_map/pallas_call | solution.py:291
  15.6 0.4 collective-permute-start.9
  16.0 1.4 %collective-permute-done.scens = bf16[144,1024]{1,0:T(8,128)(2,1)S(1)} collective-permute-done((bf16[144,1024]{1,0:T(8,128)(2,1)}, bf16[144,1024]{1,0:T(8,128)(2,1)S(1)}, u32[]{:S(2)}, u32[]{:S(2)}) %collective-permute-start) | collective-permute-done | bytes 294944 | tf_op jit(solution)/shard_map/ppermute | solution.py:352
  17.4 3.5 %shard_map.88 = (bf16[512,1024]{1,0:T(8,128)(2,1)S(1)}, bf16[512,1024]{1,0:T(8,128)(2,1)S(1)}, bf16[1024,128]{1,0:T(8,128)(2,1)S(1)}, f32[128,512]{1,0:T(8,128)S(1)}, f32[128,512]{1,0:T(8,128)S(1)}) custom-call(s32[2]{0:T(128)S(1)} %pad_add_fusion.1.start, s32[512,40]{1,0:T(8,128)S(1)} %copy.10.exps, bf16[144,1024]{1,0:T(8,128)(2,1)S(1)} %collective-permute-done.scens, ...), custom_call_target="tpu_custom_call" | custom-call | flops 3000000000 | bytes 3145728 | tf_op jit(solution)/shard_map/pallas_call | solution.py:304
  21.0 2.6 %shard_map.89.refs_5_ = f32[1024,64]{1,0:T(8,128)S(1)} custom-call(bf16[1024,128]{1,0:T(8,128)(2,1)S(1)} %get-tuple-element.36.rt.refs_1_, bf16[80,1024]{1,0:T(8,128)(2,1)S(1)} %copy-done.1, bf16[80,1024]{1,0:T(8,128)(2,1)S(1)} %collective-permute-done.1.p1.refs_1_), custom_call_target="tpu_custom_call" | custom-call | flops 3565158400 | bytes 1048576 | tf_op jit(solution)/shard_map/pallas_call | solution.py:194
  23.7 0.5 collective-permute-start.3
  24.2 5.0 %shard_map.90.refs_4_ = f32[1024,128]{1,0:T(8,128)S(1)} custom-call(bf16[1024,128]{1,0:T(8,128)(2,1)S(1)} %get-tuple-element.39.refs_0_, bf16[1024,128]{1,0:T(8,128)(2,1)S(1)} %get-tuple-element.36.rt.refs_1_, bf16[80,1024]{1,0:T(8,128)(2,1)S(1)} %collective-permute-done.4.refs_2_, bf16[80,1024]{1,0:T(8,128)(2,1)S(1)} %collective-permute-done.5.refs_3_, ...), custom_call_target="tpu_custom_call" | custom-call | flops 7130316800 | bytes 1048576 | tf_op jit(solution)/shard_map/pallas_call | solution.py:194
  29.2 0.3 collective-permute-start.10
  29.5 0.3 collective-permute-start.8
  29.8 1.4 %collective-permute-start.6 = (f16[128,512]{1,0:T(8,128)(2,1)S(1)}, f16[128,512]{1,0:T(8,128)(2,1)S(1)}, u32[]{:S(2)}, u32[]{:S(2)}) collective-permute-start(f16[128,512]{1,0:T(8,128)(2,1)S(1)} %fusion.1), channel_id=1, source_target_pairs={{0,8},{1,9},{2,10},{3,11},{4,12},{5,13},{6,14},{7,15},{8,0},{9,1},... | collective-permute-start | bytes 393224 | tf_op jit(solution)/shard_map/ppermute | solution.py:352
  31.2 4.8 %shard_map.91.refs_3_ = f32[1024,128]{1,0:T(8,128)S(1)} custom-call(bf16[1024,128]{1,0:T(8,128)(2,1)S(1)} %get-tuple-element.39.refs_0_, bf16[1024,128]{1,0:T(8,128)(2,1)S(1)} %get-tuple-element.36.rt.refs_1_, bf16[80,1024]{1,0:T(8,128)(2,1)S(1)} %collective-permute-done.7.refs_2_, bf16[80,1024]{1,0:T(8,128)(2,1)S(1)} %collective-permute-done.9.refs_3_, ...), custom_call_target="tpu_custom_call" | custom-call | flops 7130316800 | bytes 1048576 | tf_op jit(solution)/shard_map/pallas_call | solution.py:194
  36.0 2.8 %shard_map.92.refs_3_ = f32[1024,128]{1,0:T(8,128)S(1)} custom-call(bf16[1024,128]{1,0:T(8,128)(2,1)S(1)} %get-tuple-element.39.refs_0_, bf16[1024,128]{1,0:T(8,128)(2,1)S(1)} %get-tuple-element.36.rt.refs_1_, bf16[80,1024]{1,0:T(8,128)(2,1)S(1)} %collective-permute-done.8.refs_2_, f32[1024,128]{1,0:T(8,128)S(1)} %shard_map.91.refs_3_), custom_call_target="tpu_custom_call" | custom-call | flops 3565158400 | bytes 1048576 | tf_op jit(solution)/shard_map/pallas_call | solution.py:194
  38.8 0.4 collective-permute-done.6
  39.3 4.3 %shard_map.93 = f32[64,512]{1,0:T(8,128)S(1)} custom-call(bf16[1024,128]{1,0:T(8,128)(2,1)S(1)} %get-tuple-element.39.refs_0_, bf16[1024,128]{1,0:T(8,128)(2,1)S(1)} %get-tuple-element.36.rt.refs_1_, bf16[80,1024]{1,0:T(8,128)(2,1)S(1)} %collective-permute-done.10.refs_2_, f32[1024,128]{1,0:T(8,128)S(1)} %shard_map.92.refs_3_, ...), custom_call_target="tpu_custom_call" | custom-call | flops 3565158400 | bytes 1048576 | tf_op jit(solution)/shard_map/pallas_call | solution.py:194
  43.7 1.3 %collective-permute-done.11 = f32[64,512]{1,0:T(8,128)S(1)} collective-permute-done((f32[64,512]{1,0:T(8,128)S(1)}, f32[64,512]{1,0:T(8,128)S(1)}, u32[]{:S(2)}, u32[]{:S(2)}) %collective-permute-start.11) | collective-permute-done | bytes 131104 | tf_op jit(solution)/shard_map/ppermute | solution.py:352
  45.0 1.6 %collective-permute-start.12 = (f16[64,512]{1,0:T(8,128)(2,1)S(1)}, f16[64,512]{1,0:T(8,128)(2,1)S(1)}, u32[]{:S(2)}, u32[]{:S(2)}) collective-permute-start(f16[64,512]{1,0:T(8,128)(2,1)S(1)} %add_convert_fusion.1), channel_id=1, source_target_pairs={{0,2},{1,3},{2,0},{3,1},{4,6},{5,7},{6,4},{7,5},{8,10},{9,11},{10,... | collective-permute-start | bytes 196616 | tf_op jit(solution)/shard_map/ppermute | solution.py:352
  46.6 0.6 collective-permute-start.13
  47.2 2.4 %collective-permute-done.12 = f16[64,512]{1,0:T(8,128)(2,1)S(1)} collective-permute-done((f16[64,512]{1,0:T(8,128)(2,1)S(1)}, f16[64,512]{1,0:T(8,128)(2,1)S(1)}, u32[]{:S(2)}, u32[]{:S(2)}) %collective-permute-start.12) | collective-permute-done | bytes 65568 | tf_op jit(solution)/shard_map/ppermute | solution.py:352
  49.6 1.7 %collective-permute-start.15 = (f16[64,512]{1,0:T(8,128)(2,1)S(1)}, f16[64,512]{1,0:T(8,128)(2,1)S(1)}, u32[]{:S(2)}, u32[]{:S(2)}) collective-permute-start(f16[64,512]{1,0:T(8,128)(2,1)S(1)} %fusion), channel_id=1, source_target_pairs={{0,4},{1,5},{2,6},{3,7},{4,0},{5,1},{6,2},{7,3},{8,12},{9,13},{10,... | collective-permute-start | bytes 196616 | tf_op jit(solution)/shard_map/ppermute | solution.py:352
  51.3 0.9 %collective-permute-done.13 = f16[128,512]{1,0:T(8,128)(2,1)S(1)} collective-permute-done((f16[128,512]{1,0:T(8,128)(2,1)S(1)}, f16[128,512]{1,0:T(8,128)(2,1)S(1)}, u32[]{:S(2)}, u32[]{:S(2)}) %collective-permute-start.13) | collective-permute-done | bytes 131104 | tf_op jit(solution)/shard_map/ppermute | solution.py:352
  52.3 1.7 %collective-permute-done.15 = f16[64,512]{1,0:T(8,128)(2,1)S(1)} collective-permute-done((f16[64,512]{1,0:T(8,128)(2,1)S(1)}, f16[64,512]{1,0:T(8,128)(2,1)S(1)}, u32[]{:S(2)}, u32[]{:S(2)}) %collective-permute-start.15) | collective-permute-done | bytes 65568 | tf_op jit(solution)/shard_map/ppermute | solution.py:352
  54.0 1.3 %collective-permute-start.16 = (f16[64,512]{1,0:T(8,128)(2,1)S(1)}, f16[64,512]{1,0:T(8,128)(2,1)S(1)}, u32[]{:S(2)}, u32[]{:S(2)}) collective-permute-start(f16[64,512]{1,0:T(8,128)(2,1)S(1)} %add_convert_fusion), channel_id=1, source_target_pairs={{0,8},{1,9},{2,10},{3,11},{4,12},{5,13},{6,14},{7,15},{8,0},{9,1},... | collective-permute-start | bytes 196616 | tf_op jit(solution)/shard_map/ppermute | solution.py:352
  55.4 1.6 %shard_map.94 = f32[512,512]{1,0:T(8,128)} custom-call(s32[4]{0:T(128)S(1)} %pad_add_fusion.refs_0_, f32[128,512]{1,0:T(8,128)S(1)} %get-tuple-element.56.refs_1_, f32[128,512]{1,0:T(8,128)S(1)} %convert_element_type.68.refs_2_, f32[256,512]{1,0:T(8,128)S(1)} %convert_element_type.69.refs_3_), custom_call_target="tpu_custom_call" | custom-call | flops 1048576 | bytes 2097152 | tf_op jit(solution)/shard_map/pallas_call | solution.py:327
  57.0 2.2 %collective-permute-done.16 = f16[64,512]{1,0:T(8,128)(2,1)S(1)} collective-permute-done((f16[64,512]{1,0:T(8,128)(2,1)S(1)}, f16[64,512]{1,0:T(8,128)(2,1)S(1)}, u32[]{:S(2)}, u32[]{:S(2)}) %collective-permute-start.16) | collective-permute-done | bytes 65568 | tf_op jit(solution)/shard_map/ppermute | solution.py:352
  59.2 0.7 %add_bitcast_fusion = f32[512,64]{0,1:T(8,128)} fusion(f16[64,512]{1,0:T(8,128)(2,1)S(1)} %collective-permute-done.16, f16[64,512]{1,0:T(8,128)(2,1)S(1)} %add_convert_fusion), kind=kLoop, calls=%fused_computation.4 | loop fusion | flops 98304 | bytes 262144 | tf_op jit(solution)/shard_map/transpose | solution.py:420
  (31 shorter events, 0.8 us)
Async XLA Ops:
  0.6 9.4 %copy-start.2 = (s32[512,40]{0,1:T(8,128)S(1)}, s32[512,40]{0,1:T(8,128)}, u32[]{:S(2)}) copy-start(s32[512,40]{0,1:T(8,128)} %param.13) | copy-start | bytes 245764
  2.6 7.5 %copy-start = (bf16[144,1024]{1,0:T(8,128)(2,1)S(1)}, bf16[144,1024]{1,0:T(8,128)(2,1)}, u32[]{:S(2)}) copy-start(bf16[144,1024]{1,0:T(8,128)(2,1)} %get-tuple-element.29.scens) | copy-start | bytes 884740
  2.7 7.5 %collective-permute-start.1 = (bf16[80,1024]{1,0:T(8,128)(2,1)}, bf16[80,1024]{1,0:T(8,128)(2,1)S(1)}, u32[]{:S(2)}, u32[]{:S(2)}) collective-permute-start(bf16[80,1024]{1,0:T(8,128)(2,1)} %get-tuple-element.30.p0.refs_0_), channel_id=1, source_target_pairs={{0,1},{1,0},{2,3},{3,2},{4,5},{5,4},{6,7},{7,6},{8,9},{9,8},{10,11... | collective-permute-start | bytes 491528 | tf_op jit(solution)/shard_map/ppermute | solution.py:352
  3.2 12.3 %collective-permute-start.4 = (bf16[80,1024]{1,0:T(8,128)(2,1)}, bf16[80,1024]{1,0:T(8,128)(2,1)S(1)}, u32[]{:S(2)}, u32[]{:S(2)}) collective-permute-start(bf16[80,1024]{1,0:T(8,128)(2,1)} %get-tuple-element.30.p0.refs_0_), channel_id=1, source_target_pairs={{0,4},{1,5},{2,6},{3,7},{4,0},{5,1},{6,2},{7,3},{8,12},{9,13},{10,... | collective-permute-start | bytes 491528 | tf_op jit(solution)/shard_map/ppermute | solution.py:352
  5.8 23.7 %collective-permute-start.7 = (bf16[80,1024]{1,0:T(8,128)(2,1)}, bf16[80,1024]{1,0:T(8,128)(2,1)S(1)}, u32[]{:S(2)}, u32[]{:S(2)}) collective-permute-start(bf16[80,1024]{1,0:T(8,128)(2,1)} %get-tuple-element.30.p0.refs_0_), channel_id=1, source_target_pairs={{0,8},{1,9},{2,10},{3,11},{4,12},{5,13},{6,14},{7,15},{8,0},{9,1},... | collective-permute-start | bytes 491528 | tf_op jit(solution)/shard_map/ppermute | solution.py:352
  8.4 9.0 %collective-permute-start = (bf16[144,1024]{1,0:T(8,128)(2,1)}, bf16[144,1024]{1,0:T(8,128)(2,1)S(1)}, u32[]{:S(2)}, u32[]{:S(2)}) collective-permute-start(bf16[144,1024]{1,0:T(8,128)(2,1)} %get-tuple-element.29.scens), channel_id=1, source_target_pairs={{0,2},{1,3},{2,0},{3,1},{4,6},{5,7},{6,4},{7,5},{8,10},{9,11},{10,... | collective-permute-start | bytes 884744 | tf_op jit(solution)/shard_map/ppermute | solution.py:352
  10.2 0.9 %copy-start.1 = (bf16[80,1024]{1,0:T(8,128)(2,1)S(1)}, bf16[80,1024]{1,0:T(8,128)(2,1)}, u32[]{:S(2)}) copy-start(bf16[80,1024]{1,0:T(8,128)(2,1)} %get-tuple-element.30.p0.refs_0_) | copy-start | bytes 491524
  15.5 8.2 %collective-permute-start.5 = (bf16[80,1024]{1,0:T(8,128)(2,1)S(1)}, bf16[80,1024]{1,0:T(8,128)(2,1)S(1)}, u32[]{:S(2)}, u32[]{:S(2)}) collective-permute-start(bf16[80,1024]{1,0:T(8,128)(2,1)S(1)} %collective-permute-done.4.refs_2_), channel_id=1, source_target_pairs={{0,1},{1,0},{2,3},{3,2},{4,5},{5,4},{6,7},{7,6},{8,9},{9,8},{10,11... | collective-permute-start | bytes 491528 | tf_op jit(solution)/shard_map/ppermute | solution.py:352
  15.6 13.6 %collective-permute-start.9 = (bf16[80,1024]{1,0:T(8,128)(2,1)S(1)}, bf16[80,1024]{1,0:T(8,128)(2,1)S(1)}, u32[]{:S(2)}, u32[]{:S(2)}) collective-permute-start(bf16[80,1024]{1,0:T(8,128)(2,1)S(1)} %collective-permute-done.4.refs_2_), channel_id=1, source_target_pairs={{0,8},{1,9},{2,10},{3,11},{4,12},{5,13},{6,14},{7,15},{8,0},{9,1},... | collective-permute-start | bytes 491528 | tf_op jit(solution)/shard_map/ppermute | solution.py:352
  21.0 2.7 %collective-permute-start.2 = (f32[128,512]{1,0:T(8,128)S(1)}, f32[128,512]{1,0:T(8,128)S(1)}, u32[]{:S(2)}, u32[]{:S(2)}) collective-permute-start(f32[128,512]{1,0:T(8,128)S(1)} %get-tuple-element.35), channel_id=1, source_target_pairs={{0,1},{1,0},{2,3},{3,2},{4,5},{5,4},{6,7},{7,6},{8,9},{9,8},{10,11... | collective-permute-start | bytes 786440 | tf_op jit(solution)/shard_map/ppermute | solution.py:352
  23.7 6.1 %collective-permute-start.3 = (f16[128,512]{1,0:T(8,128)(2,1)S(1)}, f16[128,512]{1,0:T(8,128)(2,1)S(1)}, u32[]{:S(2)}, u32[]{:S(2)}) collective-permute-start(f16[128,512]{1,0:T(8,128)(2,1)S(1)} %fusion.3), channel_id=1, source_target_pairs={{0,4},{1,5},{2,6},{3,7},{4,0},{5,1},{6,2},{7,3},{8,12},{9,13},{10,... | collective-permute-start | bytes 393224 | tf_op jit(solution)/shard_map/ppermute | solution.py:352
  29.2 10.1 %collective-permute-start.10 = (bf16[80,1024]{1,0:T(8,128)(2,1)S(1)}, bf16[80,1024]{1,0:T(8,128)(2,1)S(1)}, u32[]{:S(2)}, u32[]{:S(2)}) collective-permute-start(bf16[80,1024]{1,0:T(8,128)(2,1)S(1)} %collective-permute-done.9.refs_3_), channel_id=1, source_target_pairs={{0,1},{1,0},{2,3},{3,2},{4,5},{5,4},{6,7},{7,6},{8,9},{9,8},{10,11... | collective-permute-start | bytes 491528 | tf_op jit(solution)/shard_map/ppermute | solution.py:352
  29.5 6.5 %collective-permute-start.8 = (bf16[80,1024]{1,0:T(8,128)(2,1)S(1)}, bf16[80,1024]{1,0:T(8,128)(2,1)S(1)}, u32[]{:S(2)}, u32[]{:S(2)}) collective-permute-start(bf16[80,1024]{1,0:T(8,128)(2,1)S(1)} %collective-permute-done.7.refs_2_), channel_id=1, source_target_pairs={{0,1},{1,0},{2,3},{3,2},{4,5},{5,4},{6,7},{7,6},{8,9},{9,8},{10,11... | collective-permute-start | bytes 491528 | tf_op jit(solution)/shard_map/ppermute | solution.py:352
  29.8 9.4 %collective-permute-start.6 = (f16[128,512]{1,0:T(8,128)(2,1)S(1)}, f16[128,512]{1,0:T(8,128)(2,1)S(1)}, u32[]{:S(2)}, u32[]{:S(2)}) collective-permute-start(f16[128,512]{1,0:T(8,128)(2,1)S(1)} %fusion.1), channel_id=1, source_target_pairs={{0,8},{1,9},{2,10},{3,11},{4,12},{5,13},{6,14},{7,15},{8,0},{9,1},... | collective-permute-start | bytes 393224 | tf_op jit(solution)/shard_map/ppermute | solution.py:352
  43.6 1.4 %collective-permute-start.11 = (f32[64,512]{1,0:T(8,128)S(1)}, f32[64,512]{1,0:T(8,128)S(1)}, u32[]{:S(2)}, u32[]{:S(2)}) collective-permute-start(f32[64,512]{1,0:T(8,128)S(1)} %shard_map.93), channel_id=1, source_target_pairs={{0,1},{1,0},{2,3},{3,2},{4,5},{5,4},{6,7},{7,6},{8,9},{9,8},{10,11... | collective-permute-start | bytes 393224 | tf_op jit(solution)/shard_map/ppermute | solution.py:352
  45.0 4.6 %collective-permute-start.12 = (f16[64,512]{1,0:T(8,128)(2,1)S(1)}, f16[64,512]{1,0:T(8,128)(2,1)S(1)}, u32[]{:S(2)}, u32[]{:S(2)}) collective-permute-start(f16[64,512]{1,0:T(8,128)(2,1)S(1)} %add_convert_fusion.1), channel_id=1, source_target_pairs={{0,2},{1,3},{2,0},{3,1},{4,6},{5,7},{6,4},{7,5},{8,10},{9,11},{10,... | collective-permute-start | bytes 196616 | tf_op jit(solution)/shard_map/ppermute | solution.py:352
  46.6 5.5 %collective-permute-start.13 = (f16[128,512]{1,0:T(8,128)(2,1)S(1)}, f16[128,512]{1,0:T(8,128)(2,1)S(1)}, u32[]{:S(2)}, u32[]{:S(2)}) collective-permute-start(f16[128,512]{1,0:T(8,128)(2,1)S(1)} %get-tuple-element.57), channel_id=1, source_target_pairs={{0,2},{1,3},{2,0},{3,1},{4,6},{5,7},{6,4},{7,5},{8,10},{9,11},{10,... | collective-permute-start | bytes 393224 | tf_op jit(solution)/shard_map/ppermute | solution.py:352
  49.6 4.3 %collective-permute-start.15 = (f16[64,512]{1,0:T(8,128)(2,1)S(1)}, f16[64,512]{1,0:T(8,128)(2,1)S(1)}, u32[]{:S(2)}, u32[]{:S(2)}) collective-permute-start(f16[64,512]{1,0:T(8,128)(2,1)S(1)} %fusion), channel_id=1, source_target_pairs={{0,4},{1,5},{2,6},{3,7},{4,0},{5,1},{6,2},{7,3},{8,12},{9,13},{10,... | collective-permute-start | bytes 196616 | tf_op jit(solution)/shard_map/ppermute | solution.py:352
  52.2 3.2 %collective-permute-start.14 = (f16[256,512]{1,0:T(8,128)(2,1)S(1)}, f16[256,512]{1,0:T(8,128)(2,1)S(1)}, u32[]{:S(2)}, u32[]{:S(2)}) collective-permute-start(f16[256,512]{1,0:T(8,128)(2,1)S(1)} %pad_maximum_fusion), channel_id=1, source_target_pairs={{0,1},{1,0},{2,3},{3,2},{4,5},{5,4},{6,7},{7,6},{8,9},{9,8},{10,11... | collective-permute-start | bytes 786440 | tf_op jit(solution)/shard_map/ppermute | solution.py:352
  54.0 5.2 %collective-permute-start.16 = (f16[64,512]{1,0:T(8,128)(2,1)S(1)}, f16[64,512]{1,0:T(8,128)(2,1)S(1)}, u32[]{:S(2)}, u32[]{:S(2)}) collective-permute-start(f16[64,512]{1,0:T(8,128)(2,1)S(1)} %add_convert_fusion), channel_id=1, source_target_pairs={{0,8},{1,9},{2,10},{3,11},{4,12},{5,13},{6,14},{7,15},{8,0},{9,1},... | collective-permute-start | bytes 196616 | tf_op jit(solution)/shard_map/ppermute | solution.py:352

commit v9 on v8

--- a/solution.py
+++ b/solution.py
@@ -256,7 +256,7 @@
 
 
 def gram_kernel(start, exps, scens, earlier, *refs):
-    outs, keep, send, (sems, first, *held) = refs[:3], refs[3], refs[4], refs[5:]
+    outs, keep, send, (sems, both, first, *held) = refs[:3], refs[3], refs[4], refs[5:]
     load = pltpu.make_async_copy(earlier, first, sems.at[3])
     load.start()
     stores = [pltpu.make_async_copy(a, b, sems.at[i]) for i, (a, b) in enumerate(zip(held, outs))]
@@ -266,15 +266,16 @@
         store.start()
     load.wait()
     rows = keep.shape[0]
-    for i, out in enumerate((keep, send)):
-        r0 = pl.multiple_of(start[i] * rows, rows)
-        total = None
-        for b in (first, high):
-            part = lax.dot_general(
-                b[pl.ds(r0, rows), :], b[...], (((1,), (1,)), ((), ())), preferred_element_type=F32
-            )
-            total = part if total is None else total + part
-        out[...] = total
+    r0 = pl.multiple_of(start[0] * (2 * rows), 2 * rows)
+    total = None
+    for b in (first, high):
+        part = lax.dot_general(
+            b[pl.ds(r0, 2 * rows), :], b[...], (((1,), (1,)), ((), ())), preferred_element_type=F32
+        )
+        total = part if total is None else total + part
+    both[...] = total
+    keep[...] = both[pl.ds(pl.multiple_of(start[1] * rows, rows), rows), :]
+    send[...] = both[pl.ds(pl.multiple_of((1 - start[1]) * rows, rows), rows), :]
     for store in stores:
         store.wait()
 
@@ -299,7 +300,8 @@
             compiler_params=params(),
             cost_estimate=cost,
         )(exponents, scens, *near)
-    scratch = [pltpu.SemaphoreType.DMA((4,)), *like([first]), *like(shapes)]
+    both = pltpu.VMEM((terms // 2, terms), F32)
+    scratch = [pltpu.SemaphoreType.DMA((4,)), both, *like([first]), *like(shapes)]
     shapes += [jax.ShapeDtypeStruct((terms // 4, terms), F32)] * 2
     return pl.pallas_call(
         gram_kernel,
@@ -370,7 +372,7 @@
             packs[m] = swap(packs[m ^ top], top)
 
     base = side * 2 + core
-    start = jnp.stack([base, base ^ 1])
+    start = jnp.stack([side, core])
     high1, low1, rt1, keep, send = basis_of(
         exponents, after(scens1, v), start=start, first=high0
     )

time: 60 us -> 59.4 us (0.990)
  Pallas kernels: 30.9 us -> 30.2 us
    pallas_call x1, Pallas kernels: 3.53 us -> 2.79 us  [basis_of(): pl.pallas_call(gram_kernel, in_specs=[SSPEC, VSPEC, VSPEC, HSPEC], out_sp...]
  transfers between devices with their start and end apart: 17 -> 17, of which waited for: 7 -> 8; matrix products, arithmetic and copies ran while one was open for 1% -> 1% of each run, Pallas kernels for 41% -> 40%
where the time goes in v9:
time: 59.4 us; the launch traced here: 59.3 us
  Pallas kernels  30.2 us (51%)
  starting transfers between devices  15.4 us (26%)
  waiting for transfers between devices  10.5 us (18%)
  other arithmetic  1.17 us (2%)
  local copies, waits for them, and re-layouts  1.04 us (2%)
  between operations  0.9 us (2%)
    pallas_call x5, Pallas kernels, values_of(): pl.pallas_call(kernel, in_specs=[HSPEC] * len(rts) + [VSPEC] * (len(packs...  19.4 us
    ppermute x17, starting transfers between devices, swap(): return lax.ppermute(x, 'scen', [(i, i ^ mask) for i in range(n)])  15.4 us
    ppermute x17, waiting for transfers between devices, swap(): return lax.ppermute(x, 'scen', [(i, i ^ mask) for i in range(n)])  10.5 us
    pallas_call x1, Pallas kernels, basis_of(): pl.pallas_call(first_kernel, in_specs=[VSPEC] * 2 + [HSPEC] * 2, out_spec...  4.41 us
    pallas_call x1, Pallas kernels, basis_of(): pl.pallas_call(gram_kernel, in_specs=[SSPEC, VSPEC, VSPEC, HSPEC], out_sp...  2.79 us
    pallas_call x1, Pallas kernels, packs_of(): pl.pallas_call(pack_kernel, in_specs=[pl.BlockSpec(memory_space=pltpu.HBM...  1.99 us
    pallas_call x1, Pallas kernels, placed(): pl.pallas_call(functools.partial(place_kernel, blocks), in_specs=[pl.Bloc...  1.59 us
  transfers between devices with their start and end apart: 17, of which 8 were waited for; matrix products, arithmetic and copies ran while one was open for 1% of the time, Pallas kernels for 40%

profile of v9, /device:TPU:0, one launch (start us, length us, event | category | flops | bytes accessed | tf_op | source)
XLA Modules:
  0.0 59.3 jit_solution(4816157406526153472)
XLA Ops:
  0.6 2.0 %shard_map.86 = (bf16[80,1024]{1,0:T(8,128)(2,1)}, bf16[144,1024]{1,0:T(8,128)(2,1)}) custom-call(bf16[64,1024]{1,0:T(8,128)(2,1)} %bitcast.12, f32[1,1024]{1,0:T(1,128)} %bitcast.13, s32[1,1024]{1,0:T(1,128)} %bitcast.14, s32[1,1024]{1,0:T(1,128)} %bitcast.15, bf16[64,1024]{1,0:T(8,128)(2,1)} %refs_4_.1, f32[40,1024]{1,0:T(8,128)} %refs_5_.1), custom_call_target="tpu_custom_call" | custom-call | flops 1048576 | bytes 1048576 | tf_op jit(solution)/shard_map/pallas_call | solution.py:65
  2.7 0.5 collective-permute-start.1
  3.2 2.6 %collective-permute-start.4 = (bf16[80,1024]{1,0:T(8,128)(2,1)}, bf16[80,1024]{1,0:T(8,128)(2,1)S(1)}, u32[]{:S(2)}, u32[]{:S(2)}) collective-permute-start(bf16[80,1024]{1,0:T(8,128)(2,1)} %get-tuple-element.30.p0.refs_0_), channel_id=1, source_target_pairs={{0,4},{1,5},{2,6},{3,7},{4,0},{5,1},{6,2},{7,3},{8,12},{9,13},{10,... | collective-permute-start | bytes 491528 | tf_op jit(solution)/shard_map/ppermute | solution.py:354
  5.8 2.6 %collective-permute-start.7 = (bf16[80,1024]{1,0:T(8,128)(2,1)}, bf16[80,1024]{1,0:T(8,128)(2,1)S(1)}, u32[]{:S(2)}, u32[]{:S(2)}) collective-permute-start(bf16[80,1024]{1,0:T(8,128)(2,1)} %get-tuple-element.30.p0.refs_0_), channel_id=1, source_target_pairs={{0,8},{1,9},{2,10},{3,11},{4,12},{5,13},{6,14},{7,15},{8,0},{9,1},... | collective-permute-start | bytes 491528 | tf_op jit(solution)/shard_map/ppermute | solution.py:354
  8.4 1.5 %collective-permute-start = (bf16[144,1024]{1,0:T(8,128)(2,1)}, bf16[144,1024]{1,0:T(8,128)(2,1)S(1)}, u32[]{:S(2)}, u32[]{:S(2)}) collective-permute-start(bf16[144,1024]{1,0:T(8,128)(2,1)} %get-tuple-element.29.scens), channel_id=1, source_target_pairs={{0,2},{1,3},{2,0},{3,1},{4,6},{5,7},{6,4},{7,5},{8,10},{9,11},{10,... | collective-permute-start | bytes 884744 | tf_op jit(solution)/shard_map/ppermute | solution.py:354
  10.2 0.9 %copy-done.1 = bf16[80,1024]{1,0:T(8,128)(2,1)S(1)} copy-done((bf16[80,1024]{1,0:T(8,128)(2,1)S(1)}, bf16[80,1024]{1,0:T(8,128)(2,1)}, u32[]{:S(2)}) %copy-start.1) | copy-done | bytes 163864
  11.1 4.4 %shard_map.87 = (bf16[512,1024]{1,0:T(8,128)(2,1)S(1)}, bf16[512,1024]{1,0:T(8,128)(2,1)S(1)}, bf16[1024,128]{1,0:T(8,128)(2,1)S(1)}, f32[1024,64]{1,0:T(8,128)S(1)}) custom-call(s32[512,40]{1,0:T(8,128)S(1)} %copy.10.exps, bf16[144,1024]{1,0:T(8,128)(2,1)S(1)} %copy-done, bf16[80,1024]{1,0:T(8,128)(2,1)S(1)} %copy-done.1, ...), custom_call_target="tpu_custom_call" | custom-call | flops 3000000000 | bytes 3145728 | tf_op jit(solution)/shard_map/pallas_call | solution.py:292
  15.6 0.4 collective-permute-start.9
  16.0 1.4 %collective-permute-done.scens = bf16[144,1024]{1,0:T(8,128)(2,1)S(1)} collective-permute-done((bf16[144,1024]{1,0:T(8,128)(2,1)}, bf16[144,1024]{1,0:T(8,128)(2,1)S(1)}, u32[]{:S(2)}, u32[]{:S(2)}) %collective-permute-start) | collective-permute-done | bytes 294944 | tf_op jit(solution)/shard_map/ppermute | solution.py:354
  17.4 2.8 %shard_map.88 = (bf16[512,1024]{1,0:T(8,128)(2,1)S(1)}, bf16[512,1024]{1,0:T(8,128)(2,1)S(1)}, bf16[1024,128]{1,0:T(8,128)(2,1)S(1)}, f32[128,512]{1,0:T(8,128)S(1)}, f32[128,512]{1,0:T(8,128)S(1)}) custom-call(s32[2]{0:T(128)S(1)} %pad_add_fusion.1.start, s32[512,40]{1,0:T(8,128)S(1)} %copy.10.exps, bf16[144,1024]{1,0:T(8,128)(2,1)S(1)} %collective-permute-done.scens, ...), custom_call_target="tpu_custom_call" | custom-call | flops 3000000000 | bytes 3145728 | tf_op jit(solution)/shard_map/pallas_call | solution.py:306
  20.3 2.6 %shard_map.89.refs_5_ = f32[1024,64]{1,0:T(8,128)S(1)} custom-call(bf16[1024,128]{1,0:T(8,128)(2,1)S(1)} %get-tuple-element.36.rt.refs_1_, bf16[80,1024]{1,0:T(8,128)(2,1)S(1)} %copy-done.1, bf16[80,1024]{1,0:T(8,128)(2,1)S(1)} %collective-permute-done.1.p1.refs_1_), custom_call_target="tpu_custom_call" | custom-call | flops 3565158400 | bytes 1048576 | tf_op jit(solution)/shard_map/pallas_call | solution.py:194
  23.0 0.5 collective-permute-start.3
  23.5 5.0 %shard_map.90.refs_4_ = f32[1024,128]{1,0:T(8,128)S(1)} custom-call(bf16[1024,128]{1,0:T(8,128)(2,1)S(1)} %get-tuple-element.39.refs_0_, bf16[1024,128]{1,0:T(8,128)(2,1)S(1)} %get-tuple-element.36.rt.refs_1_, bf16[80,1024]{1,0:T(8,128)(2,1)S(1)} %collective-permute-done.4.refs_2_, bf16[80,1024]{1,0:T(8,128)(2,1)S(1)} %collective-permute-done.5.refs_3_, ...), custom_call_target="tpu_custom_call" | custom-call | flops 7130316800 | bytes 1048576 | tf_op jit(solution)/shard_map/pallas_call | solution.py:194
  28.5 0.3 collective-permute-start.10
  28.8 0.3 collective-permute-start.8
  29.1 0.2 collective-permute-done.3
  29.4 1.1 %collective-permute-start.6 = (f16[128,512]{1,0:T(8,128)(2,1)S(1)}, f16[128,512]{1,0:T(8,128)(2,1)S(1)}, u32[]{:S(2)}, u32[]{:S(2)}) collective-permute-start(f16[128,512]{1,0:T(8,128)(2,1)S(1)} %fusion.1), channel_id=1, source_target_pairs={{0,8},{1,9},{2,10},{3,11},{4,12},{5,13},{6,14},{7,15},{8,0},{9,1},... | collective-permute-start | bytes 393224 | tf_op jit(solution)/shard_map/ppermute | solution.py:354
  30.5 4.8 %shard_map.91.refs_3_ = f32[1024,128]{1,0:T(8,128)S(1)} custom-call(bf16[1024,128]{1,0:T(8,128)(2,1)S(1)} %get-tuple-element.39.refs_0_, bf16[1024,128]{1,0:T(8,128)(2,1)S(1)} %get-tuple-element.36.rt.refs_1_, bf16[80,1024]{1,0:T(8,128)(2,1)S(1)} %collective-permute-done.7.refs_2_, bf16[80,1024]{1,0:T(8,128)(2,1)S(1)} %collective-permute-done.9.refs_3_, ...), custom_call_target="tpu_custom_call" | custom-call | flops 7130316800 | bytes 1048576 | tf_op jit(solution)/shard_map/pallas_call | solution.py:194
  35.3 2.8 %shard_map.92.refs_3_ = f32[1024,128]{1,0:T(8,128)S(1)} custom-call(bf16[1024,128]{1,0:T(8,128)(2,1)S(1)} %get-tuple-element.39.refs_0_, bf16[1024,128]{1,0:T(8,128)(2,1)S(1)} %get-tuple-element.36.rt.refs_1_, bf16[80,1024]{1,0:T(8,128)(2,1)S(1)} %collective-permute-done.8.refs_2_, f32[1024,128]{1,0:T(8,128)S(1)} %shard_map.91.refs_3_), custom_call_target="tpu_custom_call" | custom-call | flops 3565158400 | bytes 1048576 | tf_op jit(solution)/shard_map/pallas_call | solution.py:194
  38.1 0.5 collective-permute-done.6
  38.6 4.3 %shard_map.93 = f32[64,512]{1,0:T(8,128)S(1)} custom-call(bf16[1024,128]{1,0:T(8,128)(2,1)S(1)} %get-tuple-element.39.refs_0_, bf16[1024,128]{1,0:T(8,128)(2,1)S(1)} %get-tuple-element.36.rt.refs_1_, bf16[80,1024]{1,0:T(8,128)(2,1)S(1)} %collective-permute-done.10.refs_2_, f32[1024,128]{1,0:T(8,128)S(1)} %shard_map.92.refs_3_, ...), custom_call_target="tpu_custom_call" | custom-call | flops 3565158400 | bytes 1048576 | tf_op jit(solution)/shard_map/pallas_call | solution.py:194
  43.0 1.3 %collective-permute-done.11 = f32[64,512]{1,0:T(8,128)S(1)} collective-permute-done((f32[64,512]{1,0:T(8,128)S(1)}, f32[64,512]{1,0:T(8,128)S(1)}, u32[]{:S(2)}, u32[]{:S(2)}) %collective-permute-start.11) | collective-permute-done | bytes 131104 | tf_op jit(solution)/shard_map/ppermute | solution.py:354
  44.3 1.5 %collective-permute-start.12 = (f16[64,512]{1,0:T(8,128)(2,1)S(1)}, f16[64,512]{1,0:T(8,128)(2,1)S(1)}, u32[]{:S(2)}, u32[]{:S(2)}) collective-permute-start(f16[64,512]{1,0:T(8,128)(2,1)S(1)} %add_convert_fusion.1), channel_id=1, source_target_pairs={{0,2},{1,3},{2,0},{3,1},{4,6},{5,7},{6,4},{7,5},{8,10},{9,11},{10,... | collective-permute-start | bytes 196616 | tf_op jit(solution)/shard_map/ppermute | solution.py:354
  45.9 0.6 %collective-permute-start.13 = (f16[128,512]{1,0:T(8,128)(2,1)S(1)}, f16[128,512]{1,0:T(8,128)(2,1)S(1)}, u32[]{:S(2)}, u32[]{:S(2)}) collective-permute-start(f16[128,512]{1,0:T(8,128)(2,1)S(1)} %get-tuple-element.57), channel_id=1, source_target_pairs={{0,2},{1,3},{2,0},{3,1},{4,6},{5,7},{6,4},{7,5},{8,10},{9,11},{10,... | collective-permute-start | bytes 393224 | tf_op jit(solution)/shard_map/ppermute | solution.py:354
  46.5 2.5 %collective-permute-done.12 = f16[64,512]{1,0:T(8,128)(2,1)S(1)} collective-permute-done((f16[64,512]{1,0:T(8,128)(2,1)S(1)}, f16[64,512]{1,0:T(8,128)(2,1)S(1)}, u32[]{:S(2)}, u32[]{:S(2)}) %collective-permute-start.12) | collective-permute-done | bytes 65568 | tf_op jit(solution)/shard_map/ppermute | solution.py:354
  49.0 1.5 %collective-permute-start.15 = (f16[64,512]{1,0:T(8,128)(2,1)S(1)}, f16[64,512]{1,0:T(8,128)(2,1)S(1)}, u32[]{:S(2)}, u32[]{:S(2)}) collective-permute-start(f16[64,512]{1,0:T(8,128)(2,1)S(1)} %fusion), channel_id=1, source_target_pairs={{0,4},{1,5},{2,6},{3,7},{4,0},{5,1},{6,2},{7,3},{8,12},{9,13},{10,... | collective-permute-start | bytes 196616 | tf_op jit(solution)/shard_map/ppermute | solution.py:354
  50.5 0.9 %collective-permute-done.13 = f16[128,512]{1,0:T(8,128)(2,1)S(1)} collective-permute-done((f16[128,512]{1,0:T(8,128)(2,1)S(1)}, f16[128,512]{1,0:T(8,128)(2,1)S(1)}, u32[]{:S(2)}, u32[]{:S(2)}) %collective-permute-start.13) | collective-permute-done | bytes 131104 | tf_op jit(solution)/shard_map/ppermute | solution.py:354
  51.6 1.7 %collective-permute-done.15 = f16[64,512]{1,0:T(8,128)(2,1)S(1)} collective-permute-done((f16[64,512]{1,0:T(8,128)(2,1)S(1)}, f16[64,512]{1,0:T(8,128)(2,1)S(1)}, u32[]{:S(2)}, u32[]{:S(2)}) %collective-permute-start.15) | collective-permute-done | bytes 65568 | tf_op jit(solution)/shard_map/ppermute | solution.py:354
  53.4 1.6 %collective-permute-start.16 = (f16[64,512]{1,0:T(8,128)(2,1)S(1)}, f16[64,512]{1,0:T(8,128)(2,1)S(1)}, u32[]{:S(2)}, u32[]{:S(2)}) collective-permute-start(f16[64,512]{1,0:T(8,128)(2,1)S(1)} %add_convert_fusion), channel_id=1, source_target_pairs={{0,8},{1,9},{2,10},{3,11},{4,12},{5,13},{6,14},{7,15},{8,0},{9,1},... | collective-permute-start | bytes 196616 | tf_op jit(solution)/shard_map/ppermute | solution.py:354
  55.1 1.6 %shard_map.94 = f32[512,512]{1,0:T(8,128)} custom-call(s32[4]{0:T(128)S(1)} %pad_add_fusion.refs_0_, f32[128,512]{1,0:T(8,128)S(1)} %get-tuple-element.56.refs_1_, f32[128,512]{1,0:T(8,128)S(1)} %convert_element_type.68.refs_2_, f32[256,512]{1,0:T(8,128)S(1)} %convert_element_type.69.refs_3_), custom_call_target="tpu_custom_call" | custom-call | flops 1048576 | bytes 2097152 | tf_op jit(solution)/shard_map/pallas_call | solution.py:329
  56.7 1.9 %collective-permute-done.16 = f16[64,512]{1,0:T(8,128)(2,1)S(1)} collective-permute-done((f16[64,512]{1,0:T(8,128)(2,1)S(1)}, f16[64,512]{1,0:T(8,128)(2,1)S(1)}, u32[]{:S(2)}, u32[]{:S(2)}) %collective-permute-start.16) | collective-permute-done | bytes 65568 | tf_op jit(solution)/shard_map/ppermute | solution.py:354
  58.6 0.7 %add_bitcast_fusion = f32[512,64]{0,1:T(8,128)} fusion(f16[64,512]{1,0:T(8,128)(2,1)S(1)} %collective-permute-done.16, f16[64,512]{1,0:T(8,128)(2,1)S(1)} %add_convert_fusion), kind=kLoop, calls=%fused_computation.4 | loop fusion | flops 98304 | bytes 262144 | tf_op jit(solution)/shard_map/transpose | solution.py:422
  (31 shorter events, 0.9 us)
Async XLA Ops:
  0.6 9.4 %copy-start.2 = (s32[512,40]{0,1:T(8,128)S(1)}, s32[512,40]{0,1:T(8,128)}, u32[]{:S(2)}) copy-start(s32[512,40]{0,1:T(8,128)} %param.13) | copy-start | bytes 245764
  2.6 7.5 %copy-start = (bf16[144,1024]{1,0:T(8,128)(2,1)S(1)}, bf16[144,1024]{1,0:T(8,128)(2,1)}, u32[]{:S(2)}) copy-start(bf16[144,1024]{1,0:T(8,128)(2,1)} %get-tuple-element.29.scens) | copy-start | bytes 884740
  2.7 7.5 %collective-permute-start.1 = (bf16[80,1024]{1,0:T(8,128)(2,1)}, bf16[80,1024]{1,0:T(8,128)(2,1)S(1)}, u32[]{:S(2)}, u32[]{:S(2)}) collective-permute-start(bf16[80,1024]{1,0:T(8,128)(2,1)} %get-tuple-element.30.p0.refs_0_), channel_id=1, source_target_pairs={{0,1},{1,0},{2,3},{3,2},{4,5},{5,4},{6,7},{7,6},{8,9},{9,8},{10,11... | collective-permute-start | bytes 491528 | tf_op jit(solution)/shard_map/ppermute | solution.py:354
  3.2 12.3 %collective-permute-start.4 = (bf16[80,1024]{1,0:T(8,128)(2,1)}, bf16[80,1024]{1,0:T(8,128)(2,1)S(1)}, u32[]{:S(2)}, u32[]{:S(2)}) collective-permute-start(bf16[80,1024]{1,0:T(8,128)(2,1)} %get-tuple-element.30.p0.refs_0_), channel_id=1, source_target_pairs={{0,4},{1,5},{2,6},{3,7},{4,0},{5,1},{6,2},{7,3},{8,12},{9,13},{10,... | collective-permute-start | bytes 491528 | tf_op jit(solution)/shard_map/ppermute | solution.py:354
  5.8 22.9 %collective-permute-start.7 = (bf16[80,1024]{1,0:T(8,128)(2,1)}, bf16[80,1024]{1,0:T(8,128)(2,1)S(1)}, u32[]{:S(2)}, u32[]{:S(2)}) collective-permute-start(bf16[80,1024]{1,0:T(8,128)(2,1)} %get-tuple-element.30.p0.refs_0_), channel_id=1, source_target_pairs={{0,8},{1,9},{2,10},{3,11},{4,12},{5,13},{6,14},{7,15},{8,0},{9,1},... | collective-permute-start | bytes 491528 | tf_op jit(solution)/shard_map/ppermute | solution.py:354
  8.4 9.0 %collective-permute-start = (bf16[144,1024]{1,0:T(8,128)(2,1)}, bf16[144,1024]{1,0:T(8,128)(2,1)S(1)}, u32[]{:S(2)}, u32[]{:S(2)}) collective-permute-start(bf16[144,1024]{1,0:T(8,128)(2,1)} %get-tuple-element.29.scens), channel_id=1, source_target_pairs={{0,2},{1,3},{2,0},{3,1},{4,6},{5,7},{6,4},{7,5},{8,10},{9,11},{10,... | collective-permute-start | bytes 884744 | tf_op jit(solution)/shard_map/ppermute | solution.py:354
  10.2 0.9 %copy-start.1 = (bf16[80,1024]{1,0:T(8,128)(2,1)S(1)}, bf16[80,1024]{1,0:T(8,128)(2,1)}, u32[]{:S(2)}) copy-start(bf16[80,1024]{1,0:T(8,128)(2,1)} %get-tuple-element.30.p0.refs_0_) | copy-start | bytes 491524
  15.5 7.4 %collective-permute-start.5 = (bf16[80,1024]{1,0:T(8,128)(2,1)S(1)}, bf16[80,1024]{1,0:T(8,128)(2,1)S(1)}, u32[]{:S(2)}, u32[]{:S(2)}) collective-permute-start(bf16[80,1024]{1,0:T(8,128)(2,1)S(1)} %collective-permute-done.4.refs_2_), channel_id=1, source_target_pairs={{0,1},{1,0},{2,3},{3,2},{4,5},{5,4},{6,7},{7,6},{8,9},{9,8},{10,11... | collective-permute-start | bytes 491528 | tf_op jit(solution)/shard_map/ppermute | solution.py:354
  15.6 12.9 %collective-permute-start.9 = (bf16[80,1024]{1,0:T(8,128)(2,1)S(1)}, bf16[80,1024]{1,0:T(8,128)(2,1)S(1)}, u32[]{:S(2)}, u32[]{:S(2)}) collective-permute-start(bf16[80,1024]{1,0:T(8,128)(2,1)S(1)} %collective-permute-done.4.refs_2_), channel_id=1, source_target_pairs={{0,8},{1,9},{2,10},{3,11},{4,12},{5,13},{6,14},{7,15},{8,0},{9,1},... | collective-permute-start | bytes 491528 | tf_op jit(solution)/shard_map/ppermute | solution.py:354
  20.2 2.7 %collective-permute-start.2 = (f32[128,512]{1,0:T(8,128)S(1)}, f32[128,512]{1,0:T(8,128)S(1)}, u32[]{:S(2)}, u32[]{:S(2)}) collective-permute-start(f32[128,512]{1,0:T(8,128)S(1)} %get-tuple-element.35), channel_id=1, source_target_pairs={{0,1},{1,0},{2,3},{3,2},{4,5},{5,4},{6,7},{7,6},{8,9},{9,8},{10,11... | collective-permute-start | bytes 786440 | tf_op jit(solution)/shard_map/ppermute | solution.py:354
  23.0 6.4 %collective-permute-start.3 = (f16[128,512]{1,0:T(8,128)(2,1)S(1)}, f16[128,512]{1,0:T(8,128)(2,1)S(1)}, u32[]{:S(2)}, u32[]{:S(2)}) collective-permute-start(f16[128,512]{1,0:T(8,128)(2,1)S(1)} %fusion.3), channel_id=1, source_target_pairs={{0,4},{1,5},{2,6},{3,7},{4,0},{5,1},{6,2},{7,3},{8,12},{9,13},{10,... | collective-permute-start | bytes 393224 | tf_op jit(solution)/shard_map/ppermute | solution.py:354
  28.5 10.1 %collective-permute-start.10 = (bf16[80,1024]{1,0:T(8,128)(2,1)S(1)}, bf16[80,1024]{1,0:T(8,128)(2,1)S(1)}, u32[]{:S(2)}, u32[]{:S(2)}) collective-permute-start(bf16[80,1024]{1,0:T(8,128)(2,1)S(1)} %collective-permute-done.9.refs_3_), channel_id=1, source_target_pairs={{0,1},{1,0},{2,3},{3,2},{4,5},{5,4},{6,7},{7,6},{8,9},{9,8},{10,11... | collective-permute-start | bytes 491528 | tf_op jit(solution)/shard_map/ppermute | solution.py:354
  28.8 6.5 %collective-permute-start.8 = (bf16[80,1024]{1,0:T(8,128)(2,1)S(1)}, bf16[80,1024]{1,0:T(8,128)(2,1)S(1)}, u32[]{:S(2)}, u32[]{:S(2)}) collective-permute-start(bf16[80,1024]{1,0:T(8,128)(2,1)S(1)} %collective-permute-done.7.refs_2_), channel_id=1, source_target_pairs={{0,1},{1,0},{2,3},{3,2},{4,5},{5,4},{6,7},{7,6},{8,9},{9,8},{10,11... | collective-permute-start | bytes 491528 | tf_op jit(solution)/shard_map/ppermute | solution.py:354
  29.4 9.2 %collective-permute-start.6 = (f16[128,512]{1,0:T(8,128)(2,1)S(1)}, f16[128,512]{1,0:T(8,128)(2,1)S(1)}, u32[]{:S(2)}, u32[]{:S(2)}) collective-permute-start(f16[128,512]{1,0:T(8,128)(2,1)S(1)} %fusion.1), channel_id=1, source_target_pairs={{0,8},{1,9},{2,10},{3,11},{4,12},{5,13},{6,14},{7,15},{8,0},{9,1},... | collective-permute-start | bytes 393224 | tf_op jit(solution)/shard_map/ppermute | solution.py:354
  42.9 1.4 %collective-permute-start.11 = (f32[64,512]{1,0:T(8,128)S(1)}, f32[64,512]{1,0:T(8,128)S(1)}, u32[]{:S(2)}, u32[]{:S(2)}) collective-permute-start(f32[64,512]{1,0:T(8,128)S(1)} %shard_map.93), channel_id=1, source_target_pairs={{0,1},{1,0},{2,3},{3,2},{4,5},{5,4},{6,7},{7,6},{8,9},{9,8},{10,11... | collective-permute-start | bytes 393224 | tf_op jit(solution)/shard_map/ppermute | solution.py:354
  44.3 4.6 %collective-permute-start.12 = (f16[64,512]{1,0:T(8,128)(2,1)S(1)}, f16[64,512]{1,0:T(8,128)(2,1)S(1)}, u32[]{:S(2)}, u32[]{:S(2)}) collective-permute-start(f16[64,512]{1,0:T(8,128)(2,1)S(1)} %add_convert_fusion.1), channel_id=1, source_target_pairs={{0,2},{1,3},{2,0},{3,1},{4,6},{5,7},{6,4},{7,5},{8,10},{9,11},{10,... | collective-permute-start | bytes 196616 | tf_op jit(solution)/shard_map/ppermute | solution.py:354
  45.9 5.6 %collective-permute-start.13 = (f16[128,512]{1,0:T(8,128)(2,1)S(1)}, f16[128,512]{1,0:T(8,128)(2,1)S(1)}, u32[]{:S(2)}, u32[]{:S(2)}) collective-permute-start(f16[128,512]{1,0:T(8,128)(2,1)S(1)} %get-tuple-element.57), channel_id=1, source_target_pairs={{0,2},{1,3},{2,0},{3,1},{4,6},{5,7},{6,4},{7,5},{8,10},{9,11},{10,... | collective-permute-start | bytes 393224 | tf_op jit(solution)/shard_map/ppermute | solution.py:354
  49.0 4.3 %collective-permute-start.15 = (f16[64,512]{1,0:T(8,128)(2,1)S(1)}, f16[64,512]{1,0:T(8,128)(2,1)S(1)}, u32[]{:S(2)}, u32[]{:S(2)}) collective-permute-start(f16[64,512]{1,0:T(8,128)(2,1)S(1)} %fusion), channel_id=1, source_target_pairs={{0,4},{1,5},{2,6},{3,7},{4,0},{5,1},{6,2},{7,3},{8,12},{9,13},{10,... | collective-permute-start | bytes 196616 | tf_op jit(solution)/shard_map/ppermute | solution.py:354
  51.5 3.5 %collective-permute-start.14 = (f16[256,512]{1,0:T(8,128)(2,1)S(1)}, f16[256,512]{1,0:T(8,128)(2,1)S(1)}, u32[]{:S(2)}, u32[]{:S(2)}) collective-permute-start(f16[256,512]{1,0:T(8,128)(2,1)S(1)} %pad_maximum_fusion), channel_id=1, source_target_pairs={{0,1},{1,0},{2,3},{3,2},{4,5},{5,4},{6,7},{7,6},{8,9},{9,8},{10,11... | collective-permute-start | bytes 786440 | tf_op jit(solution)/shard_map/ppermute | solution.py:354
  53.4 5.2 %collective-permute-start.16 = (f16[64,512]{1,0:T(8,128)(2,1)S(1)}, f16[64,512]{1,0:T(8,128)(2,1)S(1)}, u32[]{:S(2)}, u32[]{:S(2)}) collective-permute-start(f16[64,512]{1,0:T(8,128)(2,1)S(1)} %add_convert_fusion), channel_id=1, source_target_pairs={{0,8},{1,9},{2,10},{3,11},{4,12},{5,13},{6,14},{7,15},{8,0},{9,1},... | collective-permute-start | bytes 196616 | tf_op jit(solution)/shard_map/ppermute | solution.py:354

commit v10 on v9

--- a/solution.py
+++ b/solution.py
@@ -149,14 +149,11 @@
 
 
 def plain_kernel(rt, *refs):
-    packs, (out, w, oh, lev, sems, held) = refs[:-6], refs[-6:]
-    load = pltpu.make_async_copy(rt, held, sems.at[0])
-    load.start()
+    packs, (out, w, oh, lev) = refs[:-4], refs[-4:]
     prepare(packs, w, oh, lev)
-    load.wait()
     rows = TILE // w.shape[1]
     for s0 in range(0, rt.shape[0], rows):
-        out[s0 : s0 + rows, :] = chunk_values(held[s0 : s0 + rows, :], w, oh, lev)
+        out[s0 : s0 + rows, :] = chunk_values(rt[s0 : s0 + rows, :], w, oh, lev)
 
 
 VSPEC = pl.BlockSpec(memory_space=pltpu.VMEM)
@@ -191,9 +188,10 @@
         shape = jax.ShapeDtypeStruct((own, lines * len(rts)), F32)
     if not before:
         kernel = plain_kernel
+        scratch, held = scratch[:3], []
     return pl.pallas_call(
         kernel,
-        in_specs=[HSPEC] * len(rts)
+        in_specs=[HSPEC if before else VSPEC] * len(rts)
         + [VSPEC] * (len(packs) + len(before))
         + [HSPEC] * len(basis),
         out_specs=VSPEC,
@@ -236,17 +234,12 @@
 
 
 def first_kernel(exps, scens, p0, p1, *refs):
-    outs, (w, oh, lev, sems, packs, *held) = refs[:4], refs[4:]
-    loads = [pltpu.make_async_copy(p, packs.at[i], sems.at[4 + i]) for i, p in enumerate((p0, p1))]
-    for load in loads:
-        load.start()
+    outs, (w, oh, lev, sems, *held) = refs[:4], refs[4:]
     stores = [pltpu.make_async_copy(a, b, sems.at[i]) for i, (a, b) in enumerate(zip(held, outs))]
     basis_kernel(exps, scens, *held[:3])
     for store in stores[:3]:
         store.start()
-    for load in loads:
-        load.wait()
-    prepare([packs.at[0], packs.at[1]], w, oh, lev)
+    prepare([p0, p1], w, oh, lev)
     rows = TILE // w.shape[1]
     for s0 in range(0, held[2].shape[0], rows):
         held[3][s0 : s0 + rows, :] = chunk_values(held[2][s0 : s0 + rows, :], w, oh, lev)
@@ -291,11 +284,11 @@
         shapes.append(jax.ShapeDtypeStruct((own, lines), F32))
         return pl.pallas_call(
             first_kernel,
-            in_specs=[VSPEC] * 2 + [HSPEC] * 2,
+            in_specs=[VSPEC] * 4,
             out_specs=[HSPEC] * 4,
             out_shape=shapes,
             scratch_shapes=point_scratch(2 * factors, lines, 2 * points)
-            + [pltpu.SemaphoreType.DMA((6,)), pltpu.VMEM((2, *near[0].shape), BF)]
+            + [pltpu.SemaphoreType.DMA((4,))]
             + like(shapes),
             compiler_params=params(),
             cost_estimate=cost,

time: 59.4 us -> 59.2 us (level)
  waiting for transfers between devices: 10.5 us -> 11.5 us
  starting transfers between devices: 15.4 us -> 14.7 us
  Pallas kernels: 30.2 us -> 29.6 us
    ppermute x17, waiting for transfers between devices: 10.5 us -> 11.5 us  [swap(): return lax.ppermute(x, 'scen', [(i, i ^ mask) for i in range(n)])]
    ppermute x17, starting transfers between devices: 15.4 us -> 14.7 us  [swap(): return lax.ppermute(x, 'scen', [(i, i ^ mask) for i in range(n)])]
  transfers between devices with their start and end apart: 17 -> 17, of which waited for: 8 -> 7; matrix products, arithmetic and copies ran while one was open for 1% -> 1% of each run, Pallas kernels for 40% -> 40%
where the time goes in v10:
time: 59.2 us; the launch traced here: 59 us
  Pallas kernels  29.6 us (50%)
  starting transfers between devices  14.7 us (25%)
  waiting for transfers between devices  11.5 us (19%)
  other arithmetic  1.17 us (2%)
  local copies, waits for them, and re-layouts  1.04 us (2%)
  between operations  0.9 us (2%)
    pallas_call x5, Pallas kernels, values_of(): pl.pallas_call(kernel, in_specs=[HSPEC if before else VSPEC] * len(rts) +...  19.3 us
    ppermute x17, starting transfers between devices, swap(): return lax.ppermute(x, 'scen', [(i, i ^ mask) for i in range(n)])  14.7 us
    ppermute x17, waiting for transfers between devices, swap(): return lax.ppermute(x, 'scen', [(i, i ^ mask) for i in range(n)])  11.5 us
    pallas_call x1, Pallas kernels, basis_of(): pl.pallas_call(first_kernel, in_specs=[VSPEC] * 4, out_specs=[HSPEC] * 4,...  4.01 us
    pallas_call x1, Pallas kernels, basis_of(): pl.pallas_call(gram_kernel, in_specs=[SSPEC, VSPEC, VSPEC, HSPEC], out_sp...  2.79 us
    pallas_call x1, Pallas kernels, packs_of(): pl.pallas_call(pack_kernel, in_specs=[pl.BlockSpec(memory_space=pltpu.HBM...  1.99 us
    pallas_call x1, Pallas kernels, placed(): pl.pallas_call(functools.partial(place_kernel, blocks), in_specs=[pl.Bloc...  1.59 us
  transfers between devices with their start and end apart: 17, of which 7 were waited for; matrix products, arithmetic and copies ran while one was open for 1% of the time, Pallas kernels for 40%

profile of v10, /device:TPU:0, one launch (start us, length us, event | category | flops | bytes accessed | tf_op | source)
XLA Modules:
  0.0 59.0 jit_solution(1125645739017544329)
XLA Ops:
  0.6 2.0 %shard_map.86 = (bf16[80,1024]{1,0:T(8,128)(2,1)}, bf16[144,1024]{1,0:T(8,128)(2,1)}) custom-call(bf16[64,1024]{1,0:T(8,128)(2,1)} %bitcast.12, f32[1,1024]{1,0:T(1,128)} %bitcast.13, s32[1,1024]{1,0:T(1,128)} %bitcast.14, s32[1,1024]{1,0:T(1,128)} %bitcast.15, bf16[64,1024]{1,0:T(8,128)(2,1)} %refs_4_.1, f32[40,1024]{1,0:T(8,128)} %refs_5_.1), custom_call_target="tpu_custom_call" | custom-call | flops 1048576 | bytes 1048576 | tf_op jit(solution)/shard_map/pallas_call | solution.py:65
  2.7 0.5 collective-permute-start.1
  3.2 2.6 %collective-permute-start.4 = (bf16[80,1024]{1,0:T(8,128)(2,1)}, bf16[80,1024]{1,0:T(8,128)(2,1)S(1)}, u32[]{:S(2)}, u32[]{:S(2)}) collective-permute-start(bf16[80,1024]{1,0:T(8,128)(2,1)} %get-tuple-element.30.p0.refs_0_), channel_id=1, source_target_pairs={{0,4},{1,5},{2,6},{3,7},{4,0},{5,1},{6,2},{7,3},{8,12},{9,13},{10,... | collective-permute-start | bytes 491528 | tf_op jit(solution)/shard_map/ppermute | solution.py:347
  5.8 2.6 %collective-permute-start.7 = (bf16[80,1024]{1,0:T(8,128)(2,1)}, bf16[80,1024]{1,0:T(8,128)(2,1)S(1)}, u32[]{:S(2)}, u32[]{:S(2)}) collective-permute-start(bf16[80,1024]{1,0:T(8,128)(2,1)} %get-tuple-element.30.p0.refs_0_), channel_id=1, source_target_pairs={{0,8},{1,9},{2,10},{3,11},{4,12},{5,13},{6,14},{7,15},{8,0},{9,1},... | collective-permute-start | bytes 491528 | tf_op jit(solution)/shard_map/ppermute | solution.py:347
  8.4 1.5 %collective-permute-start = (bf16[144,1024]{1,0:T(8,128)(2,1)}, bf16[144,1024]{1,0:T(8,128)(2,1)S(1)}, u32[]{:S(2)}, u32[]{:S(2)}) collective-permute-start(bf16[144,1024]{1,0:T(8,128)(2,1)} %get-tuple-element.29.scens), channel_id=1, source_target_pairs={{0,2},{1,3},{2,0},{3,1},{4,6},{5,7},{6,4},{7,5},{8,10},{9,11},{10,... | collective-permute-start | bytes 884744 | tf_op jit(solution)/shard_map/ppermute | solution.py:347
  10.0 0.1 copy.10.exps
  10.2 0.9 %copy-done.1 = bf16[80,1024]{1,0:T(8,128)(2,1)S(1)} copy-done((bf16[80,1024]{1,0:T(8,128)(2,1)S(1)}, bf16[80,1024]{1,0:T(8,128)(2,1)}, u32[]{:S(2)}) %copy-start.1) | copy-done | bytes 163864
  11.1 4.0 %shard_map.87 = (bf16[512,1024]{1,0:T(8,128)(2,1)S(1)}, bf16[512,1024]{1,0:T(8,128)(2,1)S(1)}, bf16[1024,128]{1,0:T(8,128)(2,1)S(1)}, f32[1024,64]{1,0:T(8,128)S(1)}) custom-call(s32[512,40]{1,0:T(8,128)S(1)} %copy.10.exps, bf16[144,1024]{1,0:T(8,128)(2,1)S(1)} %copy-done, bf16[80,1024]{1,0:T(8,128)(2,1)S(1)} %copy-done.1, ...), custom_call_target="tpu_custom_call" | custom-call | flops 3000000000 | bytes 3145728 | tf_op jit(solution)/shard_map/pallas_call | solution.py:285
  15.2 0.4 collective-permute-start.9
  15.6 1.8 %collective-permute-done.scens = bf16[144,1024]{1,0:T(8,128)(2,1)S(1)} collective-permute-done((bf16[144,1024]{1,0:T(8,128)(2,1)}, bf16[144,1024]{1,0:T(8,128)(2,1)S(1)}, u32[]{:S(2)}, u32[]{:S(2)}) %collective-permute-start) | collective-permute-done | bytes 294944 | tf_op jit(solution)/shard_map/ppermute | solution.py:347
  17.4 2.8 %shard_map.88 = (bf16[512,1024]{1,0:T(8,128)(2,1)S(1)}, bf16[512,1024]{1,0:T(8,128)(2,1)S(1)}, bf16[1024,128]{1,0:T(8,128)(2,1)S(1)}, f32[128,512]{1,0:T(8,128)S(1)}, f32[128,512]{1,0:T(8,128)S(1)}) custom-call(s32[2]{0:T(128)S(1)} %pad_add_fusion.1.start, s32[512,40]{1,0:T(8,128)S(1)} %copy.10.exps, bf16[144,1024]{1,0:T(8,128)(2,1)S(1)} %collective-permute-done.scens, ...), custom_call_target="tpu_custom_call" | custom-call | flops 3000000000 | bytes 3145728 | tf_op jit(solution)/shard_map/pallas_call | solution.py:299
  20.3 2.4 %shard_map.89.refs_5_ = f32[1024,64]{1,0:T(8,128)S(1)} custom-call(bf16[1024,128]{1,0:T(8,128)(2,1)S(1)} %get-tuple-element.36.rt.refs_1_, bf16[80,1024]{1,0:T(8,128)(2,1)S(1)} %copy-done.1, bf16[80,1024]{1,0:T(8,128)(2,1)S(1)} %collective-permute-done.1.p1.refs_1_), custom_call_target="tpu_custom_call" | custom-call | flops 3565158400 | bytes 1048576 | tf_op jit(solution)/shard_map/pallas_call | solution.py:192
  22.8 0.5 collective-permute-start.3
  23.3 5.0 %shard_map.90.refs_4_ = f32[1024,128]{1,0:T(8,128)S(1)} custom-call(bf16[1024,128]{1,0:T(8,128)(2,1)S(1)} %get-tuple-element.39.refs_0_, bf16[1024,128]{1,0:T(8,128)(2,1)S(1)} %get-tuple-element.36.rt.refs_1_, bf16[80,1024]{1,0:T(8,128)(2,1)S(1)} %collective-permute-done.4.refs_2_, bf16[80,1024]{1,0:T(8,128)(2,1)S(1)} %collective-permute-done.5.refs_3_, ...), custom_call_target="tpu_custom_call" | custom-call | flops 7130316800 | bytes 1048576 | tf_op jit(solution)/shard_map/pallas_call | solution.py:192
  28.3 0.3 collective-permute-start.10
  28.6 0.3 collective-permute-start.8
  29.0 1.0 %collective-permute-start.6 = (f16[128,512]{1,0:T(8,128)(2,1)S(1)}, f16[128,512]{1,0:T(8,128)(2,1)S(1)}, u32[]{:S(2)}, u32[]{:S(2)}) collective-permute-start(f16[128,512]{1,0:T(8,128)(2,1)S(1)} %fusion.1), channel_id=1, source_target_pairs={{0,8},{1,9},{2,10},{3,11},{4,12},{5,13},{6,14},{7,15},{8,0},{9,1},... | collective-permute-start | bytes 393224 | tf_op jit(solution)/shard_map/ppermute | solution.py:347
  29.9 4.8 %shard_map.91.refs_3_ = f32[1024,128]{1,0:T(8,128)S(1)} custom-call(bf16[1024,128]{1,0:T(8,128)(2,1)S(1)} %get-tuple-element.39.refs_0_, bf16[1024,128]{1,0:T(8,128)(2,1)S(1)} %get-tuple-element.36.rt.refs_1_, bf16[80,1024]{1,0:T(8,128)(2,1)S(1)} %collective-permute-done.7.refs_2_, bf16[80,1024]{1,0:T(8,128)(2,1)S(1)} %collective-permute-done.9.refs_3_, ...), custom_call_target="tpu_custom_call" | custom-call | flops 7130316800 | bytes 1048576 | tf_op jit(solution)/shard_map/pallas_call | solution.py:192
  34.8 2.8 %shard_map.92.refs_3_ = f32[1024,128]{1,0:T(8,128)S(1)} custom-call(bf16[1024,128]{1,0:T(8,128)(2,1)S(1)} %get-tuple-element.39.refs_0_, bf16[1024,128]{1,0:T(8,128)(2,1)S(1)} %get-tuple-element.36.rt.refs_1_, bf16[80,1024]{1,0:T(8,128)(2,1)S(1)} %collective-permute-done.8.refs_2_, f32[1024,128]{1,0:T(8,128)S(1)} %shard_map.91.refs_3_), custom_call_target="tpu_custom_call" | custom-call | flops 3565158400 | bytes 1048576 | tf_op jit(solution)/shard_map/pallas_call | solution.py:192
  37.5 0.8 %collective-permute-done.6 = f16[128,512]{1,0:T(8,128)(2,1)S(1)} collective-permute-done((f16[128,512]{1,0:T(8,128)(2,1)S(1)}, f16[128,512]{1,0:T(8,128)(2,1)S(1)}, u32[]{:S(2)}, u32[]{:S(2)}) %collective-permute-start.6) | collective-permute-done | bytes 131104 | tf_op jit(solution)/shard_map/ppermute | solution.py:347
  38.4 4.3 %shard_map.93 = f32[64,512]{1,0:T(8,128)S(1)} custom-call(bf16[1024,128]{1,0:T(8,128)(2,1)S(1)} %get-tuple-element.39.refs_0_, bf16[1024,128]{1,0:T(8,128)(2,1)S(1)} %get-tuple-element.36.rt.refs_1_, bf16[80,1024]{1,0:T(8,128)(2,1)S(1)} %collective-permute-done.10.refs_2_, f32[1024,128]{1,0:T(8,128)S(1)} %shard_map.92.refs_3_, ...), custom_call_target="tpu_custom_call" | custom-call | flops 3565158400 | bytes 1048576 | tf_op jit(solution)/shard_map/pallas_call | solution.py:192
  42.8 1.3 %collective-permute-done.11 = f32[64,512]{1,0:T(8,128)S(1)} collective-permute-done((f32[64,512]{1,0:T(8,128)S(1)}, f32[64,512]{1,0:T(8,128)S(1)}, u32[]{:S(2)}, u32[]{:S(2)}) %collective-permute-start.11) | collective-permute-done | bytes 131104 | tf_op jit(solution)/shard_map/ppermute | solution.py:347
  44.1 1.6 %collective-permute-start.12 = (f16[64,512]{1,0:T(8,128)(2,1)S(1)}, f16[64,512]{1,0:T(8,128)(2,1)S(1)}, u32[]{:S(2)}, u32[]{:S(2)}) collective-permute-start(f16[64,512]{1,0:T(8,128)(2,1)S(1)} %add_convert_fusion.1), channel_id=1, source_target_pairs={{0,2},{1,3},{2,0},{3,1},{4,6},{5,7},{6,4},{7,5},{8,10},{9,11},{10,... | collective-permute-start | bytes 196616 | tf_op jit(solution)/shard_map/ppermute | solution.py:347
  45.7 0.6 collective-permute-start.13
  46.3 2.4 %collective-permute-done.12 = f16[64,512]{1,0:T(8,128)(2,1)S(1)} collective-permute-done((f16[64,512]{1,0:T(8,128)(2,1)S(1)}, f16[64,512]{1,0:T(8,128)(2,1)S(1)}, u32[]{:S(2)}, u32[]{:S(2)}) %collective-permute-start.12) | collective-permute-done | bytes 65568 | tf_op jit(solution)/shard_map/ppermute | solution.py:347
  48.7 1.3 %collective-permute-start.15 = (f16[64,512]{1,0:T(8,128)(2,1)S(1)}, f16[64,512]{1,0:T(8,128)(2,1)S(1)}, u32[]{:S(2)}, u32[]{:S(2)}) collective-permute-start(f16[64,512]{1,0:T(8,128)(2,1)S(1)} %fusion), channel_id=1, source_target_pairs={{0,4},{1,5},{2,6},{3,7},{4,0},{5,1},{6,2},{7,3},{8,12},{9,13},{10,... | collective-permute-start | bytes 196616 | tf_op jit(solution)/shard_map/ppermute | solution.py:347
  50.0 1.2 %collective-permute-done.13 = f16[128,512]{1,0:T(8,128)(2,1)S(1)} collective-permute-done((f16[128,512]{1,0:T(8,128)(2,1)S(1)}, f16[128,512]{1,0:T(8,128)(2,1)S(1)}, u32[]{:S(2)}, u32[]{:S(2)}) %collective-permute-start.13) | collective-permute-done | bytes 131104 | tf_op jit(solution)/shard_map/ppermute | solution.py:347
  51.4 1.7 %collective-permute-done.15 = f16[64,512]{1,0:T(8,128)(2,1)S(1)} collective-permute-done((f16[64,512]{1,0:T(8,128)(2,1)S(1)}, f16[64,512]{1,0:T(8,128)(2,1)S(1)}, u32[]{:S(2)}, u32[]{:S(2)}) %collective-permute-start.15) | collective-permute-done | bytes 65568 | tf_op jit(solution)/shard_map/ppermute | solution.py:347
  53.1 1.3 %collective-permute-start.16 = (f16[64,512]{1,0:T(8,128)(2,1)S(1)}, f16[64,512]{1,0:T(8,128)(2,1)S(1)}, u32[]{:S(2)}, u32[]{:S(2)}) collective-permute-start(f16[64,512]{1,0:T(8,128)(2,1)S(1)} %add_convert_fusion), channel_id=1, source_target_pairs={{0,8},{1,9},{2,10},{3,11},{4,12},{5,13},{6,14},{7,15},{8,0},{9,1},... | collective-permute-start | bytes 196616 | tf_op jit(solution)/shard_map/ppermute | solution.py:347
  54.5 1.6 %shard_map.94 = f32[512,512]{1,0:T(8,128)} custom-call(s32[4]{0:T(128)S(1)} %pad_add_fusion.refs_0_, f32[128,512]{1,0:T(8,128)S(1)} %get-tuple-element.56.refs_1_, f32[128,512]{1,0:T(8,128)S(1)} %convert_element_type.68.refs_2_, f32[256,512]{1,0:T(8,128)S(1)} %convert_element_type.69.refs_3_), custom_call_target="tpu_custom_call" | custom-call | flops 1048576 | bytes 2097152 | tf_op jit(solution)/shard_map/pallas_call | solution.py:322
  56.1 2.2 %collective-permute-done.16 = f16[64,512]{1,0:T(8,128)(2,1)S(1)} collective-permute-done((f16[64,512]{1,0:T(8,128)(2,1)S(1)}, f16[64,512]{1,0:T(8,128)(2,1)S(1)}, u32[]{:S(2)}, u32[]{:S(2)}) %collective-permute-start.16) | collective-permute-done | bytes 65568 | tf_op jit(solution)/shard_map/ppermute | solution.py:347
  58.3 0.7 %add_bitcast_fusion = f32[512,64]{0,1:T(8,128)} fusion(f16[64,512]{1,0:T(8,128)(2,1)S(1)} %collective-permute-done.16, f16[64,512]{1,0:T(8,128)(2,1)S(1)} %add_convert_fusion), kind=kLoop, calls=%fused_computation.4 | loop fusion | flops 98304 | bytes 262144 | tf_op jit(solution)/shard_map/transpose | solution.py:415
  (31 shorter events, 0.8 us)
Async XLA Ops:
  0.6 9.4 %copy-start.2 = (s32[512,40]{0,1:T(8,128)S(1)}, s32[512,40]{0,1:T(8,128)}, u32[]{:S(2)}) copy-start(s32[512,40]{0,1:T(8,128)} %param.13) | copy-start | bytes 245764
  2.6 7.5 %copy-start = (bf16[144,1024]{1,0:T(8,128)(2,1)S(1)}, bf16[144,1024]{1,0:T(8,128)(2,1)}, u32[]{:S(2)}) copy-start(bf16[144,1024]{1,0:T(8,128)(2,1)} %get-tuple-element.29.scens) | copy-start | bytes 884740
  2.7 7.5 %collective-permute-start.1 = (bf16[80,1024]{1,0:T(8,128)(2,1)}, bf16[80,1024]{1,0:T(8,128)(2,1)S(1)}, u32[]{:S(2)}, u32[]{:S(2)}) collective-permute-start(bf16[80,1024]{1,0:T(8,128)(2,1)} %get-tuple-element.30.p0.refs_0_), channel_id=1, source_target_pairs={{0,1},{1,0},{2,3},{3,2},{4,5},{5,4},{6,7},{7,6},{8,9},{9,8},{10,11... | collective-permute-start | bytes 491528 | tf_op jit(solution)/shard_map/ppermute | solution.py:347
  3.2 11.9 %collective-permute-start.4 = (bf16[80,1024]{1,0:T(8,128)(2,1)}, bf16[80,1024]{1,0:T(8,128)(2,1)S(1)}, u32[]{:S(2)}, u32[]{:S(2)}) collective-permute-start(bf16[80,1024]{1,0:T(8,128)(2,1)} %get-tuple-element.30.p0.refs_0_), channel_id=1, source_target_pairs={{0,4},{1,5},{2,6},{3,7},{4,0},{5,1},{6,2},{7,3},{8,12},{9,13},{10,... | collective-permute-start | bytes 491528 | tf_op jit(solution)/shard_map/ppermute | solution.py:347
  5.8 22.8 %collective-permute-start.7 = (bf16[80,1024]{1,0:T(8,128)(2,1)}, bf16[80,1024]{1,0:T(8,128)(2,1)S(1)}, u32[]{:S(2)}, u32[]{:S(2)}) collective-permute-start(bf16[80,1024]{1,0:T(8,128)(2,1)} %get-tuple-element.30.p0.refs_0_), channel_id=1, source_target_pairs={{0,8},{1,9},{2,10},{3,11},{4,12},{5,13},{6,14},{7,15},{8,0},{9,1},... | collective-permute-start | bytes 491528 | tf_op jit(solution)/shard_map/ppermute | solution.py:347
  8.4 9.0 %collective-permute-start = (bf16[144,1024]{1,0:T(8,128)(2,1)}, bf16[144,1024]{1,0:T(8,128)(2,1)S(1)}, u32[]{:S(2)}, u32[]{:S(2)}) collective-permute-start(bf16[144,1024]{1,0:T(8,128)(2,1)} %get-tuple-element.29.scens), channel_id=1, source_target_pairs={{0,2},{1,3},{2,0},{3,1},{4,6},{5,7},{6,4},{7,5},{8,10},{9,11},{10,... | collective-permute-start | bytes 884744 | tf_op jit(solution)/shard_map/ppermute | solution.py:347
  10.2 0.9 %copy-start.1 = (bf16[80,1024]{1,0:T(8,128)(2,1)S(1)}, bf16[80,1024]{1,0:T(8,128)(2,1)}, u32[]{:S(2)}) copy-start(bf16[80,1024]{1,0:T(8,128)(2,1)} %get-tuple-element.30.p0.refs_0_) | copy-start | bytes 491524
  15.1 7.7 %collective-permute-start.5 = (bf16[80,1024]{1,0:T(8,128)(2,1)S(1)}, bf16[80,1024]{1,0:T(8,128)(2,1)S(1)}, u32[]{:S(2)}, u32[]{:S(2)}) collective-permute-start(bf16[80,1024]{1,0:T(8,128)(2,1)S(1)} %collective-permute-done.4.refs_2_), channel_id=1, source_target_pairs={{0,1},{1,0},{2,3},{3,2},{4,5},{5,4},{6,7},{7,6},{8,9},{9,8},{10,11... | collective-permute-start | bytes 491528 | tf_op jit(solution)/shard_map/ppermute | solution.py:347
  15.2 13.1 %collective-permute-start.9 = (bf16[80,1024]{1,0:T(8,128)(2,1)S(1)}, bf16[80,1024]{1,0:T(8,128)(2,1)S(1)}, u32[]{:S(2)}, u32[]{:S(2)}) collective-permute-start(bf16[80,1024]{1,0:T(8,128)(2,1)S(1)} %collective-permute-done.4.refs_2_), channel_id=1, source_target_pairs={{0,8},{1,9},{2,10},{3,11},{4,12},{5,13},{6,14},{7,15},{8,0},{9,1},... | collective-permute-start | bytes 491528 | tf_op jit(solution)/shard_map/ppermute | solution.py:347
  20.2 2.5 %collective-permute-start.2 = (f32[128,512]{1,0:T(8,128)S(1)}, f32[128,512]{1,0:T(8,128)S(1)}, u32[]{:S(2)}, u32[]{:S(2)}) collective-permute-start(f32[128,512]{1,0:T(8,128)S(1)} %get-tuple-element.35), channel_id=1, source_target_pairs={{0,1},{1,0},{2,3},{3,2},{4,5},{5,4},{6,7},{7,6},{8,9},{9,8},{10,11... | collective-permute-start | bytes 786440 | tf_op jit(solution)/shard_map/ppermute | solution.py:347
  22.8 6.1 %collective-permute-start.3 = (f16[128,512]{1,0:T(8,128)(2,1)S(1)}, f16[128,512]{1,0:T(8,128)(2,1)S(1)}, u32[]{:S(2)}, u32[]{:S(2)}) collective-permute-start(f16[128,512]{1,0:T(8,128)(2,1)S(1)} %fusion.3), channel_id=1, source_target_pairs={{0,4},{1,5},{2,6},{3,7},{4,0},{5,1},{6,2},{7,3},{8,12},{9,13},{10,... | collective-permute-start | bytes 393224 | tf_op jit(solution)/shard_map/ppermute | solution.py:347
  28.3 10.1 %collective-permute-start.10 = (bf16[80,1024]{1,0:T(8,128)(2,1)S(1)}, bf16[80,1024]{1,0:T(8,128)(2,1)S(1)}, u32[]{:S(2)}, u32[]{:S(2)}) collective-permute-start(bf16[80,1024]{1,0:T(8,128)(2,1)S(1)} %collective-permute-done.9.refs_3_), channel_id=1, source_target_pairs={{0,1},{1,0},{2,3},{3,2},{4,5},{5,4},{6,7},{7,6},{8,9},{9,8},{10,11... | collective-permute-start | bytes 491528 | tf_op jit(solution)/shard_map/ppermute | solution.py:347
  28.6 6.1 %collective-permute-start.8 = (bf16[80,1024]{1,0:T(8,128)(2,1)S(1)}, bf16[80,1024]{1,0:T(8,128)(2,1)S(1)}, u32[]{:S(2)}, u32[]{:S(2)}) collective-permute-start(bf16[80,1024]{1,0:T(8,128)(2,1)S(1)} %collective-permute-done.7.refs_2_), channel_id=1, source_target_pairs={{0,1},{1,0},{2,3},{3,2},{4,5},{5,4},{6,7},{7,6},{8,9},{9,8},{10,11... | collective-permute-start | bytes 491528 | tf_op jit(solution)/shard_map/ppermute | solution.py:347
  29.0 9.4 %collective-permute-start.6 = (f16[128,512]{1,0:T(8,128)(2,1)S(1)}, f16[128,512]{1,0:T(8,128)(2,1)S(1)}, u32[]{:S(2)}, u32[]{:S(2)}) collective-permute-start(f16[128,512]{1,0:T(8,128)(2,1)S(1)} %fusion.1), channel_id=1, source_target_pairs={{0,8},{1,9},{2,10},{3,11},{4,12},{5,13},{6,14},{7,15},{8,0},{9,1},... | collective-permute-start | bytes 393224 | tf_op jit(solution)/shard_map/ppermute | solution.py:347
  42.7 1.4 %collective-permute-start.11 = (f32[64,512]{1,0:T(8,128)S(1)}, f32[64,512]{1,0:T(8,128)S(1)}, u32[]{:S(2)}, u32[]{:S(2)}) collective-permute-start(f32[64,512]{1,0:T(8,128)S(1)} %shard_map.93), channel_id=1, source_target_pairs={{0,1},{1,0},{2,3},{3,2},{4,5},{5,4},{6,7},{7,6},{8,9},{9,8},{10,11... | collective-permute-start | bytes 393224 | tf_op jit(solution)/shard_map/ppermute | solution.py:347
  44.1 4.6 %collective-permute-start.12 = (f16[64,512]{1,0:T(8,128)(2,1)S(1)}, f16[64,512]{1,0:T(8,128)(2,1)S(1)}, u32[]{:S(2)}, u32[]{:S(2)}) collective-permute-start(f16[64,512]{1,0:T(8,128)(2,1)S(1)} %add_convert_fusion.1), channel_id=1, source_target_pairs={{0,2},{1,3},{2,0},{3,1},{4,6},{5,7},{6,4},{7,5},{8,10},{9,11},{10,... | collective-permute-start | bytes 196616 | tf_op jit(solution)/shard_map/ppermute | solution.py:347
  45.7 5.5 %collective-permute-start.13 = (f16[128,512]{1,0:T(8,128)(2,1)S(1)}, f16[128,512]{1,0:T(8,128)(2,1)S(1)}, u32[]{:S(2)}, u32[]{:S(2)}) collective-permute-start(f16[128,512]{1,0:T(8,128)(2,1)S(1)} %get-tuple-element.57), channel_id=1, source_target_pairs={{0,2},{1,3},{2,0},{3,1},{4,6},{5,7},{6,4},{7,5},{8,10},{9,11},{10,... | collective-permute-start | bytes 393224 | tf_op jit(solution)/shard_map/ppermute | solution.py:347
  48.7 4.3 %collective-permute-start.15 = (f16[64,512]{1,0:T(8,128)(2,1)S(1)}, f16[64,512]{1,0:T(8,128)(2,1)S(1)}, u32[]{:S(2)}, u32[]{:S(2)}) collective-permute-start(f16[64,512]{1,0:T(8,128)(2,1)S(1)} %fusion), channel_id=1, source_target_pairs={{0,4},{1,5},{2,6},{3,7},{4,0},{5,1},{6,2},{7,3},{8,12},{9,13},{10,... | collective-permute-start | bytes 196616 | tf_op jit(solution)/shard_map/ppermute | solution.py:347
  51.3 3.1 %collective-permute-start.14 = (f16[256,512]{1,0:T(8,128)(2,1)S(1)}, f16[256,512]{1,0:T(8,128)(2,1)S(1)}, u32[]{:S(2)}, u32[]{:S(2)}) collective-permute-start(f16[256,512]{1,0:T(8,128)(2,1)S(1)} %pad_maximum_fusion), channel_id=1, source_target_pairs={{0,1},{1,0},{2,3},{3,2},{4,5},{5,4},{6,7},{7,6},{8,9},{9,8},{10,11... | collective-permute-start | bytes 786440 | tf_op jit(solution)/shard_map/ppermute | solution.py:347
  53.1 5.2 %collective-permute-start.16 = (f16[64,512]{1,0:T(8,128)(2,1)S(1)}, f16[64,512]{1,0:T(8,128)(2,1)S(1)}, u32[]{:S(2)}, u32[]{:S(2)}) collective-permute-start(f16[64,512]{1,0:T(8,128)(2,1)S(1)} %add_convert_fusion), channel_id=1, source_target_pairs={{0,8},{1,9},{2,10},{3,11},{4,12},{5,13},{6,14},{7,15},{8,0},{9,1},... | collective-permute-start | bytes 196616 | tf_op jit(solution)/shard_map/ppermute | solution.py:347
